TPU v7x, 256 devices: a whole 4x4x8 slice. The times are simulated.
256 devices in a mesh: dp: 32 (over y, z_hi, core), mp: 8 (over z_lo, x).
Axes of the slice: x: 4, y: 4, z: 8 (z_hi: 4, z_lo: 2; z = z_hi * 2 + z_lo), core: 2. Of those that a mesh axis runs over, the one named last changes fastest.
Arguments:
- inputs: bfloat16 [4, 8192, 4096], P(None, 'dp'), may hold values from -60 to 60
- gate_cotangent: bfloat16 [4, 8192, 6144], P(None, 'dp', 'mp'), may hold values from -6 to 6
- ff_blocks: int32 [4], replicated, may hold values from 24 to 48, as said below
- layer_active: int32 [4], replicated, may hold values from 0 to 1, as said below
- param: float32 [4096, 6144], P(('dp', 'mp')), may hold values from -0.09375 to 0.09375
- moment: float32 [4096, 6144], P(('dp', 'mp')), may hold values from -3 to 3
- second_moment: float32 [4096, 6144], P(('dp', 'mp')), may hold values from 0.5 to 2
Outputs:
- new_param: float32 [4096, 6144], P(('dp', 'mp'))
- new_moment: float32 [4096, 6144], P(('dp', 'mp'))
- new_second: float32 [4096, 6144], P(('dp', 'mp'))
Inputs may be any that keep to these rules, and one draw needn't show every extreme that they name: `ff_blocks`: entry 0 is 6144 // 128 (the largest subnet), entry 1 is 6144 // (256) (the smallest). `layer_active`: entry 0 is 1, and exactly one of entries 1, 2 and 3 is 0.
All inputs are finite; a program needn't handle non-finite values.
Results may differ from a plain program's by a relative error of at most 0.0003.
Values sent between devices are 32-bit elements; how exact they have to be, the bound alone decides.
No kernel may reach another device: no remote copies, remote signals or barrier semaphores. Data moves between devices by JAX's collectives and lax.ppermute only.
A program may use at most 128 MiB of HBM per device.

v0:
```python
import math

import jax
import jax.numpy as jnp
from jax import lax
from jax.sharding import Mesh
from jax.sharding import PartitionSpec as P

D = 4096
FF = 6144
BLOCK = 128
STEP = 10
DP_MP = ("dp_0", "dp_1", "dp_2", "mp_0", "mp_1")
MP = ("mp_0", "mp_1")
DP = ("dp_0", "dp_1", "dp_2")


def over_axes(x, axes):
    for axis in axes:
        x = lax.psum(x, axis)
    return x


def squared_total(values):
    return over_axes(jnp.sum(values * values), DP_MP)


def shards(inputs, gate_cotangent, ff_blocks, layer_active, param, moment, second_moment):
    subnets, tokens, width = inputs.shape
    local_cols = gate_cotangent.shape[2]
    first_col = lax.axis_index(MP) * local_cols
    column = first_col + lax.broadcasted_iota(jnp.int32, (subnets, local_cols), 1)
    keep = (column < BLOCK * ff_blocks[:, None]) & (layer_active[:, None] == 1)
    masked = jnp.where(keep[:, None, :], gate_cotangent, jnp.zeros((), jnp.bfloat16))
    rows_in = inputs.reshape(subnets * tokens, width)
    rows_ct = masked.reshape(subnets * tokens, local_cols)
    tile = lax.psum_scatter(
        lax.dot_general(
            rows_in, rows_ct, (((0,), (0,)), ((), ())), preferred_element_type=jnp.float32
        ),
        DP,
        scatter_dimension=0,
        tiled=True,
    )
    gradient = lax.all_to_all(tile, MP, split_axis=0, concat_axis=1, tiled=True)
    total_sq = squared_total(gradient)
    total = jnp.sqrt(total_sq)
    factor = jnp.minimum(1.0, math.sqrt(1.0 * D * FF) / (total + 1e-06))
    clipped = gradient * factor
    new_moment = 0.9 * moment + 0.1 * clipped
    new_second = 0.95 * second_moment + 0.05 * clipped * clipped
    first_hat = new_moment / (1.0 - 0.9**STEP)
    second_hat = new_second / (1.0 - 0.95**STEP)
    new_param = param - 0.02 * (first_hat / (jnp.sqrt(second_hat) + 1e-08) + 0.1 * param)
    return (new_param, new_moment, new_second)


def solution(mesh):
    split = Mesh(mesh.devices.reshape(4, 4, 2, 2, 4), ("dp_0", "dp_1", "dp_2", "mp_0", "mp_1"))
    return jax.shard_map(
        shards,
        mesh=split,
        in_specs=(
            P(None, DP, None),
            P(None, DP, MP),
            P(),
            P(),
            P(DP_MP, None),
            P(DP_MP, None),
            P(DP_MP, None),
        ),
        out_specs=(P(DP_MP, None), P(DP_MP, None), P(DP_MP, None)),
        check_vma=False,
    )
```

profile of v0, /device:TPU:2, one launch (start us, length us, event | category | flops | bytes accessed | tf_op | source)
XLA Modules:
  0.0 230.7 jit_solution(5905588080318845541)
XLA Ops:
  7.2 0.0 reduce-scatter.2.cloned.1.call-start
  7.2 0.7 broadcast_multiply_fusion
  7.9 0.7 broadcast_compare_fusion
  8.5 0.1 compare_and_fusion
  8.6 13.3 %convolution_bitcast_fusion = f32[4096,768]{0,1:T(8,128)} fusion(bf16[4,256,4096]{2,1,0:T(8,128)(2,1)} %param.7, bf16[4,256,768]{2,1,0:T(8,128)(2,1)} %param.8, pred[4,768]{1,0:T(4,128)(4,1)S(1)} %compare_and_fusion), kind=kOutput, calls=%fused_computation | convolution fusion | flops 6443237376 | bytes 22547456 | tf_op jit(solution)/shard_map/dot_general | solution.py:38
  21.9 0.0 copy-start
  21.9 0.0 copy-start.1
  21.9 0.0 copy-start.2
  21.9 0.0 reduce-scatter.2.cloned.1.call-update
  22.0 145.7 %reduce-scatter.2.cloned.1.call-done = f32[128,768]{0,1:T(8,128)} async-done(((f32[4096,768]{0,1:T(8,128)}), f32[128,768]{0,1:T(8,128)}) %reduce-scatter.2.cloned.1.call-update) | async-done | bytes 393232 | tf_op jit(solution)/shard_map/reduce_scatter | solution.py:37
  167.7 1.2 copy.15
  168.8 11.1 %all_to_all.13 = f32[8,16,768]{2,1,0:T(8,128)S(1)} all-to-all(f32[8,16,768]{2,1,0:T(8,128)S(1)} %bitcast.10), channel_id=1, replica_groups=mesh['dp_0'=4,'dp_1'=4,'dp_2'=2,'mp_0'=2,'mp_1'=4] {'mp_0','mp_1'}, dimensions={0} | all-to-all | bytes 786432 | tf_op jit(solution)/shard_map/all_to_all | solution.py:45
  180.0 0.7 multiply_reduce_fusion
  180.7 11.4 %psum.35 = f32[]{:T(128)} all-reduce(f32[]{:T(128)} %multiply_reduce_fusion), channel_id=1, replica_groups=mesh['dp_0'=4,'dp_1'=4,'dp_2'=2,'mp_0'=2,'mp_1'=4] {'dp_0'}, use_global_device_ids=true, to_apply=%region_2.3 | all-reduce | flops 1 | bytes 8 | tf_op jit(solution)/shard_map/psum | solution.py:20
  192.1 11.3 %psum.36 = f32[]{:T(128)} all-reduce(f32[]{:T(128)} %psum.35), channel_id=1, replica_groups=mesh['dp_0'=4,'dp_1'=4,'dp_2'=2,'mp_0'=2,'mp_1'=4] {'dp_1'}, use_global_device_ids=true, to_apply=%region_3.4 | all-reduce | flops 1 | bytes 8 | tf_op jit(solution)/shard_map/psum | solution.py:20
  203.4 3.1 %psum.37 = f32[]{:T(128)} all-reduce(f32[]{:T(128)} %psum.36), channel_id=1, replica_groups=mesh['dp_0'=4,'dp_1'=4,'dp_2'=2,'mp_0'=2,'mp_1'=4] {'dp_2'}, use_global_device_ids=true, to_apply=%region_4.5 | all-reduce | flops 1 | bytes 8 | tf_op jit(solution)/shard_map/psum | solution.py:20
  206.4 5.5 %psum.38 = f32[]{:T(128)} all-reduce(f32[]{:T(128)} %psum.37), channel_id=1, replica_groups=mesh['dp_0'=4,'dp_1'=4,'dp_2'=2,'mp_0'=2,'mp_1'=4] {'mp_0'}, use_global_device_ids=true, to_apply=%region_5.6 | all-reduce | flops 1 | bytes 8 | tf_op jit(solution)/shard_map/psum | solution.py:20
  212.0 9.8 %psum.39 = f32[]{:T(128)} all-reduce(f32[]{:T(128)} %psum.38), channel_id=1, replica_groups=mesh['dp_0'=4,'dp_1'=4,'dp_2'=2,'mp_0'=2,'mp_1'=4] {'mp_1'}, use_global_device_ids=true, to_apply=%region_6.7 | all-reduce | flops 1 | bytes 8 | tf_op jit(solution)/shard_map/psum | solution.py:20
  222.7 0.0 copy-done
  222.7 0.0 copy-done.1
  222.7 0.0 copy-done.2
  222.7 1.2 multiply_subtract_fusion
  (3 shorter events, 0.1 us)
Async XLA Ops:
  7.2 160.5 %reduce-scatter.2.cloned.1.call-start = ((), (), s32[]{:S(2)}) async-start(), calls=%async_computation.2 | async-start | bytes 12976128 | tf_op jit(solution)/shard_map/reduce_scatter | solution.py:37
  21.9 200.7 %copy-start = (f32[16,6144]{1,0:T(8,128)S(1)}, f32[16,6144]{1,0:T(8,128)}, u32[]{:S(2)}) copy-start(f32[16,6144]{1,0:T(8,128)} %param.11) | copy-start | bytes 1179652
  21.9 200.7 %copy-start.1 = (f32[16,6144]{1,0:T(8,128)S(1)}, f32[16,6144]{1,0:T(8,128)}, u32[]{:S(2)}) copy-start(f32[16,6144]{1,0:T(8,128)} %param.12) | copy-start | bytes 1179652
  21.9 200.8 %copy-start.2 = (f32[16,6144]{1,0:T(8,128)S(1)}, f32[16,6144]{1,0:T(8,128)}, u32[]{:S(2)}) copy-start(f32[16,6144]{1,0:T(8,128)} %param.13) | copy-start | bytes 1179652
Sparse Core Ops, SparseCore 0:
  22.1 145.5 reduce-scatter.1
where the time goes:
time: 231 us
  waiting for transfers between devices  146 us (63%)
  blocking collectives  52.3 us (23%)
  between operations  14.8 us (6%)
  matrix products  13.3 us (6%)
  other arithmetic  3.31 us (1%)
    reduce_scatter x1, waiting for transfers between devices, shards(): lax.psum_scatter(lax.dot_general(rows_in, rows_ct, (((0,), (0,)), ((), ()...  146 us
    psum x5, blocking collectives, over_axes(): x = lax.psum(x, axis)  41.2 us
    dot_general x1, matrix products, shards(): lax.dot_general(rows_in, rows_ct, (((0,), (0,)), ((), ())), preferred_ele...  13.3 us
    all_to_all x1, blocking collectives, shards(): gradient = lax.all_to_all(tile, MP, split_axis=0, concat_axis=1, tiled=True)  11.1 us
  transfers between devices with their start and end apart: 1, of which 1 were waited for; matrix products, arithmetic and copies ran while one was open for 0% of the time, Pallas kernels for 0%

commit v1 on v0

v1 whole, which is shorter than its diff:
```python
import functools
import math

import jax
import jax.numpy as jnp
from jax import lax
from jax.experimental import pallas as pl
from jax.experimental.pallas import tpu as pltpu
from jax.sharding import Mesh
from jax.sharding import PartitionSpec as P

D = 4096
FF = 6144
BLOCK = 128
STEP = 10
LANES = 128
LIVE = 3
AXES = ("y", "z", "core", "z_lo", "x")
DP = ("y", "z", "core")
MP = ("z_lo", "x")
SIZES = {"y": 4, "z": 4, "core": 2, "z_lo": 2, "x": 4}

CHUNKS = (160, 144, 80)
STREAM_A = (("y", 1), ("z", 1), ("y", 3), ("z", 3))
STREAM_B = (("y", 3), ("z", 3), ("y", 1), ("z", 1))


def swap(value, axis, mask):
    return lax.ppermute(value, axis, [(i, i ^ mask) for i in range(SIZES[axis])])


def product_kernel(widths, tile_ref, live_ref, limit_ref, *refs):
    x_refs, m_refs = refs[: 4 * LIVE], refs[4 * LIVE : 5 * LIVE]
    outs, mt_ref = refs[5 * LIVE : -1], refs[-1]

    @pl.when(pl.program_id(0) == 0)
    def _():
        for s in range(LIVE):
            values = m_refs[s][0]
            column = lax.broadcasted_iota(jnp.int32, values.shape, 1)
            values = jnp.where(column < limit_ref[s], values, jnp.zeros_like(values))
            mt_ref[:, s * 256 : (s + 1) * 256] = values.T

    first = 0
    for k, width in enumerate(widths):
        rows = slice(first, first + width)
        total = None
        for s in range(LIVE):
            right = jnp.concatenate([x_refs[4 * s + t][0] for t in range(4)], axis=1)
            part = jnp.dot(
                mt_ref[rows, s * 256 : (s + 1) * 256], right, preferred_element_type=jnp.float32
            )
            total = part if total is None else total + part
        for half in range(2):
            low = half * (width // 2)
            for t in range(4):
                at = (t // 2, t % 2) if half == 0 else (t % 2, t // 2)
                outs[2 * k + half][0, at[0], 0, at[1]] = total[
                    low : low + width // 2, t * LANES : (t + 1) * LANES
                ]
        first += width


def product(tiles, live, limits, x, m, chunks):
    widths = tuple(2 * j for j in chunks)
    x_specs = [
        pl.BlockSpec((1, 256, LANES), lambda i, tile, lv, lim, s=s, t=t: (lv[s], 0, tile[4 * i + t]))
        for s in range(LIVE)
        for t in range(4)
    ]
    m_specs = [
        pl.BlockSpec((1, 256, m.shape[2]), lambda i, tile, lv, lim, s=s: (lv[s], 0, 0))
        for s in range(LIVE)
    ]
    out_shape, out_specs = [], []
    for j in chunks:
        for half in range(2):
            out_shape.append(jax.ShapeDtypeStruct((2, 2, 2, 2, j, LANES), jnp.float32))
            if half == 0:
                place = lambda i, tile, lv, lim: (i // 2, 0, i % 2, 0, 0, 0)
            else:
                place = lambda i, tile, lv, lim: (i % 2, 0, i // 2, 0, 0, 0)
            out_specs.append(pl.BlockSpec((1, 2, 1, 2, j, LANES), place))
    return pl.pallas_call(
        functools.partial(product_kernel, widths),
        grid_spec=pltpu.PrefetchScalarGridSpec(
            num_scalar_prefetch=3,
            grid=(4,),
            in_specs=x_specs + m_specs,
            out_specs=out_specs,
            scratch_shapes=[pltpu.VMEM((m.shape[2], LIVE * 256), jnp.bfloat16)],
        ),
        out_shape=out_shape,
        compiler_params=pltpu.CompilerParams(vmem_limit_bytes=24 * 1024 * 1024),
    )(tiles, live, limits, *([x] * (4 * LIVE)), *([m] * LIVE))


def reduce_stream(own, other, steps):
    parts = [own, other]
    for axis, mask in steps:
        send = sum(p[0] for p in parts[1:]) + parts[0][0]
        received = swap(send, axis, mask)
        parts = [p[1] for p in parts] + [received]
    return sum(parts[1:]) + parts[0]


def shards(inputs, gate_cotangent, ff_blocks, layer_active, param, moment, second_moment):
    y, z, core = (lax.axis_index(a) for a in DP)
    cols = gate_cotangent.shape[2]
    me = lax.axis_index(MP)
    index = jnp.arange(LIVE, dtype=jnp.int32)
    idle = jnp.sum(jnp.where(layer_active == 1, 0, jnp.arange(4, dtype=jnp.int32)))
    live = index + (index >= idle).astype(jnp.int32)
    limits = BLOCK * ff_blocks[live] - me * cols
    step = jnp.arange(4, dtype=jnp.int32)
    offset = (1 - step // 2) * 1 ^ (1 - step % 2) * 3
    tiles = (((y ^ offset)[:, None] * 4 + (z ^ offset)[None, :]) * 2).reshape(16)
    others = product(tiles + (1 - core), live, limits, inputs, gate_cotangent, CHUNKS)
    others = [swap(o, "core", 1) for o in others]
    owns = product(tiles + core, live, limits, inputs, gate_cotangent, CHUNKS)
    done = [
        reduce_stream(own, other, STREAM_A if n % 2 == 0 else STREAM_B)
        for n, (own, other) in enumerate(zip(owns, others))
    ]
    tile = jnp.concatenate(done, axis=0)
    squares = jnp.sum((tile * tile).reshape(-1, 8, LANES), axis=0)
    gradient = lax.all_to_all(tile.T, MP, split_axis=0, concat_axis=1, tiled=True)
    for axis, mask in (
        ("core", 1), ("y", 1), ("y", 3), ("x", 1), ("x", 3), ("z_lo", 1), ("z", 1), ("z", 3),
    ):
        squares = squares + swap(squares, axis, mask)
    total = jnp.sqrt(jnp.sum(squares))
    factor = jnp.minimum(1.0, math.sqrt(1.0 * D * FF) / (total + 1e-06))
    clipped = gradient * factor
    new_moment = 0.9 * moment + 0.1 * clipped
    new_second = 0.95 * second_moment + 0.05 * clipped * clipped
    first_hat = new_moment / (1.0 - 0.9**STEP)
    second_hat = new_second / (1.0 - 0.95**STEP)
    new_param = param - 0.02 * (first_hat / (jnp.sqrt(second_hat) + 1e-08) + 0.1 * param)
    return (new_param, new_moment, new_second)


def solution(mesh):
    split = Mesh(mesh.devices.reshape(4, 4, 2, 2, 4), AXES)
    rows = P(AXES, None)
    return jax.shard_map(
        shards,
        mesh=split,
        in_specs=(P(None, DP, None), P(None, DP, MP), P(), P(), rows, rows, rows),
        out_specs=(rows, rows, rows),
        check_vma=False,
    )
```

time: 231 us -> 203 us (0.88)
  starting transfers between devices: 0.04 us -> 81.6 us
  waiting for transfers between devices: 146 us -> 71.7 us
  blocking collectives: 52.3 us -> 0 us
  other arithmetic: 3.31 us -> 19.9 us
  Pallas kernels: 0 us -> 13.4 us
  matrix products: 13.3 us -> 0 us
  between operations: 14.8 us -> 1.74 us
  local copies, waits for them, and re-layouts: 1.19 us -> 12.8 us
    reduce_scatter x1 -> x0, waiting for transfers between devices: 146 us -> none  [shards(): lax.psum_scatter(lax.dot_general(rows_in, rows_ct, (((0,), (0,)), ((), ()...]
    ppermute x0 -> x38, starting transfers between devices: none -> 76.6 us  [swap(): lax.ppermute(value, axis, [(i, i ^ mask) for i in range(SIZES[axis])])]
    ppermute x0 -> x38, waiting for transfers between devices: none -> 71.7 us  [swap(): lax.ppermute(value, axis, [(i, i ^ mask) for i in range(SIZES[axis])])]
    psum x5 -> x0, blocking collectives: 41.2 us -> none  [over_axes(): x = lax.psum(x, axis)]
    add x1 -> x33, other arithmetic: 0.01 us -> 13.4 us  [the longest x24 12.1 us: reduce_stream(): send = sum((p[0] for p in parts[1:])) + parts[0][0]]
    pallas_call x0 -> x2, Pallas kernels: none -> 13.4 us  [product(): pl.pallas_call(functools.partial(product_kernel, widths), grid_spec=pltpu...]
    dot_general x1 -> x0, matrix products: 13.3 us -> none  [shards(): lax.dot_general(rows_in, rows_ct, (((0,), (0,)), ((), ())), preferred_ele...]
    all_to_all x1 -> x0, blocking collectives: 11.1 us -> none  [shards(): gradient = lax.all_to_all(tile, MP, split_axis=0, concat_axis=1, tiled=True)]
  transfers between devices with their start and end apart: 1 -> 39, of which waited for: 1 -> 21; matrix products, arithmetic and copies ran while one was open for 0% -> 8% of each run, Pallas kernels for 0% -> 3%
where the time goes in v1:
time: 203 us; the launch traced here: 201 us
  starting transfers between devices  81.6 us (40%)
  waiting for transfers between devices  71.7 us (35%)
  other arithmetic  19.9 us (10%)
  Pallas kernels  13.4 us (7%)
  local copies, waits for them, and re-layouts  12.8 us (6%)
    ppermute x38, starting transfers between devices, swap(): lax.ppermute(value, axis, [(i, i ^ mask) for i in range(SIZES[axis])])  76.6 us
    ppermute x38, waiting for transfers between devices, swap(): lax.ppermute(value, axis, [(i, i ^ mask) for i in range(SIZES[axis])])  71.7 us
    pallas_call x2, Pallas kernels, product(): pl.pallas_call(functools.partial(product_kernel, widths), grid_spec=pltpu...  13.4 us
    add x24, other arithmetic, reduce_stream(): send = sum((p[0] for p in parts[1:])) + parts[0][0]  12.1 us
    unnamed x24, local copies, waits for them, and re-layouts  10.4 us
    all_to_all x1, starting transfers between devices, shards(): lax.all_to_all(tile.T, MP, split_axis=0, concat_axis=1, tiled=True)  4.97 us
  transfers between devices with their start and end apart: 39, of which 21 were waited for; matrix products, arithmetic and copies ran while one was open for 8% of the time, Pallas kernels for 3%

profile of v1, /device:TPU:2, one launch (start us, length us, event | category | flops | bytes accessed | tf_op | source)
XLA Modules:
  0.0 201.1 jit_solution(7977243113640320180)
XLA Ops:
  1.4 1.3 fusion.103
  4.7 3.4 %copy-done.1 = bf16[4,256,4096]{2,1,0:T(8,128)(2,1)S(1)} copy-done((bf16[4,256,4096]{2,1,0:T(8,128)(2,1)S(1)}, bf16[4,256,4096]{2,1,0:T(8,128)(2,1)}, u32[]{:S(2)}) %copy-start.1) | copy-done | bytes 8388632
  8.1 1.4 copy-done.3
  9.5 6.9 %shard_map.94 = (f32[2,2,2,2,160,128]{5,4,3,2,1,0:T(8,128)S(1)}, f32[2,2,2,2,160,128]{5,4,3,2,1,0:T(8,128)S(1)}, f32[2,2,2,2,144,128]{5,4,3,2,1,0:T(8,128)}, f32...) custom-call(s32[16]{0:T(128)S(1)} %add.410.tile_ref, ...), custom_call_target="tpu_custom_call" | custom-call | tf_op jit(solution)/shard_map/pallas_call | solution.py:84
  16.4 1.1 copy-done.5
  17.5 1.1 copy-done.7
  19.8 3.4 %copy-done.2 = bf16[4,256,4096]{2,1,0:T(8,128)(2,1)S(1)} copy-done((bf16[4,256,4096]{2,1,0:T(8,128)(2,1)S(1)}, bf16[4,256,4096]{2,1,0:T(8,128)(2,1)}, u32[]{:S(2)}) %copy-start.2) | copy-done | bytes 8388632
  23.2 6.5 %shard_map.95 = (f32[2,2,2,2,160,128]{5,4,3,2,1,0:T(8,128)S(1)}, f32[2,2,2,2,160,128]{5,4,3,2,1,0:T(8,128)S(1)}, f32[2,2,2,2,144,128]{5,4,3,2,1,0:T(8,128)S(1)},...) custom-call(s32[16]{0:T(128)S(1)} %add.417.tile_ref, ...), custom_call_target="tpu_custom_call" | custom-call | tf_op jit(solution)/shard_map/pallas_call | solution.py:84
  29.7 1.1 fusion.6
  30.9 1.7 collective-permute-start.21
  32.5 1.0 fusion.5
  33.5 2.3 %collective-permute-start.26 = (f32[2,2,2,80,128]{4,3,2,1,0:T(8,128)S(1)}, f32[2,2,2,80,128]{4,3,2,1,0:T(8,128)S(1)}, u32[]{:S(2)}, u32[]{:S(2)}) collective-permute-start(f32[2,2,2,80,128]{4,3,2,1,0:T(8,128)S(1)} %fusion.5), channel_id=1, source_target_pairs={{0,192},{64,128},{128,64},{192,0},{1,193},{65,129},{129,65},{193,1... | collective-permute-start | bytes 983048 | tf_op jit(solution)/shard_map/ppermute | solution.py:29
  36.3 4.7 %collective-permute-done.21 = f32[2,2,2,80,128]{4,3,2,1,0:T(8,128)S(1)} collective-permute-done((f32[2,2,2,80,128]{4,3,2,1,0:T(8,128)S(1)}, f32[2,2,2,80,128]{4,3,2,1,0:T(8,128)S(1)}, u32[]{:S(2)}, u32[]{:S(2)}) %collective-permute-start.21) | collective-permute-done | bytes 327712 | tf_op jit(solution)/shard_map/ppermute | solution.py:29
  41.1 1.0 fusion.18
  42.0 2.7 %collective-permute-done.26 = f32[2,2,2,80,128]{4,3,2,1,0:T(8,128)S(1)} collective-permute-done((f32[2,2,2,80,128]{4,3,2,1,0:T(8,128)S(1)}, f32[2,2,2,80,128]{4,3,2,1,0:T(8,128)S(1)}, u32[]{:S(2)}, u32[]{:S(2)}) %collective-permute-start.26) | collective-permute-done | bytes 327712 | tf_op jit(solution)/shard_map/ppermute | solution.py:29
  44.7 3.3 %collective-permute-start.22 = (f32[2,2,80,128]{3,2,1,0:T(8,128)S(1)}, f32[2,2,80,128]{3,2,1,0:T(8,128)S(1)}, u32[]{:S(2)}, u32[]{:S(2)}) collective-permute-start(f32[2,2,80,128]{3,2,1,0:T(8,128)S(1)} %fusion.18), channel_id=1, source_target_pairs={{0,16},{16,0},{32,48},{48,32},{1,17},{17,1},{33,49},{49,33},{2,18}... | collective-permute-start | bytes 491528 | tf_op jit(solution)/shard_map/ppermute | solution.py:29
  48.0 0.9 fusion.16
  48.9 6.3 %collective-permute-done.22 = f32[2,2,80,128]{3,2,1,0:T(8,128)S(1)} collective-permute-done((f32[2,2,80,128]{3,2,1,0:T(8,128)S(1)}, f32[2,2,80,128]{3,2,1,0:T(8,128)S(1)}, u32[]{:S(2)}, u32[]{:S(2)}) %collective-permute-start.22) | collective-permute-done | bytes 163872 | tf_op jit(solution)/shard_map/ppermute | solution.py:29
  55.2 3.7 %collective-permute-start.27 = (f32[2,2,80,128]{3,2,1,0:T(8,128)S(1)}, f32[2,2,80,128]{3,2,1,0:T(8,128)S(1)}, u32[]{:S(2)}, u32[]{:S(2)}) collective-permute-start(f32[2,2,80,128]{3,2,1,0:T(8,128)S(1)} %fusion.16), channel_id=1, source_target_pairs={{0,48},{16,32},{32,16},{48,0},{1,49},{17,33},{33,17},{49,1},{2,50}... | collective-permute-start | bytes 491528 | tf_op jit(solution)/shard_map/ppermute | solution.py:29
  59.0 0.9 fusion.35
  59.9 5.8 %collective-permute-done.27 = f32[2,2,80,128]{3,2,1,0:T(8,128)S(1)} collective-permute-done((f32[2,2,80,128]{3,2,1,0:T(8,128)S(1)}, f32[2,2,80,128]{3,2,1,0:T(8,128)S(1)}, u32[]{:S(2)}, u32[]{:S(2)}) %collective-permute-start.27) | collective-permute-done | bytes 163872 | tf_op jit(solution)/shard_map/ppermute | solution.py:29
  65.6 2.2 %collective-permute-start.23 = (f32[2,80,128]{2,1,0:T(8,128)S(1)}, f32[2,80,128]{2,1,0:T(8,128)S(1)}, u32[]{:S(2)}, u32[]{:S(2)}) collective-permute-start(f32[2,80,128]{2,1,0:T(8,128)S(1)} %fusion.35), channel_id=1, source_target_pairs={{0,192},{64,128},{128,64},{192,0},{1,193},{65,129},{129,65},{193,1... | collective-permute-start | bytes 245768 | tf_op jit(solution)/shard_map/ppermute | solution.py:29
  68.8 1.2 fusion.3
  70.0 2.1 %collective-permute-start.11 = (f32[2,2,2,144,128]{4,3,2,1,0:T(8,128)S(1)}, f32[2,2,2,144,128]{4,3,2,1,0:T(8,128)S(1)}, u32[]{:S(2)}, u32[]{:S(2)}) collective-permute-start(f32[2,2,2,144,128]{4,3,2,1,0:T(8,128)S(1)} %fusion.3), channel_id=1, source_target_pairs={{0,64},{64,0},{128,192},{192,128},{1,65},{65,1},{129,193},{193,129... | collective-permute-start | bytes 1769480 | tf_op jit(solution)/shard_map/ppermute | solution.py:29
  72.2 1.7 collective-permute-start.16
  74.7 5.1 %collective-permute-start.24 = (f32[80,128]{1,0:T(8,128)S(1)}, f32[80,128]{1,0:T(8,128)S(1)}, u32[]{:S(2)}, u32[]{:S(2)}) collective-permute-start(f32[80,128]{1,0:T(8,128)S(1)} %fusion.88), channel_id=1, source_target_pairs={{0,48},{16,32},{32,16},{48,0},{1,49},{17,33},{33,17},{49,1},{2,50}... | collective-permute-start | bytes 122888 | tf_op jit(solution)/shard_map/ppermute | solution.py:29
  81.2 4.7 %collective-permute-done.11 = f32[2,2,2,144,128]{4,3,2,1,0:T(8,128)S(1)} collective-permute-done((f32[2,2,2,144,128]{4,3,2,1,0:T(8,128)S(1)}, f32[2,2,2,144,128]{4,3,2,1,0:T(8,128)S(1)}, u32[]{:S(2)}, u32[]{:S(2)}) %collective-permute-start.11) | collective-permute-done | bytes 589856 | tf_op jit(solution)/shard_map/ppermute | solution.py:29
  86.1 1.0 fusion.14
  87.1 5.9 %collective-permute-start.12 = (f32[2,2,144,128]{3,2,1,0:T(8,128)S(1)}, f32[2,2,144,128]{3,2,1,0:T(8,128)S(1)}, u32[]{:S(2)}, u32[]{:S(2)}) collective-permute-start(f32[2,2,144,128]{3,2,1,0:T(8,128)S(1)} %fusion.14), channel_id=1, source_target_pairs={{0,16},{16,0},{32,48},{48,32},{1,17},{17,1},{33,49},{49,33},{2,18}... | collective-permute-start | bytes 884744 | tf_op jit(solution)/shard_map/ppermute | solution.py:29
  93.1 3.7 %collective-permute-done.1 = f32[2,2,2,160,128]{4,3,2,1,0:T(8,128)S(1)} collective-permute-done((f32[2,2,2,160,128]{4,3,2,1,0:T(8,128)S(1)}, f32[2,2,2,160,128]{4,3,2,1,0:T(8,128)S(1)}, u32[]{:S(2)}, u32[]{:S(2)}) %collective-permute-start.1) | collective-permute-done | bytes 655392 | tf_op jit(solution)/shard_map/ppermute | solution.py:29
  96.8 2.8 %collective-permute-start.17 = (f32[2,2,144,128]{3,2,1,0:T(8,128)S(1)}, f32[2,2,144,128]{3,2,1,0:T(8,128)S(1)}, u32[]{:S(2)}, u32[]{:S(2)}) collective-permute-start(f32[2,2,144,128]{3,2,1,0:T(8,128)S(1)} %fusion.12), channel_id=1, source_target_pairs={{0,48},{16,32},{32,16},{48,0},{1,49},{17,33},{33,17},{49,1},{2,50}... | collective-permute-start | bytes 884744 | tf_op jit(solution)/shard_map/ppermute | solution.py:29
  99.7 5.9 %collective-permute-start.2 = (f32[2,2,160,128]{3,2,1,0:T(8,128)S(1)}, f32[2,2,160,128]{3,2,1,0:T(8,128)S(1)}, u32[]{:S(2)}, u32[]{:S(2)}) collective-permute-start(f32[2,2,160,128]{3,2,1,0:T(8,128)S(1)} %fusion.10), channel_id=1, source_target_pairs={{0,16},{16,0},{32,48},{48,32},{1,17},{17,1},{33,49},{49,33},{2,18}... | collective-permute-start | bytes 983048 | tf_op jit(solution)/shard_map/ppermute | solution.py:29
  105.7 2.1 %collective-permute-start.7 = (f32[2,2,160,128]{3,2,1,0:T(8,128)S(1)}, f32[2,2,160,128]{3,2,1,0:T(8,128)S(1)}, u32[]{:S(2)}, u32[]{:S(2)}) collective-permute-start(f32[2,2,160,128]{3,2,1,0:T(8,128)S(1)} %fusion.8), channel_id=1, source_target_pairs={{0,48},{16,32},{32,16},{48,0},{1,49},{17,33},{33,17},{49,1},{2,50}... | collective-permute-start | bytes 983048 | tf_op jit(solution)/shard_map/ppermute | solution.py:29
  107.7 0.9 fusion.29
  109.0 2.1 %collective-permute-start.13 = (f32[2,144,128]{2,1,0:T(8,128)S(1)}, f32[2,144,128]{2,1,0:T(8,128)S(1)}, u32[]{:S(2)}, u32[]{:S(2)}) collective-permute-start(f32[2,144,128]{2,1,0:T(8,128)S(1)} %fusion.29), channel_id=1, source_target_pairs={{0,192},{64,128},{128,64},{192,0},{1,193},{65,129},{129,65},{193,1... | collective-permute-start | bytes 442376 | tf_op jit(solution)/shard_map/ppermute | solution.py:29
  111.1 4.2 %collective-permute-done.13 = f32[2,144,128]{2,1,0:T(8,128)S(1)} collective-permute-done((f32[2,144,128]{2,1,0:T(8,128)S(1)}, f32[2,144,128]{2,1,0:T(8,128)S(1)}, u32[]{:S(2)}, u32[]{:S(2)}) %collective-permute-start.13) | collective-permute-done | bytes 147488 | tf_op jit(solution)/shard_map/ppermute | solution.py:29
  115.4 1.6 collective-permute-start.18
  117.0 0.9 fusion.68
  117.9 2.6 %collective-permute-done.18 = f32[2,144,128]{2,1,0:T(8,128)S(1)} collective-permute-done((f32[2,144,128]{2,1,0:T(8,128)S(1)}, f32[2,144,128]{2,1,0:T(8,128)S(1)}, u32[]{:S(2)}, u32[]{:S(2)}) %collective-permute-start.18) | collective-permute-done | bytes 147488 | tf_op jit(solution)/shard_map/ppermute | solution.py:29
  120.5 4.7 %collective-permute-start.14 = (f32[144,128]{1,0:T(8,128)S(1)}, f32[144,128]{1,0:T(8,128)S(1)}, u32[]{:S(2)}, u32[]{:S(2)}) collective-permute-start(f32[144,128]{1,0:T(8,128)S(1)} %fusion.68), channel_id=1, source_target_pairs={{0,48},{16,32},{32,16},{48,0},{1,49},{17,33},{33,17},{49,1},{2,50}... | collective-permute-start | bytes 221192 | tf_op jit(solution)/shard_map/ppermute | solution.py:29
  125.3 8.9 %collective-permute-start.19 = (f32[144,128]{1,0:T(8,128)S(1)}, f32[144,128]{1,0:T(8,128)S(1)}, u32[]{:S(2)}, u32[]{:S(2)}) collective-permute-start(f32[144,128]{1,0:T(8,128)S(1)} %fusion.58), channel_id=1, source_target_pairs={{0,16},{16,0},{32,48},{48,32},{1,17},{17,1},{33,49},{49,33},{2,18}... | collective-permute-start | bytes 221192 | tf_op jit(solution)/shard_map/ppermute | solution.py:29
  134.3 2.2 %collective-permute-start.3 = (f32[2,160,128]{2,1,0:T(8,128)S(1)}, f32[2,160,128]{2,1,0:T(8,128)S(1)}, u32[]{:S(2)}, u32[]{:S(2)}) collective-permute-start(f32[2,160,128]{2,1,0:T(8,128)S(1)} %fusion.23), channel_id=1, source_target_pairs={{0,192},{64,128},{128,64},{192,0},{1,193},{65,129},{129,65},{193,1... | collective-permute-start | bytes 491528 | tf_op jit(solution)/shard_map/ppermute | solution.py:29
  136.5 4.4 %collective-permute-done.3 = f32[2,160,128]{2,1,0:T(8,128)S(1)} collective-permute-done((f32[2,160,128]{2,1,0:T(8,128)S(1)}, f32[2,160,128]{2,1,0:T(8,128)S(1)}, u32[]{:S(2)}, u32[]{:S(2)}) %collective-permute-start.3) | collective-permute-done | bytes 163872 | tf_op jit(solution)/shard_map/ppermute | solution.py:29
  141.7 4.5 %collective-permute-done.8 = f32[2,160,128]{2,1,0:T(8,128)S(1)} collective-permute-done((f32[2,160,128]{2,1,0:T(8,128)S(1)}, f32[2,160,128]{2,1,0:T(8,128)S(1)}, u32[]{:S(2)}, u32[]{:S(2)}) %collective-permute-start.8) | collective-permute-done | bytes 163872 | tf_op jit(solution)/shard_map/ppermute | solution.py:29
  146.2 4.1 %collective-permute-start.4 = (f32[160,128]{1,0:T(8,128)S(1)}, f32[160,128]{1,0:T(8,128)S(1)}, u32[]{:S(2)}, u32[]{:S(2)}) collective-permute-start(f32[160,128]{1,0:T(8,128)S(1)} %fusion.48), channel_id=1, source_target_pairs={{0,48},{16,32},{32,16},{48,0},{1,49},{17,33},{33,17},{49,1},{2,50}... | collective-permute-start | bytes 245768 | tf_op jit(solution)/shard_map/ppermute | solution.py:29
  150.4 2.5 %collective-permute-done.4 = f32[160,128]{1,0:T(8,128)S(1)} collective-permute-done((f32[160,128]{1,0:T(8,128)S(1)}, f32[160,128]{1,0:T(8,128)S(1)}, u32[]{:S(2)}, u32[]{:S(2)}) %collective-permute-start.4) | collective-permute-done | bytes 81952 | tf_op jit(solution)/shard_map/ppermute | solution.py:29
  153.0 6.2 %collective-permute-done.9 = f32[160,128]{1,0:T(8,128)S(1)} collective-permute-done((f32[160,128]{1,0:T(8,128)S(1)}, f32[160,128]{1,0:T(8,128)S(1)}, u32[]{:S(2)}, u32[]{:S(2)}) %collective-permute-start.9) | collective-permute-done | bytes 81952 | tf_op jit(solution)/shard_map/ppermute | solution.py:29
  159.2 0.9 fusion.74
  161.8 0.9 copy.14
  162.7 5.0 %all-to-all-start = ((f32[8,16,768]{2,1,0:T(8,128)}), f32[8,16,768]{2,1,0:T(8,128)S(1)}, u32[]{:S(2)}, u32[]{:S(2)}) async-start(f32[8,16,768]{2,1,0:T(8,128)} %bitcast.110), calls=%async_computation | async-start | bytes 786432 | tf_op jit(solution)/shard_map/all_to_all | solution.py:127
  167.9 1.2 collective-permute-done.30
  169.7 3.0 %collective-permute-done.31 = f32[8,128]{1,0:T(8,128)S(1)} collective-permute-done((f32[8,128]{1,0:T(8,128)S(1)}, f32[8,128]{1,0:T(8,128)S(1)}, u32[]{:S(2)}, u32[]{:S(2)}) %collective-permute-start.31) | collective-permute-done | bytes 4128 | tf_op jit(solution)/shard_map/ppermute | solution.py:29
  172.6 1.9 collective-permute-start.32
  174.6 2.9 %collective-permute-done.32 = f32[8,128]{1,0:T(8,128)S(1)} collective-permute-done((f32[8,128]{1,0:T(8,128)S(1)}, f32[8,128]{1,0:T(8,128)S(1)}, u32[]{:S(2)}, u32[]{:S(2)}) %collective-permute-start.32) | collective-permute-done | bytes 4128 | tf_op jit(solution)/shard_map/ppermute | solution.py:29
  177.4 3.6 %collective-permute-done.33 = f32[8,128]{1,0:T(8,128)S(1)} collective-permute-done((f32[8,128]{1,0:T(8,128)S(1)}, f32[8,128]{1,0:T(8,128)S(1)}, u32[]{:S(2)}, u32[]{:S(2)}) %collective-permute-start.33) | collective-permute-done | bytes 4128 | tf_op jit(solution)/shard_map/ppermute | solution.py:29
  181.1 1.5 collective-permute-start.34
  182.5 2.1 %collective-permute-done.34 = f32[8,128]{1,0:T(8,128)S(1)} collective-permute-done((f32[8,128]{1,0:T(8,128)S(1)}, f32[8,128]{1,0:T(8,128)S(1)}, u32[]{:S(2)}, u32[]{:S(2)}) %collective-permute-start.34) | collective-permute-done | bytes 4128 | tf_op jit(solution)/shard_map/ppermute | solution.py:29
  184.7 1.5 collective-permute-start.35
  186.1 2.1 %collective-permute-done.35 = f32[8,128]{1,0:T(8,128)S(1)} collective-permute-done((f32[8,128]{1,0:T(8,128)S(1)}, f32[8,128]{1,0:T(8,128)S(1)}, u32[]{:S(2)}, u32[]{:S(2)}) %collective-permute-start.35) | collective-permute-done | bytes 4128 | tf_op jit(solution)/shard_map/ppermute | solution.py:29
  188.3 2.5 %collective-permute-start.36 = (f32[8,128]{1,0:T(8,128)S(1)}, f32[8,128]{1,0:T(8,128)S(1)}, u32[]{:S(2)}, u32[]{:S(2)}) collective-permute-start(f32[8,128]{1,0:T(8,128)S(1)} %add.519), channel_id=1, source_target_pairs={{0,16},{16,0},{32,48},{48,32},{1,17},{17,1},{33,49},{49,33},{2,18}... | collective-permute-start | bytes 12296 | tf_op jit(solution)/shard_map/ppermute | solution.py:29
  190.7 2.0 %collective-permute-done.36 = f32[8,128]{1,0:T(8,128)S(1)} collective-permute-done((f32[8,128]{1,0:T(8,128)S(1)}, f32[8,128]{1,0:T(8,128)S(1)}, u32[]{:S(2)}, u32[]{:S(2)}) %collective-permute-start.36) | collective-permute-done | bytes 4128 | tf_op jit(solution)/shard_map/ppermute | solution.py:29
  192.8 3.7 %collective-permute-start.37 = (f32[8,128]{1,0:T(8,128)S(1)}, f32[8,128]{1,0:T(8,128)S(1)}, u32[]{:S(2)}, u32[]{:S(2)}) collective-permute-start(f32[8,128]{1,0:T(8,128)S(1)} %add.520), channel_id=1, source_target_pairs={{0,48},{16,32},{32,16},{48,0},{1,49},{17,33},{33,17},{49,1},{2,50}... | collective-permute-start | bytes 12296 | tf_op jit(solution)/shard_map/ppermute | solution.py:29
  196.5 2.0 %collective-permute-done.37 = f32[8,128]{1,0:T(8,128)S(1)} collective-permute-done((f32[8,128]{1,0:T(8,128)S(1)}, f32[8,128]{1,0:T(8,128)S(1)}, u32[]{:S(2)}, u32[]{:S(2)}) %collective-permute-start.37) | collective-permute-done | bytes 4128 | tf_op jit(solution)/shard_map/ppermute | solution.py:29
  200.0 1.2 multiply_subtract_fusion
  (92 shorter events, 12.7 us)
Async XLA Ops:
  0.6 2.8 %copy-start = (s32[4]{0:T(128)S(1)}, s32[4]{0:T(128)}, u32[]{:S(2)}) copy-start(s32[4]{0:T(128)} %param.9) | copy-start | bytes 52
  4.7 3.4 %copy-start.1 = (bf16[4,256,4096]{2,1,0:T(8,128)(2,1)S(1)}, bf16[4,256,4096]{2,1,0:T(8,128)(2,1)}, u32[]{:S(2)}) copy-start(bf16[4,256,4096]{2,1,0:T(8,128)(2,1)} %refs_11_.3) | copy-start | bytes 25165828
  8.1 1.4 copy-start.3
  9.5 10.4 %copy-start.4 = (bf16[4,256,768]{2,1,0:T(8,128)(2,1)S(1)}, bf16[4,256,768]{2,1,0:T(8,128)(2,1)}, u32[]{:S(2)}) copy-start(bf16[4,256,768]{2,1,0:T(8,128)(2,1)} %refs_14_.3) | copy-start | bytes 4718596
  16.4 1.1 copy-start.5
  17.5 1.1 copy-start.7
  18.6 11.1 %collective-permute-start.20 = (f32[2,2,2,2,80,128]{5,4,3,2,1,0:T(8,128)}, f32[2,2,2,2,80,128]{5,4,3,2,1,0:T(8,128)}, u32[]{:S(2)}, u32[]{:S(2)}) collective-permute-start(f32[2,2,2,2,80,128]{5,4,3,2,1,0:T(8,128)} %get-tuple-element.23), channel_id=1, source_target_pairs={{0,8},{8,0},{1,9},{9,1},{2,10},{10,2},{3,11},{11,3},{4,12},{12,4},... | collective-permute-start | bytes 1966088 | tf_op jit(solution)/shard_map/ppermute | solution.py:29
  18.6 13.9 %collective-permute-start.25 = (f32[2,2,2,2,80,128]{5,4,3,2,1,0:T(8,128)S(1)}, f32[2,2,2,2,80,128]{5,4,3,2,1,0:T(8,128)}, u32[]{:S(2)}, u32[]{:S(2)}) collective-permute-start(f32[2,2,2,2,80,128]{5,4,3,2,1,0:T(8,128)S(1)} %get-tuple-element.25), channel_id=1, source_target_pairs={{0,8},{8,0},{1,9},{9,1},{2,10},{10,2},{3,11},{11,3},{4,12},{12,4},... | collective-permute-start | bytes 1966088 | tf_op jit(solution)/shard_map/ppermute | solution.py:29
  19.1 49.7 %collective-permute-start.10 = (f32[2,2,2,2,144,128]{5,4,3,2,1,0:T(8,128)}, f32[2,2,2,2,144,128]{5,4,3,2,1,0:T(8,128)}, u32[]{:S(2)}, u32[]{:S(2)}) collective-permute-start(f32[2,2,2,2,144,128]{5,4,3,2,1,0:T(8,128)} %get-tuple-element.19), channel_id=1, source_target_pairs={{0,8},{8,0},{1,9},{9,1},{2,10},{10,2},{3,11},{11,3},{4,12},{12,4},... | collective-permute-start | bytes 3538952 | tf_op jit(solution)/shard_map/ppermute | solution.py:29
  19.8 3.4 %copy-start.2 = (bf16[4,256,4096]{2,1,0:T(8,128)(2,1)S(1)}, bf16[4,256,4096]{2,1,0:T(8,128)(2,1)}, u32[]{:S(2)}) copy-start(bf16[4,256,4096]{2,1,0:T(8,128)(2,1)} %refs_11_.3) | copy-start | bytes 25165828
  23.2 17.8 %copy-start.8 = (f32[2,2,2,2,144,128]{5,4,3,2,1,0:T(8,128)S(1)}, f32[2,2,2,2,144,128]{5,4,3,2,1,0:T(8,128)}, u32[]{:S(2)}) copy-start(f32[2,2,2,2,144,128]{5,4,3,2,1,0:T(8,128)} %copy-done.7) | copy-start | bytes 3538948
  29.7 6.1 %copy-start.6 = (f32[2,2,2,2,160,128]{5,4,3,2,1,0:T(8,128)S(1)}, f32[2,2,2,2,160,128]{5,4,3,2,1,0:T(8,128)}, u32[]{:S(2)}) copy-start(f32[2,2,2,2,160,128]{5,4,3,2,1,0:T(8,128)} %copy-done.5) | copy-start | bytes 3932164
  30.9 10.2 %collective-permute-start.21 = (f32[2,2,2,80,128]{4,3,2,1,0:T(8,128)S(1)}, f32[2,2,2,80,128]{4,3,2,1,0:T(8,128)S(1)}, u32[]{:S(2)}, u32[]{:S(2)}) collective-permute-start(f32[2,2,2,80,128]{4,3,2,1,0:T(8,128)S(1)} %fusion.6), channel_id=1, source_target_pairs={{0,64},{64,0},{128,192},{192,128},{1,65},{65,1},{129,193},{193,129... | collective-permute-start | bytes 983048 | tf_op jit(solution)/shard_map/ppermute | solution.py:29
  33.5 11.1 %collective-permute-start.26 = (f32[2,2,2,80,128]{4,3,2,1,0:T(8,128)S(1)}, f32[2,2,2,80,128]{4,3,2,1,0:T(8,128)S(1)}, u32[]{:S(2)}, u32[]{:S(2)}) collective-permute-start(f32[2,2,2,80,128]{4,3,2,1,0:T(8,128)S(1)} %fusion.5), channel_id=1, source_target_pairs={{0,192},{64,128},{128,64},{192,0},{1,193},{65,129},{129,65},{193,1... | collective-permute-start | bytes 983048 | tf_op jit(solution)/shard_map/ppermute | solution.py:29
  35.8 44.8 %collective-permute-start = (f32[2,2,2,2,160,128]{5,4,3,2,1,0:T(8,128)S(1)}, f32[2,2,2,2,160,128]{5,4,3,2,1,0:T(8,128)S(1)}, u32[]{:S(2)}, u32[]{:S(2)}) collective-permute-start(f32[2,2,2,2,160,128]{5,4,3,2,1,0:T(8,128)S(1)} %copy-done.6), channel_id=1, source_target_pairs={{0,8},{8,0},{1,9},{9,1},{2,10},{10,2},{3,11},{11,3},{4,12},{12,4},... | collective-permute-start | bytes 3932168 | tf_op jit(solution)/shard_map/ppermute | solution.py:29
  35.8 45.2 %collective-permute-start.5 = (f32[2,2,2,2,160,128]{5,4,3,2,1,0:T(8,128)S(1)}, f32[2,2,2,2,160,128]{5,4,3,2,1,0:T(8,128)S(1)}, u32[]{:S(2)}, u32[]{:S(2)}) collective-permute-start(f32[2,2,2,2,160,128]{5,4,3,2,1,0:T(8,128)S(1)} %get-tuple-element.17), channel_id=1, source_target_pairs={{0,8},{8,0},{1,9},{9,1},{2,10},{10,2},{3,11},{11,3},{4,12},{12,4},... | collective-permute-start | bytes 3932168 | tf_op jit(solution)/shard_map/ppermute | solution.py:29
  41.1 29.0 %collective-permute-start.15 = (f32[2,2,2,2,144,128]{5,4,3,2,1,0:T(8,128)S(1)}, f32[2,2,2,2,144,128]{5,4,3,2,1,0:T(8,128)S(1)}, u32[]{:S(2)}, u32[]{:S(2)}) collective-permute-start(f32[2,2,2,2,144,128]{5,4,3,2,1,0:T(8,128)S(1)} %copy-done.8), channel_id=1, source_target_pairs={{0,8},{8,0},{1,9},{9,1},{2,10},{10,2},{3,11},{11,3},{4,12},{12,4},... | collective-permute-start | bytes 3538952 | tf_op jit(solution)/shard_map/ppermute | solution.py:29
  44.7 10.6 %collective-permute-start.22 = (f32[2,2,80,128]{3,2,1,0:T(8,128)S(1)}, f32[2,2,80,128]{3,2,1,0:T(8,128)S(1)}, u32[]{:S(2)}, u32[]{:S(2)}) collective-permute-start(f32[2,2,80,128]{3,2,1,0:T(8,128)S(1)} %fusion.18), channel_id=1, source_target_pairs={{0,16},{16,0},{32,48},{48,32},{1,17},{17,1},{33,49},{49,33},{2,18}... | collective-permute-start | bytes 491528 | tf_op jit(solution)/shard_map/ppermute | solution.py:29
  55.2 10.4 %collective-permute-start.27 = (f32[2,2,80,128]{3,2,1,0:T(8,128)S(1)}, f32[2,2,80,128]{3,2,1,0:T(8,128)S(1)}, u32[]{:S(2)}, u32[]{:S(2)}) collective-permute-start(f32[2,2,80,128]{3,2,1,0:T(8,128)S(1)} %fusion.16), channel_id=1, source_target_pairs={{0,48},{16,32},{32,16},{48,0},{1,49},{17,33},{33,17},{49,1},{2,50}... | collective-permute-start | bytes 491528 | tf_op jit(solution)/shard_map/ppermute | solution.py:29
  65.6 6.5 %collective-permute-start.23 = (f32[2,80,128]{2,1,0:T(8,128)S(1)}, f32[2,80,128]{2,1,0:T(8,128)S(1)}, u32[]{:S(2)}, u32[]{:S(2)}) collective-permute-start(f32[2,80,128]{2,1,0:T(8,128)S(1)} %fusion.35), channel_id=1, source_target_pairs={{0,192},{64,128},{128,64},{192,0},{1,193},{65,129},{129,65},{193,1... | collective-permute-start | bytes 245768 | tf_op jit(solution)/shard_map/ppermute | solution.py:29
  68.7 6.0 %collective-permute-start.28 = (f32[2,80,128]{2,1,0:T(8,128)S(1)}, f32[2,80,128]{2,1,0:T(8,128)S(1)}, u32[]{:S(2)}, u32[]{:S(2)}) collective-permute-start(f32[2,80,128]{2,1,0:T(8,128)S(1)} %fusion.32), channel_id=1, source_target_pairs={{0,64},{64,0},{128,192},{192,128},{1,65},{65,1},{129,193},{193,129... | collective-permute-start | bytes 245768 | tf_op jit(solution)/shard_map/ppermute | solution.py:29
  70.0 15.9 %collective-permute-start.11 = (f32[2,2,2,144,128]{4,3,2,1,0:T(8,128)S(1)}, f32[2,2,2,144,128]{4,3,2,1,0:T(8,128)S(1)}, u32[]{:S(2)}, u32[]{:S(2)}) collective-permute-start(f32[2,2,2,144,128]{4,3,2,1,0:T(8,128)S(1)} %fusion.3), channel_id=1, source_target_pairs={{0,64},{64,0},{128,192},{192,128},{1,65},{65,1},{129,193},{193,129... | collective-permute-start | bytes 1769480 | tf_op jit(solution)/shard_map/ppermute | solution.py:29
  72.2 14.9 %collective-permute-start.16 = (f32[2,2,2,144,128]{4,3,2,1,0:T(8,128)S(1)}, f32[2,2,2,144,128]{4,3,2,1,0:T(8,128)S(1)}, u32[]{:S(2)}, u32[]{:S(2)}) collective-permute-start(f32[2,2,2,144,128]{4,3,2,1,0:T(8,128)S(1)} %fusion.2), channel_id=1, source_target_pairs={{0,192},{64,128},{128,64},{192,0},{1,193},{65,129},{129,65},{193,1... | collective-permute-start | bytes 1769480 | tf_op jit(solution)/shard_map/ppermute | solution.py:29
  74.7 85.4 %collective-permute-start.24 = (f32[80,128]{1,0:T(8,128)S(1)}, f32[80,128]{1,0:T(8,128)S(1)}, u32[]{:S(2)}, u32[]{:S(2)}) collective-permute-start(f32[80,128]{1,0:T(8,128)S(1)} %fusion.88), channel_id=1, source_target_pairs={{0,48},{16,32},{32,16},{48,0},{1,49},{17,33},{33,17},{49,1},{2,50}... | collective-permute-start | bytes 122888 | tf_op jit(solution)/shard_map/ppermute | solution.py:29
  80.6 80.3 %collective-permute-start.29 = (f32[80,128]{1,0:T(8,128)S(1)}, f32[80,128]{1,0:T(8,128)S(1)}, u32[]{:S(2)}, u32[]{:S(2)}) collective-permute-start(f32[80,128]{1,0:T(8,128)S(1)} %fusion.78), channel_id=1, source_target_pairs={{0,16},{16,0},{32,48},{48,32},{1,17},{17,1},{33,49},{49,33},{2,18}... | collective-permute-start | bytes 122888 | tf_op jit(solution)/shard_map/ppermute | solution.py:29
  81.0 15.8 %collective-permute-start.1 = (f32[2,2,2,160,128]{4,3,2,1,0:T(8,128)S(1)}, f32[2,2,2,160,128]{4,3,2,1,0:T(8,128)S(1)}, u32[]{:S(2)}, u32[]{:S(2)}) collective-permute-start(f32[2,2,2,160,128]{4,3,2,1,0:T(8,128)S(1)} %fusion.1), channel_id=1, source_target_pairs={{0,64},{64,0},{128,192},{192,128},{1,65},{65,1},{129,193},{193,129... | collective-permute-start | bytes 1966088 | tf_op jit(solution)/shard_map/ppermute | solution.py:29
  85.9 13.8 %collective-permute-start.6 = (f32[2,2,2,160,128]{4,3,2,1,0:T(8,128)S(1)}, f32[2,2,2,160,128]{4,3,2,1,0:T(8,128)S(1)}, u32[]{:S(2)}, u32[]{:S(2)}) collective-permute-start(f32[2,2,2,160,128]{4,3,2,1,0:T(8,128)S(1)} %fusion), channel_id=1, source_target_pairs={{0,192},{64,128},{128,64},{192,0},{1,193},{65,129},{129,65},{193,1... | collective-permute-start | bytes 1966088 | tf_op jit(solution)/shard_map/ppermute | solution.py:29
  87.1 18.5 %collective-permute-start.12 = (f32[2,2,144,128]{3,2,1,0:T(8,128)S(1)}, f32[2,2,144,128]{3,2,1,0:T(8,128)S(1)}, u32[]{:S(2)}, u32[]{:S(2)}) collective-permute-start(f32[2,2,144,128]{3,2,1,0:T(8,128)S(1)} %fusion.14), channel_id=1, source_target_pairs={{0,16},{16,0},{32,48},{48,32},{1,17},{17,1},{33,49},{49,33},{2,18}... | collective-permute-start | bytes 884744 | tf_op jit(solution)/shard_map/ppermute | solution.py:29
  96.8 12.2 %collective-permute-start.17 = (f32[2,2,144,128]{3,2,1,0:T(8,128)S(1)}, f32[2,2,144,128]{3,2,1,0:T(8,128)S(1)}, u32[]{:S(2)}, u32[]{:S(2)}) collective-permute-start(f32[2,2,144,128]{3,2,1,0:T(8,128)S(1)} %fusion.12), channel_id=1, source_target_pairs={{0,48},{16,32},{32,16},{48,0},{1,49},{17,33},{33,17},{49,1},{2,50}... | collective-permute-start | bytes 884744 | tf_op jit(solution)/shard_map/ppermute | solution.py:29
  99.7 25.6 %collective-permute-start.2 = (f32[2,2,160,128]{3,2,1,0:T(8,128)S(1)}, f32[2,2,160,128]{3,2,1,0:T(8,128)S(1)}, u32[]{:S(2)}, u32[]{:S(2)}) collective-permute-start(f32[2,2,160,128]{3,2,1,0:T(8,128)S(1)} %fusion.10), channel_id=1, source_target_pairs={{0,16},{16,0},{32,48},{48,32},{1,17},{17,1},{33,49},{49,33},{2,18}... | collective-permute-start | bytes 983048 | tf_op jit(solution)/shard_map/ppermute | solution.py:29
  105.7 28.6 %collective-permute-start.7 = (f32[2,2,160,128]{3,2,1,0:T(8,128)S(1)}, f32[2,2,160,128]{3,2,1,0:T(8,128)S(1)}, u32[]{:S(2)}, u32[]{:S(2)}) collective-permute-start(f32[2,2,160,128]{3,2,1,0:T(8,128)S(1)} %fusion.8), channel_id=1, source_target_pairs={{0,48},{16,32},{32,16},{48,0},{1,49},{17,33},{33,17},{49,1},{2,50}... | collective-permute-start | bytes 983048 | tf_op jit(solution)/shard_map/ppermute | solution.py:29
  109.0 6.4 %collective-permute-start.13 = (f32[2,144,128]{2,1,0:T(8,128)S(1)}, f32[2,144,128]{2,1,0:T(8,128)S(1)}, u32[]{:S(2)}, u32[]{:S(2)}) collective-permute-start(f32[2,144,128]{2,1,0:T(8,128)S(1)} %fusion.29), channel_id=1, source_target_pairs={{0,192},{64,128},{128,64},{192,0},{1,193},{65,129},{129,65},{193,1... | collective-permute-start | bytes 442376 | tf_op jit(solution)/shard_map/ppermute | solution.py:29
  115.4 5.1 %collective-permute-start.18 = (f32[2,144,128]{2,1,0:T(8,128)S(1)}, f32[2,144,128]{2,1,0:T(8,128)S(1)}, u32[]{:S(2)}, u32[]{:S(2)}) collective-permute-start(f32[2,144,128]{2,1,0:T(8,128)S(1)} %fusion.26), channel_id=1, source_target_pairs={{0,64},{64,0},{128,192},{192,128},{1,65},{65,1},{129,193},{193,129... | collective-permute-start | bytes 442376 | tf_op jit(solution)/shard_map/ppermute | solution.py:29
  120.5 38.6 %collective-permute-start.14 = (f32[144,128]{1,0:T(8,128)S(1)}, f32[144,128]{1,0:T(8,128)S(1)}, u32[]{:S(2)}, u32[]{:S(2)}) collective-permute-start(f32[144,128]{1,0:T(8,128)S(1)} %fusion.68), channel_id=1, source_target_pairs={{0,48},{16,32},{32,16},{48,0},{1,49},{17,33},{33,17},{49,1},{2,50}... | collective-permute-start | bytes 221192 | tf_op jit(solution)/shard_map/ppermute | solution.py:29
  125.3 34.8 %collective-permute-start.19 = (f32[144,128]{1,0:T(8,128)S(1)}, f32[144,128]{1,0:T(8,128)S(1)}, u32[]{:S(2)}, u32[]{:S(2)}) collective-permute-start(f32[144,128]{1,0:T(8,128)S(1)} %fusion.58), channel_id=1, source_target_pairs={{0,16},{16,0},{32,48},{48,32},{1,17},{17,1},{33,49},{49,33},{2,18}... | collective-permute-start | bytes 221192 | tf_op jit(solution)/shard_map/ppermute | solution.py:29
  134.3 6.6 %collective-permute-start.3 = (f32[2,160,128]{2,1,0:T(8,128)S(1)}, f32[2,160,128]{2,1,0:T(8,128)S(1)}, u32[]{:S(2)}, u32[]{:S(2)}) collective-permute-start(f32[2,160,128]{2,1,0:T(8,128)S(1)} %fusion.23), channel_id=1, source_target_pairs={{0,192},{64,128},{128,64},{192,0},{1,193},{65,129},{129,65},{193,1... | collective-permute-start | bytes 491528 | tf_op jit(solution)/shard_map/ppermute | solution.py:29
  140.9 5.3 %collective-permute-start.8 = (f32[2,160,128]{2,1,0:T(8,128)S(1)}, f32[2,160,128]{2,1,0:T(8,128)S(1)}, u32[]{:S(2)}, u32[]{:S(2)}) collective-permute-start(f32[2,160,128]{2,1,0:T(8,128)S(1)} %fusion.20), channel_id=1, source_target_pairs={{0,64},{64,0},{128,192},{192,128},{1,65},{65,1},{129,193},{193,129... | collective-permute-start | bytes 491528 | tf_op jit(solution)/shard_map/ppermute | solution.py:29
  146.2 6.7 %collective-permute-start.4 = (f32[160,128]{1,0:T(8,128)S(1)}, f32[160,128]{1,0:T(8,128)S(1)}, u32[]{:S(2)}, u32[]{:S(2)}) collective-permute-start(f32[160,128]{1,0:T(8,128)S(1)} %fusion.48), channel_id=1, source_target_pairs={{0,48},{16,32},{32,16},{48,0},{1,49},{17,33},{33,17},{49,1},{2,50}... | collective-permute-start | bytes 245768 | tf_op jit(solution)/shard_map/ppermute | solution.py:29
  152.9 6.2 %collective-permute-start.9 = (f32[160,128]{1,0:T(8,128)S(1)}, f32[160,128]{1,0:T(8,128)S(1)}, u32[]{:S(2)}, u32[]{:S(2)}) collective-permute-start(f32[160,128]{1,0:T(8,128)S(1)} %fusion.38), channel_id=1, source_target_pairs={{0,16},{16,0},{32,48},{48,32},{1,17},{17,1},{33,49},{49,33},{2,18}... | collective-permute-start | bytes 245768 | tf_op jit(solution)/shard_map/ppermute | solution.py:29
  162.7 37.2 %copy-start.9 = (f32[16,6144]{1,0:T(8,128)S(1)}, f32[16,6144]{1,0:T(8,128)}, u32[]{:S(2)}) copy-start(f32[16,6144]{1,0:T(8,128)} %param.11) | copy-start | bytes 1179652
  162.7 37.2 %copy-start.10 = (f32[16,6144]{1,0:T(8,128)S(1)}, f32[16,6144]{1,0:T(8,128)}, u32[]{:S(2)}) copy-start(f32[16,6144]{1,0:T(8,128)} %param.12) | copy-start | bytes 1179652
  162.7 37.3 %copy-start.11 = (f32[16,6144]{1,0:T(8,128)S(1)}, f32[16,6144]{1,0:T(8,128)}, u32[]{:S(2)}) copy-start(f32[16,6144]{1,0:T(8,128)} %param.13) | copy-start | bytes 1179652
  162.7 37.2 %all-to-all-start = ((f32[8,16,768]{2,1,0:T(8,128)}), f32[8,16,768]{2,1,0:T(8,128)S(1)}, u32[]{:S(2)}, u32[]{:S(2)}) async-start(f32[8,16,768]{2,1,0:T(8,128)} %bitcast.110), calls=%async_computation | async-start | bytes 786432 | tf_op jit(solution)/shard_map/all_to_all | solution.py:127
  167.8 1.2 collective-permute-start.30
  169.0 3.6 %collective-permute-start.31 = (f32[8,128]{1,0:T(8,128)S(1)}, f32[8,128]{1,0:T(8,128)S(1)}, u32[]{:S(2)}, u32[]{:S(2)}) collective-permute-start(f32[8,128]{1,0:T(8,128)S(1)} %add.514), channel_id=1, source_target_pairs={{0,64},{64,0},{128,192},{192,128},{1,65},{65,1},{129,193},{193,129... | collective-permute-start | bytes 12296 | tf_op jit(solution)/shard_map/ppermute | solution.py:29
  172.6 4.8 %collective-permute-start.32 = (f32[8,128]{1,0:T(8,128)S(1)}, f32[8,128]{1,0:T(8,128)S(1)}, u32[]{:S(2)}, u32[]{:S(2)}) collective-permute-start(f32[8,128]{1,0:T(8,128)S(1)} %add.515), channel_id=1, source_target_pairs={{0,192},{64,128},{128,64},{192,0},{1,193},{65,129},{129,65},{193,1... | collective-permute-start | bytes 12296 | tf_op jit(solution)/shard_map/ppermute | solution.py:29
  177.4 3.6 %collective-permute-start.33 = (f32[8,128]{1,0:T(8,128)S(1)}, f32[8,128]{1,0:T(8,128)S(1)}, u32[]{:S(2)}, u32[]{:S(2)}) collective-permute-start(f32[8,128]{1,0:T(8,128)S(1)} %add.516), channel_id=1, source_target_pairs={{0,1},{1,0},{2,3},{3,2},{4,5},{5,4},{6,7},{7,6},{8,9},{9,8},{10,11... | collective-permute-start | bytes 12296 | tf_op jit(solution)/shard_map/ppermute | solution.py:29
  181.1 3.6 %collective-permute-start.34 = (f32[8,128]{1,0:T(8,128)S(1)}, f32[8,128]{1,0:T(8,128)S(1)}, u32[]{:S(2)}, u32[]{:S(2)}) collective-permute-start(f32[8,128]{1,0:T(8,128)S(1)} %add.517), channel_id=1, source_target_pairs={{0,3},{1,2},{2,1},{3,0},{4,7},{5,6},{6,5},{7,4},{8,11},{9,10},{10,... | collective-permute-start | bytes 12296 | tf_op jit(solution)/shard_map/ppermute | solution.py:29
  184.7 3.6 %collective-permute-start.35 = (f32[8,128]{1,0:T(8,128)S(1)}, f32[8,128]{1,0:T(8,128)S(1)}, u32[]{:S(2)}, u32[]{:S(2)}) collective-permute-start(f32[8,128]{1,0:T(8,128)S(1)} %add.518), channel_id=1, source_target_pairs={{0,4},{4,0},{1,5},{5,1},{2,6},{6,2},{3,7},{7,3},{8,12},{12,8},{9,1... | collective-permute-start | bytes 12296 | tf_op jit(solution)/shard_map/ppermute | solution.py:29
  188.3 4.5 %collective-permute-start.36 = (f32[8,128]{1,0:T(8,128)S(1)}, f32[8,128]{1,0:T(8,128)S(1)}, u32[]{:S(2)}, u32[]{:S(2)}) collective-permute-start(f32[8,128]{1,0:T(8,128)S(1)} %add.519), channel_id=1, source_target_pairs={{0,16},{16,0},{32,48},{48,32},{1,17},{17,1},{33,49},{49,33},{2,18}... | collective-permute-start | bytes 12296 | tf_op jit(solution)/shard_map/ppermute | solution.py:29
  192.8 5.7 %collective-permute-start.37 = (f32[8,128]{1,0:T(8,128)S(1)}, f32[8,128]{1,0:T(8,128)S(1)}, u32[]{:S(2)}, u32[]{:S(2)}) collective-permute-start(f32[8,128]{1,0:T(8,128)S(1)} %add.520), channel_id=1, source_target_pairs={{0,48},{16,32},{32,16},{48,0},{1,49},{17,33},{33,17},{49,1},{2,50}... | collective-permute-start | bytes 12296 | tf_op jit(solution)/shard_map/ppermute | solution.py:29

commit v2 on v0

v2 whole, which is shorter than its diff:
```python
import functools
import math

import jax
import jax.numpy as jnp
from jax import lax
from jax.experimental import pallas as pl
from jax.experimental.pallas import tpu as pltpu
from jax.sharding import Mesh
from jax.sharding import PartitionSpec as P

D = 4096
FF = 6144
BLOCK = 128
STEP = 10
LANES = 128
LIVE = 3
AXES = ("y", "z", "core", "z_lo", "x")
DP = ("y", "z", "core")
MP = ("z_lo", "x")
SIZES = {"y": 4, "z": 4, "core": 2, "z_lo": 2, "x": 4}

PAIRS = (
    (256, ((("y", 1), ("y", 3), ("z", 1), ("z", 3)), (("y", 3), ("y", 1), ("z", 3), ("z", 1)))),
    (128, ((("z", 1), ("z", 3), ("y", 1), ("y", 3)), (("z", 3), ("z", 1), ("y", 3), ("y", 1)))),
)
STREAMS = 2 * len(PAIRS)
FLAT = [sum(16 * rows for rows, _ in PAIRS[:n]) for n in range(len(PAIRS) + 1)]
ORDER = (
    "sent:00", "sent:01", "sent:10", "sent:11", "rest",
    "first:00", "start:00", "first:01", "start:01", "first:10", "start:10", "first:11", "start:11",
    "kept", "keep:00", "keep:01", "keep:10", "keep:11",
    "end:00", "start:00", "end:01", "start:01", "end:10", "start:10", "end:11", "start:11",
    "end:00", "start:00", "end:01", "start:01", "end:10", "start:10", "end:11", "start:11",
    "end:10", "start:10", "end:11", "start:11", "end:00", "start:00", "end:01", "start:01",
    "end:10", "end:11", "end:00", "end:01",
)


def swap(value, axis, mask):
    return lax.ppermute(value, axis, [(i, i ^ mask) for i in range(SIZES[axis])])


def place_of_tile(step, t, core):
    y_off = (1 - step // 2) * 1 ^ (1 - step % 2) * 3
    z_off = (1 - t // 2) * 1 ^ (1 - t % 2) * 3
    y, z = lax.axis_index("y") ^ y_off, lax.axis_index("z") ^ z_off
    return (y * 4 + z) * 2 + core


def multiply(mt_ref, x_buf, stores, ready=lambda i: None):
    for i in range(4):
        ready(i)
        runs, first = [], 0
        for n, (rows, kinds) in enumerate(PAIRS):
            for half, steps in enumerate(kinds):
                tiles = []
                for t in range(4):
                    bit = {("y", 1): i // 2, ("y", 3): i % 2, ("z", 1): t // 2, ("z", 3): t % 2}
                    at = [bit[step] for step in steps]
                    if stores[at[0]]:
                        tiles.append((t, at[0], 4 * at[1] + 2 * at[2] + at[3]))
                lanes = [t for t, _, _ in tiles]
                if runs and runs[-1][0] == lanes:
                    runs[-1][1].append((n, half, first, tiles))
                else:
                    runs.append((lanes, [(n, half, first, tiles)]))
                first += rows
        for lanes, members in runs:
            if not lanes:
                continue
            low, high = members[0][2], members[-1][2] + PAIRS[members[-1][0]][0]
            pieces = [x_buf[i, :, :, t * LANES : (t + 1) * LANES] for t in lanes]
            right = x_buf[i] if len(lanes) == 4 else jnp.concatenate(pieces, axis=2)
            total = jnp.dot(
                mt_ref[low:high],
                right.reshape(LIVE * 256, len(lanes) * LANES),
                preferred_element_type=jnp.float32,
            )
            for n, half, first, tiles in members:
                rows = slice(first - low, first - low + PAIRS[n][0])
                for k, (_, kept, place) in enumerate(tiles):
                    stores[kept](n, half, place, total[rows, k * LANES : (k + 1) * LANES])


def into(refs):
    def store(n, half, place, value):
        refs[2 * n + half][place // 4, place // 2 % 2, place % 2] = value

    return store


def into_flat(ref):
    def store(n, half, place, value):
        rows = PAIRS[n][0]
        first = FLAT[n] + (8 * half + place) * rows
        ref[first : first + rows] = value

    return store


def load_numbers(ff_hbm, active_hbm, ff_ref, active_ref, sem):
    copies = [
        pltpu.make_async_copy(ff_hbm, ff_ref, sem.at[0]),
        pltpu.make_async_copy(active_hbm, active_ref, sem.at[1]),
    ]
    for c in copies:
        c.start()
    for c in copies:
        c.wait()
    idle = sum(jnp.where(active_ref[i] == 1, 0, i) for i in range(1, 4))
    return [s + (s >= idle).astype(jnp.int32) for s in range(LIVE)]


def load_tiles(x_ref, x_buf, x_sem, live, core):
    for i in range(4):
        for t in range(4):
            column = pl.multiple_of(place_of_tile(i, t, core) * LANES, LANES)
            for s in range(LIVE):
                pltpu.make_async_copy(
                    x_ref.at[live[s], :, pl.ds(column, LANES)],
                    x_buf.at[i, s, :, pl.ds(t * LANES, LANES)],
                    x_sem.at[i],
                ).start()

    def ready(i):
        pltpu.make_async_copy(x_buf.at[i], x_buf.at[i], x_sem.at[i]).wait()

    return ready


def sent_kernel(ff_hbm, active_hbm, x_ref, m_ref, *refs):
    outs, refs = refs[:STREAMS], refs[STREAMS:]
    x_buf, mt_ref, ff_ref, active_ref, sem, x_sem, m_buf, m_sem = refs
    live = load_numbers(ff_hbm, active_hbm, ff_ref, active_ref, sem)
    for s in range(LIVE):
        pltpu.make_async_copy(m_ref.at[live[s]], m_buf.at[s], m_sem).start()
    ready = load_tiles(x_ref, x_buf, x_sem, live, 1 - lax.axis_index("core"))
    pltpu.make_async_copy(m_buf, m_buf, m_sem).wait()
    cols = m_buf.shape[2]
    first = lax.axis_index(MP) * cols
    for s in range(LIVE):
        values = m_buf[s]
        column = first + lax.broadcasted_iota(jnp.int32, values.shape, 1)
        keep = column < BLOCK * ff_ref[live[s]]
        values = jnp.where(keep, values, jnp.zeros_like(values))
        mt_ref[:, s * 256 : (s + 1) * 256] = values.T
    multiply(mt_ref, x_buf, (into(outs), None), ready)


def rest_kernel(ff_hbm, active_hbm, x_ref, mt_ref, other_x, *refs):
    other_kept, refs = refs[0], refs[1:]
    sent, kept = refs[:STREAMS], refs[STREAMS : 2 * STREAMS]
    ff_ref, active_ref, sem, x_buf, x_sem = refs[2 * STREAMS :]
    live = load_numbers(ff_hbm, active_hbm, ff_ref, active_ref, sem)
    ready = load_tiles(x_ref, x_buf, x_sem, live, lax.axis_index("core"))
    multiply(mt_ref, other_x, (None, into_flat(other_kept)))
    multiply(mt_ref, x_buf, (into(sent), into(kept)), ready)


def call(kernel, operands, spaces, out_shape, scratch, mebibytes):
    return pl.pallas_call(
        kernel,
        in_specs=[pl.BlockSpec(memory_space=space) for space in spaces],
        out_specs=[pl.BlockSpec(memory_space=pltpu.VMEM)] * len(out_shape),
        scratch_shapes=[
            pltpu.SMEM((4,), jnp.int32),
            pltpu.SMEM((4,), jnp.int32),
            pltpu.SemaphoreType.DMA((2,)),
            *scratch,
        ],
        out_shape=out_shape,
        compiler_params=pltpu.CompilerParams(vmem_limit_bytes=mebibytes * 1024 * 1024),
    )(*(pltpu.with_memory_space_constraint(o, s) for o, s in zip(operands, spaces)))


def products(ff_blocks, layer_active, x, m):
    hbm, vmem = pltpu.HBM, pltpu.VMEM
    pieces = [vmem((2, 2, 2, rows, LANES), jnp.float32) for rows, _ in PAIRS for _ in range(2)]
    tiles = vmem((4, LIVE, 256, 4 * LANES), jnp.bfloat16)
    sems = pltpu.SemaphoreType.DMA((4,))
    turned = vmem((m.shape[2], LIVE * 256), jnp.bfloat16)
    *sent, other_x, turned = call(
        sent_kernel,
        (ff_blocks, layer_active, x, m),
        (hbm, hbm, hbm, hbm),
        pieces + [tiles, turned],
        [sems, vmem((LIVE, 256, m.shape[2]), jnp.bfloat16), pltpu.SemaphoreType.DMA],
        6,
    )

    def rest(tie):
        return call(
            rest_kernel,
            (ff_blocks, layer_active, x, tie(turned), other_x),
            (hbm, hbm, hbm, vmem, vmem),
            [vmem((FLAT[-1], LANES), jnp.float32)] + pieces + pieces,
            [tiles, sems],
            8,
        )

    return sent, rest


class Stream:
    def __init__(self, steps):
        self.steps, self.at = steps, 0
        self.send = self.keep = self.flying = None


class Line:
    def __init__(self, token):
        self.token = token

    def tie(self, *values):
        *values, self.token = lax.optimization_barrier((*values, self.token))
        return values[0] if len(values) == 1 else values

    def first(self, stream, own, other):
        stream.send = self.token = self.tie(own + other)

    def keep(self, stream, own, other):
        stream.keep = self.token = self.tie(own + other)
        stream.keep = [stream.keep]

    def start(self, stream):
        axis, mask = stream.steps[stream.at]
        self.token = send = self.tie(stream.send)
        stream.flying = swap(send, axis, mask)
        stream.at += 1

    def end(self, stream):
        parts = stream.keep + [self.tie(stream.flying)]
        if stream.at < len(stream.steps):
            stream.send = self.token = self.tie(sum(p[0] for p in parts[1:]) + parts[0][0])
            stream.keep = [p[1] for p in parts]
        else:
            stream.send = self.token = self.tie(sum(parts[1:]) + parts[0])


def shards(inputs, gate_cotangent, ff_blocks, layer_active, param, moment, second_moment):
    sent, rest = products(ff_blocks, layer_active, inputs, gate_cotangent)
    flying, line = {}, Line(sent[0])
    streams = {(n, half): Stream(pair[1][half]) for n, pair in enumerate(PAIRS) for half in range(2)}
    for act, *names in (event.split(":") for event in ORDER):
        if act == "rest":
            other_kept, *owns = rest(line.tie)
            line.token = owns[0]
            continue
        if act == "kept":
            line.token = line.tie(other_kept)
            flat = line.tie(swap(line.token, "core", 1))
            continue
        n, half = (int(c) for c in names[0])
        if act == "sent":
            line.token = line.tie(sent[2 * n + half])
            flying[n, half] = swap(line.token, "core", 1)
        elif act == "first":
            line.first(streams[n, half], owns[2 * n + half], line.tie(flying[n, half]))
        elif act == "keep":
            own = owns[STREAMS + 2 * n + half]
            first = FLAT[n] + half * own.size // LANES
            other = flat[first : first + own.size // LANES].reshape(own.shape)
            line.keep(streams[n, half], own, other)
        else:
            getattr(line, act)(streams[n, half])
    done = [stream.send for stream in streams.values()]
    squares = sum(jnp.sum(t * t, axis=0, keepdims=True) for t in done)
    devices = math.prod(SIZES[a] for a in DP)
    squares = lax.all_to_all(jnp.broadcast_to(squares[None], (devices, 1, LANES)), DP, 0, 0, tiled=True)
    squares = jnp.sum(squares, axis=0)
    blocks = jnp.concatenate(done, axis=0).T.reshape(8, -1, gate_cotangent.shape[2])
    beside = jnp.broadcast_to(squares[None], blocks.shape[:2] + (LANES,))
    blocks = lax.all_to_all(jnp.concatenate([blocks, beside], axis=2), MP, 0, 0, tiled=True)
    total = jnp.sqrt(jnp.sum(blocks[:, 0, -LANES:]))
    gradient = blocks[:, :, :-LANES].transpose(1, 0, 2).reshape(param.shape)
    factor = jnp.minimum(1.0, math.sqrt(1.0 * D * FF) / (total + 1e-06))
    clipped = gradient * factor
    new_moment = 0.9 * moment + 0.1 * clipped
    new_second = 0.95 * second_moment + 0.05 * clipped * clipped
    first_hat = new_moment / (1.0 - 0.9**STEP)
    second_hat = new_second / (1.0 - 0.95**STEP)
    new_param = param - 0.02 * (first_hat / (jnp.sqrt(second_hat) + 1e-08) + 0.1 * param)
    return (new_param, new_moment, new_second)


def solution(mesh):
    split = Mesh(mesh.devices.reshape(4, 4, 2, 2, 4), AXES)
    rows = P(AXES, None)
    return jax.shard_map(
        shards,
        mesh=split,
        in_specs=(P(None, DP, None), P(None, DP, MP), P(), P(), rows, rows, rows),
        out_specs=(rows, rows, rows),
        check_vma=False,
    )
```

time: 231 us -> 120 us (0.52)
  waiting for transfers between devices: 146 us -> 47.3 us
  starting transfers between devices: 0.04 us -> 40.7 us
  blocking collectives: 52.3 us -> 13.8 us
  matrix products: 13.3 us -> 0 us
  between operations: 14.8 us -> 1.69 us
  Pallas kernels: 0 us -> 11.6 us
    reduce_scatter x1 -> x0, waiting for transfers between devices: 146 us -> none  [shards(): lax.psum_scatter(lax.dot_general(rows_in, rows_ct, (((0,), (0,)), ((), ()...]
    psum x5 -> x0, blocking collectives: 41.2 us -> none  [over_axes(): x = lax.psum(x, axis)]
    ppermute x0 -> x21, waiting for transfers between devices: none -> 37.8 us  [swap(): lax.ppermute(value, axis, [(i, i ^ mask) for i in range(SIZES[axis])])]
    ppermute x0 -> x21, starting transfers between devices: none -> 36.1 us  [swap(): lax.ppermute(value, axis, [(i, i ^ mask) for i in range(SIZES[axis])])]
    dot_general x1 -> x0, matrix products: 13.3 us -> none  [shards(): lax.dot_general(rows_in, rows_ct, (((0,), (0,)), ((), ())), preferred_ele...]
    pallas_call x0 -> x2, Pallas kernels: none -> 11.6 us  [call(): pl.pallas_call(kernel, in_specs=[pl.BlockSpec(memory_space=space) for spa...]
    all_to_all x0 -> x1, waiting for transfers between devices: none -> 9.53 us  [shards(): lax.all_to_all(jnp.broadcast_to(squares[None], (devices, 1, LANES)), DP,...]
    all_to_all x0 -> x1, starting transfers between devices: none -> 4.66 us  [shards(): lax.all_to_all(jnp.broadcast_to(squares[None], (devices, 1, LANES)), DP,...]
  transfers between devices with their start and end apart: 1 -> 22, of which waited for: 1 -> 9; matrix products, arithmetic and copies ran while one was open for 0% -> 1% of each run, Pallas kernels for 0% -> 5%
where the time goes in v2:
time: 120 us; the launch traced here: 119 us
  waiting for transfers between devices  47.3 us (39%)
  starting transfers between devices  40.7 us (34%)
  blocking collectives  13.8 us (12%)
  Pallas kernels  11.6 us (10%)
  other arithmetic  3.29 us (3%)
  between operations  1.69 us (1%)
    ppermute x21, waiting for transfers between devices, swap(): lax.ppermute(value, axis, [(i, i ^ mask) for i in range(SIZES[axis])])  37.8 us
    ppermute x21, starting transfers between devices, swap(): lax.ppermute(value, axis, [(i, i ^ mask) for i in range(SIZES[axis])])  36.1 us
    all_to_all x1, blocking collectives, shards(): lax.all_to_all(jnp.concatenate([blocks, beside], axis=2), MP, 0, 0, tiled...  13.8 us
    pallas_call x2, Pallas kernels, call(): pl.pallas_call(kernel, in_specs=[pl.BlockSpec(memory_space=space) for spa...  11.6 us
    all_to_all x1, waiting for transfers between devices, shards(): lax.all_to_all(jnp.broadcast_to(squares[None], (devices, 1, LANES)), DP,...  9.53 us
    all_to_all x1, starting transfers between devices, shards(): lax.all_to_all(jnp.broadcast_to(squares[None], (devices, 1, LANES)), DP,...  4.66 us
  transfers between devices with their start and end apart: 22, of which 9 were waited for; matrix products, arithmetic and copies ran while one was open for 1% of the time, Pallas kernels for 5%

profile of v2, /device:TPU:2, one launch (start us, length us, event | category | flops | bytes accessed | tf_op | source)
XLA Modules:
  0.0 119.5 jit_solution(13895618604082362482)
XLA Ops:
  0.6 5.4 %shard_map.94 = (f32[2,2,2,256,128]{4,3,2,1,0:T(8,128)S(1)}, f32[2,2,2,256,128]{4,3,2,1,0:T(8,128)S(1)}, f32[2,2,2,128,128]{4,3,2,1,0:T(8,128)S(1)}, f32[2,2,2,1...) custom-call(s32[4]{0:T(128)} %ff_hbm.3, s32[4]{0:T(128)} %active_hbm.3, ...), custom_call_target="tpu_custom_call" | custom-call | tf_op jit(solution)/shard_map/pallas_call | solution.py:162
  6.0 0.1 collective-permute-start
  6.1 0.5 collective-permute-start.4
  6.6 0.1 collective-permute-start.3
  6.7 0.4 collective-permute-start.2
  7.2 6.2 %shard_map.95 = (f32[6144,128]{1,0:T(8,128)S(1)}, f32[2,2,2,256,128]{4,3,2,1,0:T(8,128)S(1)}, f32[2,2,2,256,128]{4,3,2,1,0:T(8,128)S(1)}, f32[2,2,2,128,128]{4,3...) custom-call(s32[4]{0:T(128)} %ff_hbm.3, ...), custom_call_target="tpu_custom_call" | custom-call | tf_op jit(solution)/shard_map/pallas_call | solution.py:162
  13.4 0.1 add.201
  13.5 0.0 collective-permute-done.4
  13.5 0.1 add.202
  13.7 0.0 collective-permute-done.3
  13.7 0.1 add.203
  13.7 0.1 add.204
  13.8 0.2 collective-permute-start.5
  14.0 1.6 %collective-permute-start.1 = (f32[2,2,2,256,128]{4,3,2,1,0:T(8,128)S(1)}, f32[2,2,2,256,128]{4,3,2,1,0:T(8,128)S(1)}, u32[]{:S(2)}, u32[]{:S(2)}) collective-permute-start(f32[2,2,2,256,128]{4,3,2,1,0:T(8,128)S(1)} %add.201), channel_id=1, source_target_pairs={{0,64},{64,0},{128,192},{192,128},{1,65},{65,1},{129,193},{193,129... | collective-permute-start | bytes 3145736 | tf_op jit(solution)/shard_map/ppermute | solution.py:41
  15.6 6.3 %collective-permute-start.7 = (f32[2,2,2,128,128]{4,3,2,1,0:T(8,128)S(1)}, f32[2,2,2,128,128]{4,3,2,1,0:T(8,128)S(1)}, u32[]{:S(2)}, u32[]{:S(2)}) collective-permute-start(f32[2,2,2,128,128]{4,3,2,1,0:T(8,128)S(1)} %add.204), channel_id=1, source_target_pairs={{0,48},{16,32},{32,16},{48,0},{1,49},{17,33},{33,17},{49,1},{2,50}... | collective-permute-start | bytes 1572872 | tf_op jit(solution)/shard_map/ppermute | solution.py:41
  21.9 1.5 %collective-permute-start.8 = (f32[2,2,2,128,128]{4,3,2,1,0:T(8,128)S(1)}, f32[2,2,2,128,128]{4,3,2,1,0:T(8,128)S(1)}, u32[]{:S(2)}, u32[]{:S(2)}) collective-permute-start(f32[2,2,2,128,128]{4,3,2,1,0:T(8,128)S(1)} %add.203), channel_id=1, source_target_pairs={{0,16},{16,0},{32,48},{48,32},{1,17},{17,1},{33,49},{49,33},{2,18}... | collective-permute-start | bytes 1572872 | tf_op jit(solution)/shard_map/ppermute | solution.py:41
  23.3 2.2 %collective-permute-start.9 = (f32[2,2,2,256,128]{4,3,2,1,0:T(8,128)S(1)}, f32[2,2,2,256,128]{4,3,2,1,0:T(8,128)S(1)}, u32[]{:S(2)}, u32[]{:S(2)}) collective-permute-start(f32[2,2,2,256,128]{4,3,2,1,0:T(8,128)S(1)} %add.202), channel_id=1, source_target_pairs={{0,192},{64,128},{128,64},{192,0},{1,193},{65,129},{129,65},{193,1... | collective-permute-start | bytes 3145736 | tf_op jit(solution)/shard_map/ppermute | solution.py:41
  25.5 0.0 collective-permute-done.5
  25.5 0.1 fusion.11
  25.7 0.1 add.208
  25.8 0.1 add.207
  25.9 0.1 fusion.12
  26.0 0.1 add.206
  26.0 0.1 add.205
  26.1 13.4 %collective-permute-done.1 = f32[2,2,2,256,128]{4,3,2,1,0:T(8,128)S(1)} collective-permute-done((f32[2,2,2,256,128]{4,3,2,1,0:T(8,128)S(1)}, f32[2,2,2,256,128]{4,3,2,1,0:T(8,128)S(1)}, u32[]{:S(2)}, u32[]{:S(2)}) %collective-permute-start.1) | collective-permute-done | bytes 1048608 | tf_op jit(solution)/shard_map/ppermute | solution.py:41
  39.5 0.1 fusion
  39.5 3.1 %collective-permute-start.6 = (f32[2,2,256,128]{3,2,1,0:T(8,128)S(1)}, f32[2,2,256,128]{3,2,1,0:T(8,128)S(1)}, u32[]{:S(2)}, u32[]{:S(2)}) collective-permute-start(f32[2,2,256,128]{3,2,1,0:T(8,128)S(1)} %fusion), channel_id=1, source_target_pairs={{0,192},{64,128},{128,64},{192,0},{1,193},{65,129},{129,65},{193,1... | collective-permute-start | bytes 1572872 | tf_op jit(solution)/shard_map/ppermute | solution.py:41
  42.7 8.0 %collective-permute-done.9 = f32[2,2,2,256,128]{4,3,2,1,0:T(8,128)S(1)} collective-permute-done((f32[2,2,2,256,128]{4,3,2,1,0:T(8,128)S(1)}, f32[2,2,2,256,128]{4,3,2,1,0:T(8,128)S(1)}, u32[]{:S(2)}, u32[]{:S(2)}) %collective-permute-start.9) | collective-permute-done | bytes 1048608 | tf_op jit(solution)/shard_map/ppermute | solution.py:41
  50.6 0.1 add_bitcast_fusion
  50.7 0.1 collective-permute-start.13
  50.9 0.1 collective-permute-start.12
  50.9 0.0 collective-permute-done.7
  51.0 1.7 %collective-permute-start.11 = (f32[2,2,128,128]{3,2,1,0:T(8,128)S(1)}, f32[2,2,128,128]{3,2,1,0:T(8,128)S(1)}, u32[]{:S(2)}, u32[]{:S(2)}) collective-permute-start(f32[2,2,128,128]{3,2,1,0:T(8,128)S(1)} %add_bitcast_fusion.1), channel_id=1, source_target_pairs={{0,16},{16,0},{32,48},{48,32},{1,17},{17,1},{33,49},{49,33},{2,18}... | collective-permute-start | bytes 786440 | tf_op jit(solution)/shard_map/ppermute | solution.py:41
  52.7 7.7 %collective-permute-done.6 = f32[2,2,256,128]{3,2,1,0:T(8,128)S(1)} collective-permute-done((f32[2,2,256,128]{3,2,1,0:T(8,128)S(1)}, f32[2,2,256,128]{3,2,1,0:T(8,128)S(1)}, u32[]{:S(2)}, u32[]{:S(2)}) %collective-permute-start.6) | collective-permute-done | bytes 524320 | tf_op jit(solution)/shard_map/ppermute | solution.py:41
  60.4 0.1 fusion.3
  60.5 1.5 %collective-permute-start.10 = (f32[2,256,128]{2,1,0:T(8,128)S(1)}, f32[2,256,128]{2,1,0:T(8,128)S(1)}, u32[]{:S(2)}, u32[]{:S(2)}) collective-permute-start(f32[2,256,128]{2,1,0:T(8,128)S(1)} %fusion.3), channel_id=1, source_target_pairs={{0,16},{16,0},{32,48},{48,32},{1,17},{17,1},{33,49},{49,33},{2,18}... | collective-permute-start | bytes 786440 | tf_op jit(solution)/shard_map/ppermute | solution.py:41
  62.0 0.1 bitcast_add_fusion
  62.1 0.5 collective-permute-start.19
  62.6 0.0 collective-permute-done.12
  62.6 3.9 %collective-permute-start.15 = (f32[2,128,128]{2,1,0:T(8,128)S(1)}, f32[2,128,128]{2,1,0:T(8,128)S(1)}, u32[]{:S(2)}, u32[]{:S(2)}) collective-permute-start(f32[2,128,128]{2,1,0:T(8,128)S(1)} %bitcast_add_fusion.14), channel_id=1, source_target_pairs={{0,64},{64,0},{128,192},{192,128},{1,65},{65,1},{129,193},{193,129... | collective-permute-start | bytes 393224 | tf_op jit(solution)/shard_map/ppermute | solution.py:41
  66.5 0.0 collective-permute-done.11
  66.6 2.2 %collective-permute-start.14 = (f32[2,128,128]{2,1,0:T(8,128)S(1)}, f32[2,128,128]{2,1,0:T(8,128)S(1)}, u32[]{:S(2)}, u32[]{:S(2)}) collective-permute-start(f32[2,128,128]{2,1,0:T(8,128)S(1)} %bitcast_add_fusion.12), channel_id=1, source_target_pairs={{0,192},{64,128},{128,64},{192,0},{1,193},{65,129},{129,65},{193,1... | collective-permute-start | bytes 393224 | tf_op jit(solution)/shard_map/ppermute | solution.py:41
  68.8 0.7 collective-permute-done.15
  69.5 2.2 %collective-permute-start.18 = (f32[128,128]{1,0:T(8,128)S(1)}, f32[128,128]{1,0:T(8,128)S(1)}, u32[]{:S(2)}, u32[]{:S(2)}) collective-permute-start(f32[128,128]{1,0:T(8,128)S(1)} %bitcast_add_fusion.25), channel_id=1, source_target_pairs={{0,192},{64,128},{128,64},{192,0},{1,193},{65,129},{129,65},{193,1... | collective-permute-start | bytes 196616 | tf_op jit(solution)/shard_map/ppermute | solution.py:41
  71.7 1.1 collective-permute-done.14
  72.9 0.4 collective-permute-start.17
  73.2 0.7 collective-permute-done.10
  74.0 7.4 %collective-permute-start.16 = (f32[256,128]{1,0:T(8,128)S(1)}, f32[256,128]{1,0:T(8,128)S(1)}, u32[]{:S(2)}, u32[]{:S(2)}) collective-permute-start(f32[256,128]{1,0:T(8,128)S(1)} %fusion.5), channel_id=1, source_target_pairs={{0,48},{16,32},{32,16},{48,0},{1,49},{17,33},{33,17},{49,1},{2,50}... | collective-permute-start | bytes 393224 | tf_op jit(solution)/shard_map/ppermute | solution.py:41
  81.4 0.0 collective-permute-done.19
  81.4 0.1 collective-permute-start.20
  81.5 0.0 collective-permute-done.18
  81.6 0.0 collective-permute-done.17
  81.7 5.0 %collective-permute-done.16 = f32[256,128]{1,0:T(8,128)S(1)} collective-permute-done((f32[256,128]{1,0:T(8,128)S(1)}, f32[256,128]{1,0:T(8,128)S(1)}, u32[]{:S(2)}, u32[]{:S(2)}) %collective-permute-start.16) | collective-permute-done | bytes 131104 | tf_op jit(solution)/shard_map/ppermute | solution.py:41
  86.7 0.0 copy-start
  86.7 0.0 copy-start.1
  86.7 0.0 copy-start.2
  86.7 1.1 collective-permute-done.20
  88.0 0.6 broadcast_in_dim.4
  88.6 4.7 %all-to-all-start = ((f32[32,1,128]{2,1,0:T(1,128)}), f32[32,1,128]{2,1,0:T(1,128)S(1)}, u32[]{:S(2)}, u32[]{:S(2)}) async-start(f32[32,1,128]{2,1,0:T(1,128)} %broadcast_in_dim.4), calls=%async_computation | async-start | bytes 32768 | tf_op jit(solution)/shard_map/all_to_all | solution.py:270
  93.3 0.2 copy.16
  93.5 9.5 %all-to-all-done = f32[32,1,128]{2,1,0:T(1,128)S(1)} async-done(((f32[32,1,128]{2,1,0:T(1,128)}), f32[32,1,128]{2,1,0:T(1,128)S(1)}, u32[]{:S(2)}, u32[]{:S(2)}) %all-to-all-start) | async-done | bytes 16416 | tf_op jit(solution)/shard_map/all_to_all | solution.py:270
  103.1 13.8 %all_to_all.10 = f32[8,16,896]{2,1,0:T(8,128)S(1)} all-to-all(f32[8,16,896]{2,1,0:T(8,128)S(1)} %pad_maximum_fusion), channel_id=1, replica_groups=mesh['y'=4,'z'=4,'core'=2,'z_lo'=2,'x'=4] {'z_lo','x'}, dimensions={0} | all-to-all | bytes 917504 | tf_op jit(solution)/shard_map/all_to_all | solution.py:274
  116.8 0.6 slice_reduce_fusion
  118.3 1.2 multiply_subtract_fusion
  (28 shorter events, 0.7 us)
Async XLA Ops:
  6.0 7.4 %collective-permute-start = (f32[2,2,2,256,128]{4,3,2,1,0:T(8,128)S(1)}, f32[2,2,2,256,128]{4,3,2,1,0:T(8,128)S(1)}, u32[]{:S(2)}, u32[]{:S(2)}) collective-permute-start(f32[2,2,2,256,128]{4,3,2,1,0:T(8,128)S(1)} %get-tuple-element.51), channel_id=1, source_target_pairs={{0,8},{8,0},{1,9},{9,1},{2,10},{10,2},{3,11},{11,3},{4,12},{12,4},... | collective-permute-start | bytes 3145736 | tf_op jit(solution)/shard_map/ppermute | solution.py:41
  6.1 7.4 %collective-permute-start.4 = (f32[2,2,2,256,128]{4,3,2,1,0:T(8,128)S(1)}, f32[2,2,2,256,128]{4,3,2,1,0:T(8,128)S(1)}, u32[]{:S(2)}, u32[]{:S(2)}) collective-permute-start(f32[2,2,2,256,128]{4,3,2,1,0:T(8,128)S(1)} %get-tuple-element.52), channel_id=1, source_target_pairs={{0,8},{8,0},{1,9},{9,1},{2,10},{10,2},{3,11},{11,3},{4,12},{12,4},... | collective-permute-start | bytes 3145736 | tf_op jit(solution)/shard_map/ppermute | solution.py:41
  6.6 7.0 %collective-permute-start.3 = (f32[2,2,2,128,128]{4,3,2,1,0:T(8,128)S(1)}, f32[2,2,2,128,128]{4,3,2,1,0:T(8,128)S(1)}, u32[]{:S(2)}, u32[]{:S(2)}) collective-permute-start(f32[2,2,2,128,128]{4,3,2,1,0:T(8,128)S(1)} %get-tuple-element.53), channel_id=1, source_target_pairs={{0,8},{8,0},{1,9},{9,1},{2,10},{10,2},{3,11},{11,3},{4,12},{12,4},... | collective-permute-start | bytes 1572872 | tf_op jit(solution)/shard_map/ppermute | solution.py:41
  6.7 7.0 %collective-permute-start.2 = (f32[2,2,2,128,128]{4,3,2,1,0:T(8,128)S(1)}, f32[2,2,2,128,128]{4,3,2,1,0:T(8,128)S(1)}, u32[]{:S(2)}, u32[]{:S(2)}) collective-permute-start(f32[2,2,2,128,128]{4,3,2,1,0:T(8,128)S(1)} %get-tuple-element.54), channel_id=1, source_target_pairs={{0,8},{8,0},{1,9},{9,1},{2,10},{10,2},{3,11},{11,3},{4,12},{12,4},... | collective-permute-start | bytes 1572872 | tf_op jit(solution)/shard_map/ppermute | solution.py:41
  13.8 11.7 %collective-permute-start.5 = (f32[6144,128]{1,0:T(8,128)S(1)}, f32[6144,128]{1,0:T(8,128)S(1)}, u32[]{:S(2)}, u32[]{:S(2)}) collective-permute-start(f32[6144,128]{1,0:T(8,128)S(1)} %get-tuple-element.67), channel_id=1, source_target_pairs={{0,8},{8,0},{1,9},{9,1},{2,10},{10,2},{3,11},{11,3},{4,12},{12,4},... | collective-permute-start | bytes 9437192 | tf_op jit(solution)/shard_map/ppermute | solution.py:41
  14.0 25.5 %collective-permute-start.1 = (f32[2,2,2,256,128]{4,3,2,1,0:T(8,128)S(1)}, f32[2,2,2,256,128]{4,3,2,1,0:T(8,128)S(1)}, u32[]{:S(2)}, u32[]{:S(2)}) collective-permute-start(f32[2,2,2,256,128]{4,3,2,1,0:T(8,128)S(1)} %add.201), channel_id=1, source_target_pairs={{0,64},{64,0},{128,192},{192,128},{1,65},{65,1},{129,193},{193,129... | collective-permute-start | bytes 3145736 | tf_op jit(solution)/shard_map/ppermute | solution.py:41
  15.6 35.4 %collective-permute-start.7 = (f32[2,2,2,128,128]{4,3,2,1,0:T(8,128)S(1)}, f32[2,2,2,128,128]{4,3,2,1,0:T(8,128)S(1)}, u32[]{:S(2)}, u32[]{:S(2)}) collective-permute-start(f32[2,2,2,128,128]{4,3,2,1,0:T(8,128)S(1)} %add.204), channel_id=1, source_target_pairs={{0,48},{16,32},{32,16},{48,0},{1,49},{17,33},{33,17},{49,1},{2,50}... | collective-permute-start | bytes 1572872 | tf_op jit(solution)/shard_map/ppermute | solution.py:41
  21.9 28.9 %collective-permute-start.8 = (f32[2,2,2,128,128]{4,3,2,1,0:T(8,128)S(1)}, f32[2,2,2,128,128]{4,3,2,1,0:T(8,128)S(1)}, u32[]{:S(2)}, u32[]{:S(2)}) collective-permute-start(f32[2,2,2,128,128]{4,3,2,1,0:T(8,128)S(1)} %add.203), channel_id=1, source_target_pairs={{0,16},{16,0},{32,48},{48,32},{1,17},{17,1},{33,49},{49,33},{2,18}... | collective-permute-start | bytes 1572872 | tf_op jit(solution)/shard_map/ppermute | solution.py:41
  23.3 27.3 %collective-permute-start.9 = (f32[2,2,2,256,128]{4,3,2,1,0:T(8,128)S(1)}, f32[2,2,2,256,128]{4,3,2,1,0:T(8,128)S(1)}, u32[]{:S(2)}, u32[]{:S(2)}) collective-permute-start(f32[2,2,2,256,128]{4,3,2,1,0:T(8,128)S(1)} %add.202), channel_id=1, source_target_pairs={{0,192},{64,128},{128,64},{192,0},{1,193},{65,129},{129,65},{193,1... | collective-permute-start | bytes 3145736 | tf_op jit(solution)/shard_map/ppermute | solution.py:41
  39.5 20.9 %collective-permute-start.6 = (f32[2,2,256,128]{3,2,1,0:T(8,128)S(1)}, f32[2,2,256,128]{3,2,1,0:T(8,128)S(1)}, u32[]{:S(2)}, u32[]{:S(2)}) collective-permute-start(f32[2,2,256,128]{3,2,1,0:T(8,128)S(1)} %fusion), channel_id=1, source_target_pairs={{0,192},{64,128},{128,64},{192,0},{1,193},{65,129},{129,65},{193,1... | collective-permute-start | bytes 1572872 | tf_op jit(solution)/shard_map/ppermute | solution.py:41
  50.7 11.4 %collective-permute-start.13 = (f32[2,2,256,128]{3,2,1,0:T(8,128)S(1)}, f32[2,2,256,128]{3,2,1,0:T(8,128)S(1)}, u32[]{:S(2)}, u32[]{:S(2)}) collective-permute-start(f32[2,2,256,128]{3,2,1,0:T(8,128)S(1)} %add_bitcast_fusion), channel_id=1, source_target_pairs={{0,64},{64,0},{128,192},{192,128},{1,65},{65,1},{129,193},{193,129... | collective-permute-start | bytes 1572872 | tf_op jit(solution)/shard_map/ppermute | solution.py:41
  50.9 11.8 %collective-permute-start.12 = (f32[2,2,128,128]{3,2,1,0:T(8,128)S(1)}, f32[2,2,128,128]{3,2,1,0:T(8,128)S(1)}, u32[]{:S(2)}, u32[]{:S(2)}) collective-permute-start(f32[2,2,128,128]{3,2,1,0:T(8,128)S(1)} %add_bitcast_fusion.2), channel_id=1, source_target_pairs={{0,48},{16,32},{32,16},{48,0},{1,49},{17,33},{33,17},{49,1},{2,50}... | collective-permute-start | bytes 786440 | tf_op jit(solution)/shard_map/ppermute | solution.py:41
  51.0 15.5 %collective-permute-start.11 = (f32[2,2,128,128]{3,2,1,0:T(8,128)S(1)}, f32[2,2,128,128]{3,2,1,0:T(8,128)S(1)}, u32[]{:S(2)}, u32[]{:S(2)}) collective-permute-start(f32[2,2,128,128]{3,2,1,0:T(8,128)S(1)} %add_bitcast_fusion.1), channel_id=1, source_target_pairs={{0,16},{16,0},{32,48},{48,32},{1,17},{17,1},{33,49},{49,33},{2,18}... | collective-permute-start | bytes 786440 | tf_op jit(solution)/shard_map/ppermute | solution.py:41
  60.5 13.5 %collective-permute-start.10 = (f32[2,256,128]{2,1,0:T(8,128)S(1)}, f32[2,256,128]{2,1,0:T(8,128)S(1)}, u32[]{:S(2)}, u32[]{:S(2)}) collective-permute-start(f32[2,256,128]{2,1,0:T(8,128)S(1)} %fusion.3), channel_id=1, source_target_pairs={{0,16},{16,0},{32,48},{48,32},{1,17},{17,1},{33,49},{49,33},{2,18}... | collective-permute-start | bytes 786440 | tf_op jit(solution)/shard_map/ppermute | solution.py:41
  62.1 19.3 %collective-permute-start.19 = (f32[2,256,128]{2,1,0:T(8,128)S(1)}, f32[2,256,128]{2,1,0:T(8,128)S(1)}, u32[]{:S(2)}, u32[]{:S(2)}) collective-permute-start(f32[2,256,128]{2,1,0:T(8,128)S(1)} %bitcast_add_fusion), channel_id=1, source_target_pairs={{0,48},{16,32},{32,16},{48,0},{1,49},{17,33},{33,17},{49,1},{2,50}... | collective-permute-start | bytes 786440 | tf_op jit(solution)/shard_map/ppermute | solution.py:41
  62.6 6.9 %collective-permute-start.15 = (f32[2,128,128]{2,1,0:T(8,128)S(1)}, f32[2,128,128]{2,1,0:T(8,128)S(1)}, u32[]{:S(2)}, u32[]{:S(2)}) collective-permute-start(f32[2,128,128]{2,1,0:T(8,128)S(1)} %bitcast_add_fusion.14), channel_id=1, source_target_pairs={{0,64},{64,0},{128,192},{192,128},{1,65},{65,1},{129,193},{193,129... | collective-permute-start | bytes 393224 | tf_op jit(solution)/shard_map/ppermute | solution.py:41
  66.6 6.3 %collective-permute-start.14 = (f32[2,128,128]{2,1,0:T(8,128)S(1)}, f32[2,128,128]{2,1,0:T(8,128)S(1)}, u32[]{:S(2)}, u32[]{:S(2)}) collective-permute-start(f32[2,128,128]{2,1,0:T(8,128)S(1)} %bitcast_add_fusion.12), channel_id=1, source_target_pairs={{0,192},{64,128},{128,64},{192,0},{1,193},{65,129},{129,65},{193,1... | collective-permute-start | bytes 393224 | tf_op jit(solution)/shard_map/ppermute | solution.py:41
  69.5 12.0 %collective-permute-start.18 = (f32[128,128]{1,0:T(8,128)S(1)}, f32[128,128]{1,0:T(8,128)S(1)}, u32[]{:S(2)}, u32[]{:S(2)}) collective-permute-start(f32[128,128]{1,0:T(8,128)S(1)} %bitcast_add_fusion.25), channel_id=1, source_target_pairs={{0,192},{64,128},{128,64},{192,0},{1,193},{65,129},{129,65},{193,1... | collective-permute-start | bytes 196616 | tf_op jit(solution)/shard_map/ppermute | solution.py:41
  72.9 8.7 %collective-permute-start.17 = (f32[128,128]{1,0:T(8,128)S(1)}, f32[128,128]{1,0:T(8,128)S(1)}, u32[]{:S(2)}, u32[]{:S(2)}) collective-permute-start(f32[128,128]{1,0:T(8,128)S(1)} %bitcast_add_fusion.23), channel_id=1, source_target_pairs={{0,64},{64,0},{128,192},{192,128},{1,65},{65,1},{129,193},{193,129... | collective-permute-start | bytes 196616 | tf_op jit(solution)/shard_map/ppermute | solution.py:41
  74.0 12.6 %collective-permute-start.16 = (f32[256,128]{1,0:T(8,128)S(1)}, f32[256,128]{1,0:T(8,128)S(1)}, u32[]{:S(2)}, u32[]{:S(2)}) collective-permute-start(f32[256,128]{1,0:T(8,128)S(1)} %fusion.5), channel_id=1, source_target_pairs={{0,48},{16,32},{32,16},{48,0},{1,49},{17,33},{33,17},{49,1},{2,50}... | collective-permute-start | bytes 393224 | tf_op jit(solution)/shard_map/ppermute | solution.py:41
  81.4 6.4 %collective-permute-start.20 = (f32[256,128]{1,0:T(8,128)S(1)}, f32[256,128]{1,0:T(8,128)S(1)}, u32[]{:S(2)}, u32[]{:S(2)}) collective-permute-start(f32[256,128]{1,0:T(8,128)S(1)} %bitcast_add_fusion.6), channel_id=1, source_target_pairs={{0,16},{16,0},{32,48},{48,32},{1,17},{17,1},{33,49},{49,33},{2,18}... | collective-permute-start | bytes 393224 | tf_op jit(solution)/shard_map/ppermute | solution.py:41
  86.7 31.6 %copy-start = (f32[16,6144]{1,0:T(8,128)S(1)}, f32[16,6144]{1,0:T(8,128)}, u32[]{:S(2)}) copy-start(f32[16,6144]{1,0:T(8,128)} %param.11) | copy-start | bytes 1179652
  86.7 31.6 %copy-start.1 = (f32[16,6144]{1,0:T(8,128)S(1)}, f32[16,6144]{1,0:T(8,128)}, u32[]{:S(2)}) copy-start(f32[16,6144]{1,0:T(8,128)} %param.12) | copy-start | bytes 1179652
  86.7 31.6 %copy-start.2 = (f32[16,6144]{1,0:T(8,128)S(1)}, f32[16,6144]{1,0:T(8,128)}, u32[]{:S(2)}) copy-start(f32[16,6144]{1,0:T(8,128)} %param.13) | copy-start | bytes 1179652
  88.6 14.4 %all-to-all-start = ((f32[32,1,128]{2,1,0:T(1,128)}), f32[32,1,128]{2,1,0:T(1,128)S(1)}, u32[]{:S(2)}, u32[]{:S(2)}) async-start(f32[32,1,128]{2,1,0:T(1,128)} %broadcast_in_dim.4), calls=%async_computation | async-start | bytes 32768 | tf_op jit(solution)/shard_map/all_to_all | solution.py:270

commit v3 on v2

--- a/solution.py
+++ b/solution.py
@@ -28,9 +28,9 @@
 FLAT = [sum(16 * rows for rows, _ in PAIRS[:n]) for n in range(len(PAIRS) + 1)]
 ORDER = (
     "sent:00", "sent:01", "sent:10", "sent:11", "rest",
-    "first:00", "start:00", "first:01", "start:01", "first:10", "start:10", "first:11", "start:11",
-    "kept", "keep:00", "keep:01", "keep:10", "keep:11",
-    "end:00", "start:00", "end:01", "start:01", "end:10", "start:10", "end:11", "start:11",
+    "first:00", "first:01", "first:10", "first:11", "start:00", "start:01", "start:10", "start:11",
+    "kept", "keep:00", "keep:01", "end:00", "end:01", "start:00", "start:01",
+    "keep:10", "keep:11", "end:10", "start:10", "end:11", "start:11",
     "end:00", "start:00", "end:01", "start:01", "end:10", "start:10", "end:11", "start:11",
     "end:10", "start:10", "end:11", "start:11", "end:00", "start:00", "end:01", "start:01",
     "end:10", "end:11", "end:00", "end:01",
@@ -99,63 +99,59 @@
     return store
 
 
-def load_numbers(ff_hbm, active_hbm, ff_ref, active_ref, sem):
-    copies = [
+def load_tiles(x_ref, x_buf, x_sem, subnet, s, core):
+    for i in range(4):
+        for t in range(4):
+            column = pl.multiple_of(place_of_tile(i, t, core) * LANES, LANES)
+            pltpu.make_async_copy(
+                x_ref.at[subnet, :, pl.ds(column, LANES)],
+                x_buf.at[i, s, :, pl.ds(t * LANES, LANES)],
+                x_sem.at[i],
+            ).start()
+
+
+def await_tiles(x_buf, x_sem, i):
+    pltpu.make_async_copy(x_buf.at[i], x_buf.at[i], x_sem.at[i]).wait()
+
+
+def sent_kernel(ff_hbm, active_hbm, x_ref, m_ref, *refs):
+    outs, refs = refs[:STREAMS], refs[STREAMS:]
+    x_other, x_own, mt_ref, ff_ref, active_ref, sem, x_sem, own_sem, m_buf, m_sem = refs
+    numbers = [
         pltpu.make_async_copy(ff_hbm, ff_ref, sem.at[0]),
         pltpu.make_async_copy(active_hbm, active_ref, sem.at[1]),
     ]
-    for c in copies:
+    all_m = pltpu.make_async_copy(m_ref, m_buf, m_sem)
+    for c in (*numbers, all_m):
         c.start()
-    for c in copies:
+    core = lax.axis_index("core")
+    load_tiles(x_ref, x_other, x_sem, 0, 0, 1 - core)
+    for c in numbers:
         c.wait()
     idle = sum(jnp.where(active_ref[i] == 1, 0, i) for i in range(1, 4))
-    return [s + (s >= idle).astype(jnp.int32) for s in range(LIVE)]
-
-
-def load_tiles(x_ref, x_buf, x_sem, live, core):
-    for i in range(4):
-        for t in range(4):
-            column = pl.multiple_of(place_of_tile(i, t, core) * LANES, LANES)
-            for s in range(LIVE):
-                pltpu.make_async_copy(
-                    x_ref.at[live[s], :, pl.ds(column, LANES)],
-                    x_buf.at[i, s, :, pl.ds(t * LANES, LANES)],
-                    x_sem.at[i],
-                ).start()
-
-    def ready(i):
-        pltpu.make_async_copy(x_buf.at[i], x_buf.at[i], x_sem.at[i]).wait()
-
-    return ready
-
-
-def sent_kernel(ff_hbm, active_hbm, x_ref, m_ref, *refs):
-    outs, refs = refs[:STREAMS], refs[STREAMS:]
-    x_buf, mt_ref, ff_ref, active_ref, sem, x_sem, m_buf, m_sem = refs
-    live = load_numbers(ff_hbm, active_hbm, ff_ref, active_ref, sem)
+    live = [s + (s >= idle).astype(jnp.int32) for s in range(LIVE)]
+    for s in range(1, LIVE):
+        load_tiles(x_ref, x_other, x_sem, live[s], s, 1 - core)
     for s in range(LIVE):
-        pltpu.make_async_copy(m_ref.at[live[s]], m_buf.at[s], m_sem).start()
-    ready = load_tiles(x_ref, x_buf, x_sem, live, 1 - lax.axis_index("core"))
-    pltpu.make_async_copy(m_buf, m_buf, m_sem).wait()
+        load_tiles(x_ref, x_own, own_sem, live[s], s, core)
+    all_m.wait()
     cols = m_buf.shape[2]
     first = lax.axis_index(MP) * cols
     for s in range(LIVE):
-        values = m_buf[s]
+        values = m_buf[live[s]]
         column = first + lax.broadcasted_iota(jnp.int32, values.shape, 1)
         keep = column < BLOCK * ff_ref[live[s]]
         values = jnp.where(keep, values, jnp.zeros_like(values))
         mt_ref[:, s * 256 : (s + 1) * 256] = values.T
-    multiply(mt_ref, x_buf, (into(outs), None), ready)
-
-
-def rest_kernel(ff_hbm, active_hbm, x_ref, mt_ref, other_x, *refs):
-    other_kept, refs = refs[0], refs[1:]
-    sent, kept = refs[:STREAMS], refs[STREAMS : 2 * STREAMS]
-    ff_ref, active_ref, sem, x_buf, x_sem = refs[2 * STREAMS :]
-    live = load_numbers(ff_hbm, active_hbm, ff_ref, active_ref, sem)
-    ready = load_tiles(x_ref, x_buf, x_sem, live, lax.axis_index("core"))
-    multiply(mt_ref, other_x, (None, into_flat(other_kept)))
-    multiply(mt_ref, x_buf, (into(sent), into(kept)), ready)
+    multiply(mt_ref, x_other, (into(outs), None), functools.partial(await_tiles, x_other, x_sem))
+    for i in range(4):
+        await_tiles(x_own, own_sem, i)
+
+
+def rest_kernel(mt_ref, x_other, x_own, other_kept, *refs):
+    sent, kept = refs[:STREAMS], refs[STREAMS:]
+    multiply(mt_ref, x_other, (None, into_flat(other_kept)))
+    multiply(mt_ref, x_own, (into(sent), into(kept)))
 
 
 def call(kernel, operands, spaces, out_shape, scratch, mebibytes):
@@ -163,43 +159,65 @@
         kernel,
         in_specs=[pl.BlockSpec(memory_space=space) for space in spaces],
         out_specs=[pl.BlockSpec(memory_space=pltpu.VMEM)] * len(out_shape),
-        scratch_shapes=[
-            pltpu.SMEM((4,), jnp.int32),
-            pltpu.SMEM((4,), jnp.int32),
-            pltpu.SemaphoreType.DMA((2,)),
-            *scratch,
-        ],
+        scratch_shapes=scratch,
         out_shape=out_shape,
         compiler_params=pltpu.CompilerParams(vmem_limit_bytes=mebibytes * 1024 * 1024),
     )(*(pltpu.with_memory_space_constraint(o, s) for o, s in zip(operands, spaces)))
 
 
 def products(ff_blocks, layer_active, x, m):
-    hbm, vmem = pltpu.HBM, pltpu.VMEM
+    hbm, vmem, sems = pltpu.HBM, pltpu.VMEM, pltpu.SemaphoreType.DMA
     pieces = [vmem((2, 2, 2, rows, LANES), jnp.float32) for rows, _ in PAIRS for _ in range(2)]
     tiles = vmem((4, LIVE, 256, 4 * LANES), jnp.bfloat16)
-    sems = pltpu.SemaphoreType.DMA((4,))
-    turned = vmem((m.shape[2], LIVE * 256), jnp.bfloat16)
-    *sent, other_x, turned = call(
+    *sent, x_other, x_own, turned = call(
         sent_kernel,
         (ff_blocks, layer_active, x, m),
         (hbm, hbm, hbm, hbm),
-        pieces + [tiles, turned],
-        [sems, vmem((LIVE, 256, m.shape[2]), jnp.bfloat16), pltpu.SemaphoreType.DMA],
+        pieces + [tiles, tiles, vmem((m.shape[2], LIVE * 256), jnp.bfloat16)],
+        [
+            pltpu.SMEM((4,), jnp.int32),
+            pltpu.SMEM((4,), jnp.int32),
+            sems((2,)),
+            sems((4,)),
+            sems((4,)),
+            vmem(m.shape, jnp.bfloat16),
+            sems,
+        ],
         6,
     )
 
     def rest(tie):
         return call(
             rest_kernel,
-            (ff_blocks, layer_active, x, tie(turned), other_x),
-            (hbm, hbm, hbm, vmem, vmem),
+            (tie(turned), x_other, x_own),
+            (vmem, vmem, vmem),
             [vmem((FLAT[-1], LANES), jnp.float32)] + pieces + pieces,
-            [tiles, sems],
-            8,
+            [],
+            6,
         )
 
     return sent, rest
+
+
+def sum_kernel(*refs):
+    for own, other, out in zip(refs[:STREAMS], refs[STREAMS : 2 * STREAMS], refs[2 * STREAMS :]):
+        def step(k, _):
+            at = k // 4, k // 2 % 2, k % 2
+            out[at] = own[at] + other[at]
+            return 0
+
+        lax.fori_loop(0, 8, step, 0)
+
+
+def sums(owns, others):
+    return pl.pallas_call(
+        sum_kernel,
+        in_specs=[pl.BlockSpec(memory_space=pltpu.VMEM)] * (2 * STREAMS),
+        out_specs=[pl.BlockSpec(memory_space=pltpu.VMEM)] * STREAMS,
+        out_shape=[pltpu.VMEM(o.shape, o.dtype) for o in owns],
+        input_output_aliases={n: n for n in range(STREAMS)},
+        compiler_params=pltpu.CompilerParams(vmem_limit_bytes=2 * 1024 * 1024),
+    )(*(pltpu.with_memory_space_constraint(o, pltpu.VMEM) for o in (*owns, *others)))
 
 
 class Stream:
@@ -215,9 +233,6 @@
     def tie(self, *values):
         *values, self.token = lax.optimization_barrier((*values, self.token))
         return values[0] if len(values) == 1 else values
-
-    def first(self, stream, own, other):
-        stream.send = self.token = self.tie(own + other)
 
     def keep(self, stream, own, other):
         stream.keep = self.token = self.tie(own + other)
@@ -240,7 +255,7 @@
 
 def shards(inputs, gate_cotangent, ff_blocks, layer_active, param, moment, second_moment):
     sent, rest = products(ff_blocks, layer_active, inputs, gate_cotangent)
-    flying, line = {}, Line(sent[0])
+    flying, firsts, line = {}, None, Line(sent[0])
     streams = {(n, half): Stream(pair[1][half]) for n, pair in enumerate(PAIRS) for half in range(2)}
     for act, *names in (event.split(":") for event in ORDER):
         if act == "rest":
@@ -256,7 +271,11 @@
             line.token = line.tie(sent[2 * n + half])
             flying[n, half] = swap(line.token, "core", 1)
         elif act == "first":
-            line.first(streams[n, half], owns[2 * n + half], line.tie(flying[n, half]))
+            if not firsts:
+                others = [line.tie(f) for f in flying.values()]
+                firsts = sums(owns[:STREAMS], others)
+                line.token = firsts[0]
+            streams[n, half].send = firsts[2 * n + half]
         elif act == "keep":
             own = owns[STREAMS + 2 * n + half]
             first = FLAT[n] + half * own.size // LANES

time: 120 us -> 117 us (0.975)
  starting transfers between devices: 40.7 us -> 45.6 us
  waiting for transfers between devices: 47.3 us -> 43.1 us
  Pallas kernels: 11.6 us -> 9.75 us
  blocking collectives: 13.8 us -> 12.5 us
    ppermute x21, waiting for transfers between devices: 37.8 us -> 33.6 us  [swap(): lax.ppermute(value, axis, [(i, i ^ mask) for i in range(SIZES[axis])])]
    ppermute x21, starting transfers between devices: 36.1 us -> 39 us  [swap(): lax.ppermute(value, axis, [(i, i ^ mask) for i in range(SIZES[axis])])]
    pallas_call x2, Pallas kernels: 11.6 us -> 8.92 us  [call(): pl.pallas_call(kernel, in_specs=[pl.BlockSpec(memory_space=space) for spa...]
    all_to_all x1, starting transfers between devices: 4.66 us -> 6.55 us  [shards(): lax.all_to_all(jnp.broadcast_to(squares[None], (devices, 1, LANES)), DP,...]
    all_to_all x1, blocking collectives: 13.8 us -> 12.5 us  [shards(): lax.all_to_all(jnp.concatenate([blocks, beside], axis=2), MP, 0, 0, tiled...]
  transfers between devices with their start and end apart: 22 -> 22, of which waited for: 9 -> 11; matrix products, arithmetic and copies ran while one was open for 1% -> 1% of each run, Pallas kernels for 5% -> 3%
where the time goes in v3:
time: 117 us; the launch traced here: 116 us
  starting transfers between devices  45.6 us (39%)
  waiting for transfers between devices  43.1 us (37%)
  blocking collectives  12.5 us (11%)
  Pallas kernels  9.75 us (8%)
  other arithmetic  2.94 us (3%)
  between operations  1.62 us (1%)
    ppermute x21, starting transfers between devices, swap(): lax.ppermute(value, axis, [(i, i ^ mask) for i in range(SIZES[axis])])  39 us
    ppermute x21, waiting for transfers between devices, swap(): lax.ppermute(value, axis, [(i, i ^ mask) for i in range(SIZES[axis])])  33.6 us
    all_to_all x1, blocking collectives, shards(): lax.all_to_all(jnp.concatenate([blocks, beside], axis=2), MP, 0, 0, tiled...  12.5 us
    all_to_all x1, waiting for transfers between devices, shards(): lax.all_to_all(jnp.broadcast_to(squares[None], (devices, 1, LANES)), DP,...  9.48 us
    pallas_call x2, Pallas kernels, call(): pl.pallas_call(kernel, in_specs=[pl.BlockSpec(memory_space=space) for spa...  8.92 us
    all_to_all x1, starting transfers between devices, shards(): lax.all_to_all(jnp.broadcast_to(squares[None], (devices, 1, LANES)), DP,...  6.55 us
  transfers between devices with their start and end apart: 22, of which 11 were waited for; matrix products, arithmetic and copies ran while one was open for 1% of the time, Pallas kernels for 3%

profile of v3, /device:TPU:2, one launch (start us, length us, event | category | flops | bytes accessed | tf_op | source)
XLA Modules:
  0.0 116.5 jit_solution(18195437679897656861)
XLA Ops:
  0.6 5.1 %shard_map.94 = (f32[2,2,2,256,128]{4,3,2,1,0:T(8,128)S(1)}, f32[2,2,2,256,128]{4,3,2,1,0:T(8,128)S(1)}, f32[2,2,2,128,128]{4,3,2,1,0:T(8,128)S(1)}, f32[2,2,2,1...) custom-call(s32[4]{0:T(128)} %ff_hbm.1, ...), custom_call_target="tpu_custom_call" | custom-call | tf_op jit(solution)/shard_map/pallas_call | solution.py:158
  5.7 0.1 collective-permute-start
  5.8 0.5 collective-permute-start.1
  6.3 0.1 collective-permute-start.3
  6.4 0.4 collective-permute-start.2
  6.8 3.8 %shard_map.95 = (f32[6144,128]{1,0:T(8,128)S(1)}, f32[2,2,2,256,128]{4,3,2,1,0:T(8,128)S(1)}, f32[2,2,2,256,128]{4,3,2,1,0:T(8,128)S(1)}, f32[2,2,2,128,128]{4,3...) custom-call(bf16[768,768]{1,0:T(8,128)(2,1)S(1)} %get-tuple-element., ...), custom_call_target="tpu_custom_call" | custom-call | tf_op jit(solution)/shard_map/pallas_call | solution.py:158
  10.7 0.1 collective-permute-done.3.refs_7_
  10.7 0.7 collective-permute-done.2.refs_6_
  11.5 0.0 collective-permute-done.refs_4_
  11.5 0.0 collective-permute-done.1.refs_5_
  11.5 0.8 shard_map.96
  12.3 0.2 collective-permute-start.5
  12.5 1.6 %collective-permute-start.4 = (f32[2,2,2,256,128]{4,3,2,1,0:T(8,128)S(1)}, f32[2,2,2,256,128]{4,3,2,1,0:T(8,128)S(1)}, u32[]{:S(2)}, u32[]{:S(2)}) collective-permute-start(f32[2,2,2,256,128]{4,3,2,1,0:T(8,128)S(1)} %get-tuple-element.70), channel_id=1, source_target_pairs={{0,64},{64,0},{128,192},{192,128},{1,65},{65,1},{129,193},{193,129... | collective-permute-start | bytes 3145736 | tf_op jit(solution)/shard_map/ppermute | solution.py:41
  14.1 2.2 %collective-permute-start.6 = (f32[2,2,2,256,128]{4,3,2,1,0:T(8,128)S(1)}, f32[2,2,2,256,128]{4,3,2,1,0:T(8,128)S(1)}, u32[]{:S(2)}, u32[]{:S(2)}) collective-permute-start(f32[2,2,2,256,128]{4,3,2,1,0:T(8,128)S(1)} %get-tuple-element.76), channel_id=1, source_target_pairs={{0,192},{64,128},{128,64},{192,0},{1,193},{65,129},{129,65},{193,1... | collective-permute-start | bytes 3145736 | tf_op jit(solution)/shard_map/ppermute | solution.py:41
  16.3 6.3 %collective-permute-start.8 = (f32[2,2,2,128,128]{4,3,2,1,0:T(8,128)S(1)}, f32[2,2,2,128,128]{4,3,2,1,0:T(8,128)S(1)}, u32[]{:S(2)}, u32[]{:S(2)}) collective-permute-start(f32[2,2,2,128,128]{4,3,2,1,0:T(8,128)S(1)} %get-tuple-element.78), channel_id=1, source_target_pairs={{0,48},{16,32},{32,16},{48,0},{1,49},{17,33},{33,17},{49,1},{2,50}... | collective-permute-start | bytes 1572872 | tf_op jit(solution)/shard_map/ppermute | solution.py:41
  22.6 1.5 %collective-permute-start.9 = (f32[2,2,2,128,128]{4,3,2,1,0:T(8,128)S(1)}, f32[2,2,2,128,128]{4,3,2,1,0:T(8,128)S(1)}, u32[]{:S(2)}, u32[]{:S(2)}) collective-permute-start(f32[2,2,2,128,128]{4,3,2,1,0:T(8,128)S(1)} %get-tuple-element.77), channel_id=1, source_target_pairs={{0,16},{16,0},{32,48},{48,32},{1,17},{17,1},{33,49},{49,33},{2,18}... | collective-permute-start | bytes 1572872 | tf_op jit(solution)/shard_map/ppermute | solution.py:41
  24.1 0.0 collective-permute-done.5
  24.1 0.1 fusion.11
  24.2 0.1 add.190
  24.3 0.1 add.189
  24.5 13.5 %collective-permute-done.4 = f32[2,2,2,256,128]{4,3,2,1,0:T(8,128)S(1)} collective-permute-done((f32[2,2,2,256,128]{4,3,2,1,0:T(8,128)S(1)}, f32[2,2,2,256,128]{4,3,2,1,0:T(8,128)S(1)}, u32[]{:S(2)}, u32[]{:S(2)}) %collective-permute-start.4) | collective-permute-done | bytes 1048608 | tf_op jit(solution)/shard_map/ppermute | solution.py:41
  38.0 0.1 fusion
  38.0 2.5 %collective-permute-done.6 = f32[2,2,2,256,128]{4,3,2,1,0:T(8,128)S(1)} collective-permute-done((f32[2,2,2,256,128]{4,3,2,1,0:T(8,128)S(1)}, f32[2,2,2,256,128]{4,3,2,1,0:T(8,128)S(1)}, u32[]{:S(2)}, u32[]{:S(2)}) %collective-permute-start.6) | collective-permute-done | bytes 1048608 | tf_op jit(solution)/shard_map/ppermute | solution.py:41
  40.5 0.1 add_bitcast_fusion
  40.6 2.3 %collective-permute-start.7 = (f32[2,2,256,128]{3,2,1,0:T(8,128)S(1)}, f32[2,2,256,128]{3,2,1,0:T(8,128)S(1)}, u32[]{:S(2)}, u32[]{:S(2)}) collective-permute-start(f32[2,2,256,128]{3,2,1,0:T(8,128)S(1)} %fusion), channel_id=1, source_target_pairs={{0,192},{64,128},{128,64},{192,0},{1,193},{65,129},{129,65},{193,1... | collective-permute-start | bytes 1572872 | tf_op jit(solution)/shard_map/ppermute | solution.py:41
  42.8 0.1 fusion.12
  42.9 0.1 collective-permute-start.13
  43.0 0.1 add.196
  43.1 0.1 add.195
  43.2 5.0 %collective-permute-done.9 = f32[2,2,2,128,128]{4,3,2,1,0:T(8,128)S(1)} collective-permute-done((f32[2,2,2,128,128]{4,3,2,1,0:T(8,128)S(1)}, f32[2,2,2,128,128]{4,3,2,1,0:T(8,128)S(1)}, u32[]{:S(2)}, u32[]{:S(2)}) %collective-permute-start.9) | collective-permute-done | bytes 524320 | tf_op jit(solution)/shard_map/ppermute | solution.py:41
  48.2 1.4 %collective-permute-start.12 = (f32[2,2,128,128]{3,2,1,0:T(8,128)S(1)}, f32[2,2,128,128]{3,2,1,0:T(8,128)S(1)}, u32[]{:S(2)}, u32[]{:S(2)}) collective-permute-start(f32[2,2,128,128]{3,2,1,0:T(8,128)S(1)} %add_bitcast_fusion.2), channel_id=1, source_target_pairs={{0,48},{16,32},{32,16},{48,0},{1,49},{17,33},{33,17},{49,1},{2,50}... | collective-permute-start | bytes 786440 | tf_op jit(solution)/shard_map/ppermute | solution.py:41
  49.6 0.0 collective-permute-done.8
  49.6 1.5 %collective-permute-start.11 = (f32[2,2,128,128]{3,2,1,0:T(8,128)S(1)}, f32[2,2,128,128]{3,2,1,0:T(8,128)S(1)}, u32[]{:S(2)}, u32[]{:S(2)}) collective-permute-start(f32[2,2,128,128]{3,2,1,0:T(8,128)S(1)} %add_bitcast_fusion.1), channel_id=1, source_target_pairs={{0,16},{16,0},{32,48},{48,32},{1,17},{17,1},{33,49},{49,33},{2,18}... | collective-permute-start | bytes 786440 | tf_op jit(solution)/shard_map/ppermute | solution.py:41
  51.2 3.8 %collective-permute-done.7 = f32[2,2,256,128]{3,2,1,0:T(8,128)S(1)} collective-permute-done((f32[2,2,256,128]{3,2,1,0:T(8,128)S(1)}, f32[2,2,256,128]{3,2,1,0:T(8,128)S(1)}, u32[]{:S(2)}, u32[]{:S(2)}) %collective-permute-start.7) | collective-permute-done | bytes 524320 | tf_op jit(solution)/shard_map/ppermute | solution.py:41
  55.0 3.5 %collective-permute-start.10 = (f32[2,256,128]{2,1,0:T(8,128)S(1)}, f32[2,256,128]{2,1,0:T(8,128)S(1)}, u32[]{:S(2)}, u32[]{:S(2)}) collective-permute-start(f32[2,256,128]{2,1,0:T(8,128)S(1)} %fusion.3), channel_id=1, source_target_pairs={{0,16},{16,0},{32,48},{48,32},{1,17},{17,1},{33,49},{49,33},{2,18}... | collective-permute-start | bytes 786440 | tf_op jit(solution)/shard_map/ppermute | solution.py:41
  58.5 0.0 collective-permute-done.13
  58.5 0.1 bitcast_add_fusion
  58.6 4.6 %collective-permute-start.19 = (f32[2,256,128]{2,1,0:T(8,128)S(1)}, f32[2,256,128]{2,1,0:T(8,128)S(1)}, u32[]{:S(2)}, u32[]{:S(2)}) collective-permute-start(f32[2,256,128]{2,1,0:T(8,128)S(1)} %bitcast_add_fusion), channel_id=1, source_target_pairs={{0,48},{16,32},{32,16},{48,0},{1,49},{17,33},{33,17},{49,1},{2,50}... | collective-permute-start | bytes 786440 | tf_op jit(solution)/shard_map/ppermute | solution.py:41
  63.1 0.0 collective-permute-done.12
  63.2 0.1 collective-permute-start.15
  63.3 0.4 collective-permute-done.11
  63.7 1.9 %collective-permute-start.14 = (f32[2,128,128]{2,1,0:T(8,128)S(1)}, f32[2,128,128]{2,1,0:T(8,128)S(1)}, u32[]{:S(2)}, u32[]{:S(2)}) collective-permute-start(f32[2,128,128]{2,1,0:T(8,128)S(1)} %bitcast_add_fusion.12), channel_id=1, source_target_pairs={{0,192},{64,128},{128,64},{192,0},{1,193},{65,129},{129,65},{193,1... | collective-permute-start | bytes 393224 | tf_op jit(solution)/shard_map/ppermute | solution.py:41
  65.6 2.6 %collective-permute-done.15 = f32[2,128,128]{2,1,0:T(8,128)S(1)} collective-permute-done((f32[2,128,128]{2,1,0:T(8,128)S(1)}, f32[2,128,128]{2,1,0:T(8,128)S(1)}, u32[]{:S(2)}, u32[]{:S(2)}) %collective-permute-start.15) | collective-permute-done | bytes 131104 | tf_op jit(solution)/shard_map/ppermute | solution.py:41
  68.3 2.3 %collective-permute-start.18 = (f32[128,128]{1,0:T(8,128)S(1)}, f32[128,128]{1,0:T(8,128)S(1)}, u32[]{:S(2)}, u32[]{:S(2)}) collective-permute-start(f32[128,128]{1,0:T(8,128)S(1)} %bitcast_add_fusion.25), channel_id=1, source_target_pairs={{0,192},{64,128},{128,64},{192,0},{1,193},{65,129},{129,65},{193,1... | collective-permute-start | bytes 196616 | tf_op jit(solution)/shard_map/ppermute | solution.py:41
  70.5 0.1 collective-permute-done.14
  70.7 4.9 %collective-permute-start.17 = (f32[128,128]{1,0:T(8,128)S(1)}, f32[128,128]{1,0:T(8,128)S(1)}, u32[]{:S(2)}, u32[]{:S(2)}) collective-permute-start(f32[128,128]{1,0:T(8,128)S(1)} %bitcast_add_fusion.23), channel_id=1, source_target_pairs={{0,64},{64,0},{128,192},{192,128},{1,65},{65,1},{129,193},{193,129... | collective-permute-start | bytes 196616 | tf_op jit(solution)/shard_map/ppermute | solution.py:41
  75.6 0.0 collective-permute-done.10
  75.6 0.8 collective-permute-start.16
  76.4 0.0 collective-permute-done.19
  76.4 2.8 %collective-permute-start.20 = (f32[256,128]{1,0:T(8,128)S(1)}, f32[256,128]{1,0:T(8,128)S(1)}, u32[]{:S(2)}, u32[]{:S(2)}) collective-permute-start(f32[256,128]{1,0:T(8,128)S(1)} %bitcast_add_fusion.6), channel_id=1, source_target_pairs={{0,16},{16,0},{32,48},{48,32},{1,17},{17,1},{33,49},{49,33},{2,18}... | collective-permute-start | bytes 393224 | tf_op jit(solution)/shard_map/ppermute | solution.py:41
  79.2 0.0 collective-permute-done.18
  79.2 0.0 collective-permute-done.17
  79.3 4.9 %collective-permute-done.16 = f32[256,128]{1,0:T(8,128)S(1)} collective-permute-done((f32[256,128]{1,0:T(8,128)S(1)}, f32[256,128]{1,0:T(8,128)S(1)}, u32[]{:S(2)}, u32[]{:S(2)}) %collective-permute-start.16) | collective-permute-done | bytes 131104 | tf_op jit(solution)/shard_map/ppermute | solution.py:41
  84.3 0.0 copy-start
  84.3 0.0 copy-start.1
  84.3 0.0 copy-start.2
  84.3 0.0 collective-permute-done.20
  84.4 0.6 broadcast_in_dim.4
  85.1 6.5 %all-to-all-start = ((f32[32,1,128]{2,1,0:T(1,128)}), f32[32,1,128]{2,1,0:T(1,128)S(1)}, u32[]{:S(2)}, u32[]{:S(2)}) async-start(f32[32,1,128]{2,1,0:T(1,128)} %broadcast_in_dim.4), calls=%async_computation | async-start | bytes 32768 | tf_op jit(solution)/shard_map/all_to_all | solution.py:289
  91.7 0.2 copy.20
  91.8 9.5 %all-to-all-done = f32[32,1,128]{2,1,0:T(1,128)S(1)} async-done(((f32[32,1,128]{2,1,0:T(1,128)}), f32[32,1,128]{2,1,0:T(1,128)S(1)}, u32[]{:S(2)}, u32[]{:S(2)}) %all-to-all-start) | async-done | bytes 16416 | tf_op jit(solution)/shard_map/all_to_all | solution.py:289
  101.4 12.5 %all_to_all.10 = f32[8,16,896]{2,1,0:T(8,128)S(1)} all-to-all(f32[8,16,896]{2,1,0:T(8,128)S(1)} %pad_maximum_fusion), channel_id=1, replica_groups=mesh['y'=4,'z'=4,'core'=2,'z_lo'=2,'x'=4] {'z_lo','x'}, dimensions={0} | all-to-all | bytes 917504 | tf_op jit(solution)/shard_map/all_to_all | solution.py:293
  113.9 0.6 slice_reduce_fusion
  115.3 1.2 %multiply_subtract_fusion = (f32[16,6144]{1,0:T(8,128)}, f32[16,6144]{1,0:T(8,128)}, f32[16,6144]{1,0:T(8,128)}) fusion(f32[16,6144]{1,0:T(8,128)S(1)} %copy-done, f32[16,6144]{1,0:T(8,128)S(1)} %bitcast.167, f32[16,6144]{1,0:T(8,128)S(1)} %copy-done.1, f32[16,6144]{1,0:T(8,128)S(1)} %copy-done.2), kind=kLoop, calls=%fused_computation.9 | loop fusion | flops 1474560 | bytes 2752512 | tf_op jit(solution)/shard_map/sub | solution.py:302
  (25 shorter events, 0.6 us)
Async XLA Ops:
  5.7 5.8 %collective-permute-start = (f32[2,2,2,256,128]{4,3,2,1,0:T(8,128)S(1)}, f32[2,2,2,256,128]{4,3,2,1,0:T(8,128)S(1)}, u32[]{:S(2)}, u32[]{:S(2)}) collective-permute-start(f32[2,2,2,256,128]{4,3,2,1,0:T(8,128)S(1)} %get-tuple-element.58), channel_id=1, source_target_pairs={{0,8},{8,0},{1,9},{9,1},{2,10},{10,2},{3,11},{11,3},{4,12},{12,4},... | collective-permute-start | bytes 3145736 | tf_op jit(solution)/shard_map/ppermute | solution.py:41
  5.8 5.7 %collective-permute-start.1 = (f32[2,2,2,256,128]{4,3,2,1,0:T(8,128)S(1)}, f32[2,2,2,256,128]{4,3,2,1,0:T(8,128)S(1)}, u32[]{:S(2)}, u32[]{:S(2)}) collective-permute-start(f32[2,2,2,256,128]{4,3,2,1,0:T(8,128)S(1)} %get-tuple-element.59), channel_id=1, source_target_pairs={{0,8},{8,0},{1,9},{9,1},{2,10},{10,2},{3,11},{11,3},{4,12},{12,4},... | collective-permute-start | bytes 3145736 | tf_op jit(solution)/shard_map/ppermute | solution.py:41
  6.3 4.4 %collective-permute-start.3 = (f32[2,2,2,128,128]{4,3,2,1,0:T(8,128)S(1)}, f32[2,2,2,128,128]{4,3,2,1,0:T(8,128)S(1)}, u32[]{:S(2)}, u32[]{:S(2)}) collective-permute-start(f32[2,2,2,128,128]{4,3,2,1,0:T(8,128)S(1)} %get-tuple-element.61), channel_id=1, source_target_pairs={{0,8},{8,0},{1,9},{9,1},{2,10},{10,2},{3,11},{11,3},{4,12},{12,4},... | collective-permute-start | bytes 1572872 | tf_op jit(solution)/shard_map/ppermute | solution.py:41
  6.4 5.0 %collective-permute-start.2 = (f32[2,2,2,128,128]{4,3,2,1,0:T(8,128)S(1)}, f32[2,2,2,128,128]{4,3,2,1,0:T(8,128)S(1)}, u32[]{:S(2)}, u32[]{:S(2)}) collective-permute-start(f32[2,2,2,128,128]{4,3,2,1,0:T(8,128)S(1)} %get-tuple-element.60), channel_id=1, source_target_pairs={{0,8},{8,0},{1,9},{9,1},{2,10},{10,2},{3,11},{11,3},{4,12},{12,4},... | collective-permute-start | bytes 1572872 | tf_op jit(solution)/shard_map/ppermute | solution.py:41
  12.3 11.8 %collective-permute-start.5 = (f32[6144,128]{1,0:T(8,128)S(1)}, f32[6144,128]{1,0:T(8,128)S(1)}, u32[]{:S(2)}, u32[]{:S(2)}) collective-permute-start(f32[6144,128]{1,0:T(8,128)S(1)} %get-tuple-element.79), channel_id=1, source_target_pairs={{0,8},{8,0},{1,9},{9,1},{2,10},{10,2},{3,11},{11,3},{4,12},{12,4},... | collective-permute-start | bytes 9437192 | tf_op jit(solution)/shard_map/ppermute | solution.py:41
  12.5 25.4 %collective-permute-start.4 = (f32[2,2,2,256,128]{4,3,2,1,0:T(8,128)S(1)}, f32[2,2,2,256,128]{4,3,2,1,0:T(8,128)S(1)}, u32[]{:S(2)}, u32[]{:S(2)}) collective-permute-start(f32[2,2,2,256,128]{4,3,2,1,0:T(8,128)S(1)} %get-tuple-element.70), channel_id=1, source_target_pairs={{0,64},{64,0},{128,192},{192,128},{1,65},{65,1},{129,193},{193,129... | collective-permute-start | bytes 3145736 | tf_op jit(solution)/shard_map/ppermute | solution.py:41
  14.1 26.4 %collective-permute-start.6 = (f32[2,2,2,256,128]{4,3,2,1,0:T(8,128)S(1)}, f32[2,2,2,256,128]{4,3,2,1,0:T(8,128)S(1)}, u32[]{:S(2)}, u32[]{:S(2)}) collective-permute-start(f32[2,2,2,256,128]{4,3,2,1,0:T(8,128)S(1)} %get-tuple-element.76), channel_id=1, source_target_pairs={{0,192},{64,128},{128,64},{192,0},{1,193},{65,129},{129,65},{193,1... | collective-permute-start | bytes 3145736 | tf_op jit(solution)/shard_map/ppermute | solution.py:41
  16.3 33.3 %collective-permute-start.8 = (f32[2,2,2,128,128]{4,3,2,1,0:T(8,128)S(1)}, f32[2,2,2,128,128]{4,3,2,1,0:T(8,128)S(1)}, u32[]{:S(2)}, u32[]{:S(2)}) collective-permute-start(f32[2,2,2,128,128]{4,3,2,1,0:T(8,128)S(1)} %get-tuple-element.78), channel_id=1, source_target_pairs={{0,48},{16,32},{32,16},{48,0},{1,49},{17,33},{33,17},{49,1},{2,50}... | collective-permute-start | bytes 1572872 | tf_op jit(solution)/shard_map/ppermute | solution.py:41
  22.6 25.5 %collective-permute-start.9 = (f32[2,2,2,128,128]{4,3,2,1,0:T(8,128)S(1)}, f32[2,2,2,128,128]{4,3,2,1,0:T(8,128)S(1)}, u32[]{:S(2)}, u32[]{:S(2)}) collective-permute-start(f32[2,2,2,128,128]{4,3,2,1,0:T(8,128)S(1)} %get-tuple-element.77), channel_id=1, source_target_pairs={{0,16},{16,0},{32,48},{48,32},{1,17},{17,1},{33,49},{49,33},{2,18}... | collective-permute-start | bytes 1572872 | tf_op jit(solution)/shard_map/ppermute | solution.py:41
  40.6 14.4 %collective-permute-start.7 = (f32[2,2,256,128]{3,2,1,0:T(8,128)S(1)}, f32[2,2,256,128]{3,2,1,0:T(8,128)S(1)}, u32[]{:S(2)}, u32[]{:S(2)}) collective-permute-start(f32[2,2,256,128]{3,2,1,0:T(8,128)S(1)} %fusion), channel_id=1, source_target_pairs={{0,192},{64,128},{128,64},{192,0},{1,193},{65,129},{129,65},{193,1... | collective-permute-start | bytes 1572872 | tf_op jit(solution)/shard_map/ppermute | solution.py:41
  42.9 15.6 %collective-permute-start.13 = (f32[2,2,256,128]{3,2,1,0:T(8,128)S(1)}, f32[2,2,256,128]{3,2,1,0:T(8,128)S(1)}, u32[]{:S(2)}, u32[]{:S(2)}) collective-permute-start(f32[2,2,256,128]{3,2,1,0:T(8,128)S(1)} %add_bitcast_fusion), channel_id=1, source_target_pairs={{0,64},{64,0},{128,192},{192,128},{1,65},{65,1},{129,193},{193,129... | collective-permute-start | bytes 1572872 | tf_op jit(solution)/shard_map/ppermute | solution.py:41
  48.2 15.0 %collective-permute-start.12 = (f32[2,2,128,128]{3,2,1,0:T(8,128)S(1)}, f32[2,2,128,128]{3,2,1,0:T(8,128)S(1)}, u32[]{:S(2)}, u32[]{:S(2)}) collective-permute-start(f32[2,2,128,128]{3,2,1,0:T(8,128)S(1)} %add_bitcast_fusion.2), channel_id=1, source_target_pairs={{0,48},{16,32},{32,16},{48,0},{1,49},{17,33},{33,17},{49,1},{2,50}... | collective-permute-start | bytes 786440 | tf_op jit(solution)/shard_map/ppermute | solution.py:41
  49.6 14.0 %collective-permute-start.11 = (f32[2,2,128,128]{3,2,1,0:T(8,128)S(1)}, f32[2,2,128,128]{3,2,1,0:T(8,128)S(1)}, u32[]{:S(2)}, u32[]{:S(2)}) collective-permute-start(f32[2,2,128,128]{3,2,1,0:T(8,128)S(1)} %add_bitcast_fusion.1), channel_id=1, source_target_pairs={{0,16},{16,0},{32,48},{48,32},{1,17},{17,1},{33,49},{49,33},{2,18}... | collective-permute-start | bytes 786440 | tf_op jit(solution)/shard_map/ppermute | solution.py:41
  55.0 20.6 %collective-permute-start.10 = (f32[2,256,128]{2,1,0:T(8,128)S(1)}, f32[2,256,128]{2,1,0:T(8,128)S(1)}, u32[]{:S(2)}, u32[]{:S(2)}) collective-permute-start(f32[2,256,128]{2,1,0:T(8,128)S(1)} %fusion.3), channel_id=1, source_target_pairs={{0,16},{16,0},{32,48},{48,32},{1,17},{17,1},{33,49},{49,33},{2,18}... | collective-permute-start | bytes 786440 | tf_op jit(solution)/shard_map/ppermute | solution.py:41
  58.6 17.8 %collective-permute-start.19 = (f32[2,256,128]{2,1,0:T(8,128)S(1)}, f32[2,256,128]{2,1,0:T(8,128)S(1)}, u32[]{:S(2)}, u32[]{:S(2)}) collective-permute-start(f32[2,256,128]{2,1,0:T(8,128)S(1)} %bitcast_add_fusion), channel_id=1, source_target_pairs={{0,48},{16,32},{32,16},{48,0},{1,49},{17,33},{33,17},{49,1},{2,50}... | collective-permute-start | bytes 786440 | tf_op jit(solution)/shard_map/ppermute | solution.py:41
  63.2 5.1 %collective-permute-start.15 = (f32[2,128,128]{2,1,0:T(8,128)S(1)}, f32[2,128,128]{2,1,0:T(8,128)S(1)}, u32[]{:S(2)}, u32[]{:S(2)}) collective-permute-start(f32[2,128,128]{2,1,0:T(8,128)S(1)} %bitcast_add_fusion.14), channel_id=1, source_target_pairs={{0,64},{64,0},{128,192},{192,128},{1,65},{65,1},{129,193},{193,129... | collective-permute-start | bytes 393224 | tf_op jit(solution)/shard_map/ppermute | solution.py:41
  63.7 7.0 %collective-permute-start.14 = (f32[2,128,128]{2,1,0:T(8,128)S(1)}, f32[2,128,128]{2,1,0:T(8,128)S(1)}, u32[]{:S(2)}, u32[]{:S(2)}) collective-permute-start(f32[2,128,128]{2,1,0:T(8,128)S(1)} %bitcast_add_fusion.12), channel_id=1, source_target_pairs={{0,192},{64,128},{128,64},{192,0},{1,193},{65,129},{129,65},{193,1... | collective-permute-start | bytes 393224 | tf_op jit(solution)/shard_map/ppermute | solution.py:41
  68.3 11.0 %collective-permute-start.18 = (f32[128,128]{1,0:T(8,128)S(1)}, f32[128,128]{1,0:T(8,128)S(1)}, u32[]{:S(2)}, u32[]{:S(2)}) collective-permute-start(f32[128,128]{1,0:T(8,128)S(1)} %bitcast_add_fusion.25), channel_id=1, source_target_pairs={{0,192},{64,128},{128,64},{192,0},{1,193},{65,129},{129,65},{193,1... | collective-permute-start | bytes 196616 | tf_op jit(solution)/shard_map/ppermute | solution.py:41
  70.7 8.6 %collective-permute-start.17 = (f32[128,128]{1,0:T(8,128)S(1)}, f32[128,128]{1,0:T(8,128)S(1)}, u32[]{:S(2)}, u32[]{:S(2)}) collective-permute-start(f32[128,128]{1,0:T(8,128)S(1)} %bitcast_add_fusion.23), channel_id=1, source_target_pairs={{0,64},{64,0},{128,192},{192,128},{1,65},{65,1},{129,193},{193,129... | collective-permute-start | bytes 196616 | tf_op jit(solution)/shard_map/ppermute | solution.py:41
  75.6 8.6 %collective-permute-start.16 = (f32[256,128]{1,0:T(8,128)S(1)}, f32[256,128]{1,0:T(8,128)S(1)}, u32[]{:S(2)}, u32[]{:S(2)}) collective-permute-start(f32[256,128]{1,0:T(8,128)S(1)} %fusion.5), channel_id=1, source_target_pairs={{0,48},{16,32},{32,16},{48,0},{1,49},{17,33},{33,17},{49,1},{2,50}... | collective-permute-start | bytes 393224 | tf_op jit(solution)/shard_map/ppermute | solution.py:41
  76.4 7.9 %collective-permute-start.20 = (f32[256,128]{1,0:T(8,128)S(1)}, f32[256,128]{1,0:T(8,128)S(1)}, u32[]{:S(2)}, u32[]{:S(2)}) collective-permute-start(f32[256,128]{1,0:T(8,128)S(1)} %bitcast_add_fusion.6), channel_id=1, source_target_pairs={{0,16},{16,0},{32,48},{48,32},{1,17},{17,1},{33,49},{49,33},{2,18}... | collective-permute-start | bytes 393224 | tf_op jit(solution)/shard_map/ppermute | solution.py:41
  84.3 31.0 %copy-start = (f32[16,6144]{1,0:T(8,128)S(1)}, f32[16,6144]{1,0:T(8,128)}, u32[]{:S(2)}) copy-start(f32[16,6144]{1,0:T(8,128)} %param.11) | copy-start | bytes 1179652
  84.3 31.0 %copy-start.1 = (f32[16,6144]{1,0:T(8,128)S(1)}, f32[16,6144]{1,0:T(8,128)}, u32[]{:S(2)}) copy-start(f32[16,6144]{1,0:T(8,128)} %param.12) | copy-start | bytes 1179652
  84.3 31.0 %copy-start.2 = (f32[16,6144]{1,0:T(8,128)S(1)}, f32[16,6144]{1,0:T(8,128)}, u32[]{:S(2)}) copy-start(f32[16,6144]{1,0:T(8,128)} %param.13) | copy-start | bytes 1179652
  85.1 16.2 %all-to-all-start = ((f32[32,1,128]{2,1,0:T(1,128)}), f32[32,1,128]{2,1,0:T(1,128)S(1)}, u32[]{:S(2)}, u32[]{:S(2)}) async-start(f32[32,1,128]{2,1,0:T(1,128)} %broadcast_in_dim.4), calls=%async_computation | async-start | bytes 32768 | tf_op jit(solution)/shard_map/all_to_all | solution.py:289

commit v4 on v3

--- a/solution.py
+++ b/solution.py
@@ -27,7 +27,7 @@
 STREAMS = 2 * len(PAIRS)
 FLAT = [sum(16 * rows for rows, _ in PAIRS[:n]) for n in range(len(PAIRS) + 1)]
 ORDER = (
-    "sent:00", "sent:01", "sent:10", "sent:11", "rest",
+    "sent:0", "sent:1", "rest",
     "first:00", "first:01", "first:10", "first:11", "start:00", "start:01", "start:10", "start:11",
     "kept", "keep:00", "keep:01", "end:00", "end:01", "start:00", "start:01",
     "keep:10", "keep:11", "end:10", "start:10", "end:11", "start:11",
@@ -90,6 +90,13 @@
     return store
 
 
+def into_pairs(refs):
+    def store(n, half, place, value):
+        refs[n][half, place // 4, place // 2 % 2, place % 2] = value
+
+    return store
+
+
 def into_flat(ref):
     def store(n, half, place, value):
         rows = PAIRS[n][0]
@@ -115,7 +122,7 @@
 
 
 def sent_kernel(ff_hbm, active_hbm, x_ref, m_ref, *refs):
-    outs, refs = refs[:STREAMS], refs[STREAMS:]
+    outs, refs = refs[: len(PAIRS)], refs[len(PAIRS) :]
     x_other, x_own, mt_ref, ff_ref, active_ref, sem, x_sem, own_sem, m_buf, m_sem = refs
     numbers = [
         pltpu.make_async_copy(ff_hbm, ff_ref, sem.at[0]),
@@ -143,7 +150,7 @@
         keep = column < BLOCK * ff_ref[live[s]]
         values = jnp.where(keep, values, jnp.zeros_like(values))
         mt_ref[:, s * 256 : (s + 1) * 256] = values.T
-    multiply(mt_ref, x_other, (into(outs), None), functools.partial(await_tiles, x_other, x_sem))
+    multiply(mt_ref, x_other, (into_pairs(outs), None), functools.partial(await_tiles, x_other, x_sem))
     for i in range(4):
         await_tiles(x_own, own_sem, i)
 
@@ -173,7 +180,7 @@
         sent_kernel,
         (ff_blocks, layer_active, x, m),
         (hbm, hbm, hbm, hbm),
-        pieces + [tiles, tiles, vmem((m.shape[2], LIVE * 256), jnp.bfloat16)],
+        [vmem((2, 2, 2, 2, rows, LANES), jnp.float32) for rows, _ in PAIRS] + [tiles, tiles, vmem((m.shape[2], LIVE * 256), jnp.bfloat16)],
         [
             pltpu.SMEM((4,), jnp.int32),
             pltpu.SMEM((4,), jnp.int32),
@@ -200,10 +207,11 @@
 
 
 def sum_kernel(*refs):
-    for own, other, out in zip(refs[:STREAMS], refs[STREAMS : 2 * STREAMS], refs[2 * STREAMS :]):
+    owns, others, outs = refs[:STREAMS], refs[STREAMS:-STREAMS], refs[-STREAMS:]
+    for n, (own, out) in enumerate(zip(owns, outs)):
         def step(k, _):
             at = k // 4, k // 2 % 2, k % 2
-            out[at] = own[at] + other[at]
+            out[at] = own[at] + others[n // 2][(n % 2, *at)]
             return 0
 
         lax.fori_loop(0, 8, step, 0)
@@ -212,7 +220,7 @@
 def sums(owns, others):
     return pl.pallas_call(
         sum_kernel,
-        in_specs=[pl.BlockSpec(memory_space=pltpu.VMEM)] * (2 * STREAMS),
+        in_specs=[pl.BlockSpec(memory_space=pltpu.VMEM)] * (len(owns) + len(others)),
         out_specs=[pl.BlockSpec(memory_space=pltpu.VMEM)] * STREAMS,
         out_shape=[pltpu.VMEM(o.shape, o.dtype) for o in owns],
         input_output_aliases={n: n for n in range(STREAMS)},
@@ -251,6 +259,24 @@
             stream.keep = [p[1] for p in parts]
         else:
             stream.send = self.token = self.tie(sum(parts[1:]) + parts[0])
+
+
+def message_kernel(*refs):
+    *parts, out = refs
+    total = sum(jnp.sum((p[...] * p[...]).reshape(-1, 8, LANES), axis=0) for p in parts)
+    total = jnp.sum(jnp.sum(total, axis=0, keepdims=True), axis=1, keepdims=True)
+    out[...] = jnp.broadcast_to(total[None], out.shape)
+
+
+def message(parts):
+    devices = math.prod(SIZES[a] for a in DP)
+    return pl.pallas_call(
+        message_kernel,
+        in_specs=[pl.BlockSpec(memory_space=pltpu.VMEM)] * len(parts),
+        out_specs=pl.BlockSpec(memory_space=pltpu.VMEM),
+        out_shape=jax.ShapeDtypeStruct((devices, 1, LANES), jnp.float32),
+        compiler_params=pltpu.CompilerParams(vmem_limit_bytes=2 * 1024 * 1024),
+    )(*parts)
 
 
 def shards(inputs, gate_cotangent, ff_blocks, layer_active, param, moment, second_moment):
@@ -266,11 +292,13 @@
             line.token = line.tie(other_kept)
             flat = line.tie(swap(line.token, "core", 1))
             continue
+        if act == "sent":
+            n = int(names[0])
+            line.token = line.tie(sent[n])
+            flying[n] = swap(line.token, "core", 1)
+            continue
         n, half = (int(c) for c in names[0])
-        if act == "sent":
-            line.token = line.tie(sent[2 * n + half])
-            flying[n, half] = swap(line.token, "core", 1)
-        elif act == "first":
+        if act == "first":
             if not firsts:
                 others = [line.tie(f) for f in flying.values()]
                 firsts = sums(owns[:STREAMS], others)
@@ -284,14 +312,11 @@
         else:
             getattr(line, act)(streams[n, half])
     done = [stream.send for stream in streams.values()]
-    squares = sum(jnp.sum(t * t, axis=0, keepdims=True) for t in done)
-    devices = math.prod(SIZES[a] for a in DP)
-    squares = lax.all_to_all(jnp.broadcast_to(squares[None], (devices, 1, LANES)), DP, 0, 0, tiled=True)
-    squares = jnp.sum(squares, axis=0)
+    squares = jnp.sum(lax.all_to_all(message(done), DP, 0, 0, tiled=True), axis=0)
     blocks = jnp.concatenate(done, axis=0).T.reshape(8, -1, gate_cotangent.shape[2])
     beside = jnp.broadcast_to(squares[None], blocks.shape[:2] + (LANES,))
     blocks = lax.all_to_all(jnp.concatenate([blocks, beside], axis=2), MP, 0, 0, tiled=True)
-    total = jnp.sqrt(jnp.sum(blocks[:, 0, -LANES:]))
+    total = jnp.sqrt(jnp.sum(blocks[:, :, -LANES : 1 - LANES], axis=0))
     gradient = blocks[:, :, :-LANES].transpose(1, 0, 2).reshape(param.shape)
     factor = jnp.minimum(1.0, math.sqrt(1.0 * D * FF) / (total + 1e-06))
     clipped = gradient * factor

time: 117 us -> 116 us (level)
    ppermute x21 -> x19, waiting for transfers between devices: 33.6 us -> 33.9 us  [swap(): lax.ppermute(value, axis, [(i, i ^ mask) for i in range(SIZES[axis])])]
    ppermute x21 -> x19, starting transfers between devices: 39 us -> 38.8 us  [swap(): lax.ppermute(value, axis, [(i, i ^ mask) for i in range(SIZES[axis])])]
  transfers between devices with their start and end apart: 22 -> 20, of which waited for: 11 -> 10; matrix products, arithmetic and copies ran while one was open for 1% -> 1% of each run, Pallas kernels for 3% -> 3%
where the time goes in v4:
time: 116 us
  starting transfers between devices  45.5 us (39%)
  waiting for transfers between devices  43.4 us (37%)
  blocking collectives  12.4 us (11%)
  Pallas kernels  10.5 us (9%)
  other arithmetic  2.45 us (2%)
    ppermute x19, starting transfers between devices, swap(): lax.ppermute(value, axis, [(i, i ^ mask) for i in range(SIZES[axis])])  38.8 us
    ppermute x19, waiting for transfers between devices, swap(): lax.ppermute(value, axis, [(i, i ^ mask) for i in range(SIZES[axis])])  33.9 us
    all_to_all x1, blocking collectives, shards(): lax.all_to_all(jnp.concatenate([blocks, beside], axis=2), MP, 0, 0, tiled...  12.4 us
    all_to_all x1, waiting for transfers between devices, shards(): lax.all_to_all(message(done), DP, 0, 0, tiled=True)  9.48 us
    pallas_call x2, Pallas kernels, call(): pl.pallas_call(kernel, in_specs=[pl.BlockSpec(memory_space=space) for spa...  8.94 us
    all_to_all x1, starting transfers between devices, shards(): lax.all_to_all(message(done), DP, 0, 0, tiled=True)  6.63 us
  transfers between devices with their start and end apart: 20, of which 10 were waited for; matrix products, arithmetic and copies ran while one was open for 1% of the time, Pallas kernels for 3%

profile of v4, /device:TPU:2, one launch (start us, length us, event | category | flops | bytes accessed | tf_op | source)
XLA Modules:
  0.0 115.5 jit_solution(5592119656363512203)
XLA Ops:
  0.6 5.1 %shard_map.94 = (f32[2,2,2,2,256,128]{5,4,3,2,1,0:T(8,128)S(1)}, f32[2,2,2,2,128,128]{5,4,3,2,1,0:T(8,128)S(1)}, bf16[4,3,256,512]{3,2,1,0:T(8,128)(2,1)S(1)}, b...) custom-call(s32[4]{0:T(128)} %ff_hbm.1, s32[4]{0:T(128)} %active_hbm.1, bf16[4,256,4096]{2,1,0:T(8,128)(2,1)} %x_ref.1, ...), custom_call_target="tpu_custom_call" | custom-call | tf_op jit(solution)/shard_map/pallas_call | solution.py:165
  5.7 0.1 collective-permute-start
  5.8 0.5 collective-permute-start.1
  6.3 3.8 %shard_map.95 = (f32[6144,128]{1,0:T(8,128)S(1)}, f32[2,2,2,256,128]{4,3,2,1,0:T(8,128)S(1)}, f32[2,2,2,256,128]{4,3,2,1,0:T(8,128)S(1)}, f32[2,2,2,128,128]{4,3...) custom-call(bf16[768,768]{1,0:T(8,128)(2,1)S(1)} %get-tuple-element., ...), custom_call_target="tpu_custom_call" | custom-call | tf_op jit(solution)/shard_map/pallas_call | solution.py:165
  10.2 1.3 %collective-permute-done.1.refs_5_ = f32[2,2,2,2,128,128]{5,4,3,2,1,0:T(8,128)S(1)} collective-permute-done((f32[2,2,2,2,128,128]{5,4,3,2,1,0:T(8,128)S(1)}, f32[2,2,2,2,128,128]{5,4,3,2,1,0:T(8,128)S(1)}, u32[]{:S(2)}, u32[]{:S(2)}) %collective-permute-start.1) | collective-permute-done | bytes 1048608 | tf_op jit(solution)/shard_map/ppermute | solution.py:41
  11.5 0.0 collective-permute-done.refs_4_
  11.5 0.8 shard_map.96
  12.3 0.2 collective-permute-start.3
  12.5 1.6 %collective-permute-start.2 = (f32[2,2,2,256,128]{4,3,2,1,0:T(8,128)S(1)}, f32[2,2,2,256,128]{4,3,2,1,0:T(8,128)S(1)}, u32[]{:S(2)}, u32[]{:S(2)}) collective-permute-start(f32[2,2,2,256,128]{4,3,2,1,0:T(8,128)S(1)} %get-tuple-element.62), channel_id=1, source_target_pairs={{0,64},{64,0},{128,192},{192,128},{1,65},{65,1},{129,193},{193,129... | collective-permute-start | bytes 3145736 | tf_op jit(solution)/shard_map/ppermute | solution.py:41
  14.1 2.2 %collective-permute-start.4 = (f32[2,2,2,256,128]{4,3,2,1,0:T(8,128)S(1)}, f32[2,2,2,256,128]{4,3,2,1,0:T(8,128)S(1)}, u32[]{:S(2)}, u32[]{:S(2)}) collective-permute-start(f32[2,2,2,256,128]{4,3,2,1,0:T(8,128)S(1)} %get-tuple-element.68), channel_id=1, source_target_pairs={{0,192},{64,128},{128,64},{192,0},{1,193},{65,129},{129,65},{193,1... | collective-permute-start | bytes 3145736 | tf_op jit(solution)/shard_map/ppermute | solution.py:41
  16.3 6.3 %collective-permute-start.6 = (f32[2,2,2,128,128]{4,3,2,1,0:T(8,128)S(1)}, f32[2,2,2,128,128]{4,3,2,1,0:T(8,128)S(1)}, u32[]{:S(2)}, u32[]{:S(2)}) collective-permute-start(f32[2,2,2,128,128]{4,3,2,1,0:T(8,128)S(1)} %get-tuple-element.70), channel_id=1, source_target_pairs={{0,48},{16,32},{32,16},{48,0},{1,49},{17,33},{33,17},{49,1},{2,50}... | collective-permute-start | bytes 1572872 | tf_op jit(solution)/shard_map/ppermute | solution.py:41
  22.6 1.5 %collective-permute-start.7 = (f32[2,2,2,128,128]{4,3,2,1,0:T(8,128)S(1)}, f32[2,2,2,128,128]{4,3,2,1,0:T(8,128)S(1)}, u32[]{:S(2)}, u32[]{:S(2)}) collective-permute-start(f32[2,2,2,128,128]{4,3,2,1,0:T(8,128)S(1)} %get-tuple-element.69), channel_id=1, source_target_pairs={{0,16},{16,0},{32,48},{48,32},{1,17},{17,1},{33,49},{49,33},{2,18}... | collective-permute-start | bytes 1572872 | tf_op jit(solution)/shard_map/ppermute | solution.py:41
  24.1 0.0 collective-permute-done.3
  24.1 0.1 fusion.10
  24.2 0.1 add.168
  24.3 0.1 add.167
  24.4 13.5 %collective-permute-done.2 = f32[2,2,2,256,128]{4,3,2,1,0:T(8,128)S(1)} collective-permute-done((f32[2,2,2,256,128]{4,3,2,1,0:T(8,128)S(1)}, f32[2,2,2,256,128]{4,3,2,1,0:T(8,128)S(1)}, u32[]{:S(2)}, u32[]{:S(2)}) %collective-permute-start.2) | collective-permute-done | bytes 1048608 | tf_op jit(solution)/shard_map/ppermute | solution.py:41
  38.0 0.1 fusion
  38.0 2.4 %collective-permute-done.4 = f32[2,2,2,256,128]{4,3,2,1,0:T(8,128)S(1)} collective-permute-done((f32[2,2,2,256,128]{4,3,2,1,0:T(8,128)S(1)}, f32[2,2,2,256,128]{4,3,2,1,0:T(8,128)S(1)}, u32[]{:S(2)}, u32[]{:S(2)}) %collective-permute-start.4) | collective-permute-done | bytes 1048608 | tf_op jit(solution)/shard_map/ppermute | solution.py:41
  40.5 0.1 add_bitcast_fusion
  40.6 2.3 %collective-permute-start.5 = (f32[2,2,256,128]{3,2,1,0:T(8,128)S(1)}, f32[2,2,256,128]{3,2,1,0:T(8,128)S(1)}, u32[]{:S(2)}, u32[]{:S(2)}) collective-permute-start(f32[2,2,256,128]{3,2,1,0:T(8,128)S(1)} %fusion), channel_id=1, source_target_pairs={{0,192},{64,128},{128,64},{192,0},{1,193},{65,129},{129,65},{193,1... | collective-permute-start | bytes 1572872 | tf_op jit(solution)/shard_map/ppermute | solution.py:41
  42.8 0.1 fusion.11
  42.9 0.1 collective-permute-start.11
  43.0 0.1 add.174
  43.1 0.1 add.173
  43.2 5.0 %collective-permute-done.7 = f32[2,2,2,128,128]{4,3,2,1,0:T(8,128)S(1)} collective-permute-done((f32[2,2,2,128,128]{4,3,2,1,0:T(8,128)S(1)}, f32[2,2,2,128,128]{4,3,2,1,0:T(8,128)S(1)}, u32[]{:S(2)}, u32[]{:S(2)}) %collective-permute-start.7) | collective-permute-done | bytes 524320 | tf_op jit(solution)/shard_map/ppermute | solution.py:41
  48.2 1.4 %collective-permute-start.10 = (f32[2,2,128,128]{3,2,1,0:T(8,128)S(1)}, f32[2,2,128,128]{3,2,1,0:T(8,128)S(1)}, u32[]{:S(2)}, u32[]{:S(2)}) collective-permute-start(f32[2,2,128,128]{3,2,1,0:T(8,128)S(1)} %add_bitcast_fusion.2), channel_id=1, source_target_pairs={{0,48},{16,32},{32,16},{48,0},{1,49},{17,33},{33,17},{49,1},{2,50}... | collective-permute-start | bytes 786440 | tf_op jit(solution)/shard_map/ppermute | solution.py:41
  49.6 0.0 collective-permute-done.6
  49.6 1.5 %collective-permute-start.9 = (f32[2,2,128,128]{3,2,1,0:T(8,128)S(1)}, f32[2,2,128,128]{3,2,1,0:T(8,128)S(1)}, u32[]{:S(2)}, u32[]{:S(2)}) collective-permute-start(f32[2,2,128,128]{3,2,1,0:T(8,128)S(1)} %add_bitcast_fusion.1), channel_id=1, source_target_pairs={{0,16},{16,0},{32,48},{48,32},{1,17},{17,1},{33,49},{49,33},{2,18}... | collective-permute-start | bytes 786440 | tf_op jit(solution)/shard_map/ppermute | solution.py:41
  51.2 3.8 %collective-permute-done.5 = f32[2,2,256,128]{3,2,1,0:T(8,128)S(1)} collective-permute-done((f32[2,2,256,128]{3,2,1,0:T(8,128)S(1)}, f32[2,2,256,128]{3,2,1,0:T(8,128)S(1)}, u32[]{:S(2)}, u32[]{:S(2)}) %collective-permute-start.5) | collective-permute-done | bytes 524320 | tf_op jit(solution)/shard_map/ppermute | solution.py:41
  55.0 3.4 %collective-permute-start.8 = (f32[2,256,128]{2,1,0:T(8,128)S(1)}, f32[2,256,128]{2,1,0:T(8,128)S(1)}, u32[]{:S(2)}, u32[]{:S(2)}) collective-permute-start(f32[2,256,128]{2,1,0:T(8,128)S(1)} %fusion.2), channel_id=1, source_target_pairs={{0,16},{16,0},{32,48},{48,32},{1,17},{17,1},{33,49},{49,33},{2,18}... | collective-permute-start | bytes 786440 | tf_op jit(solution)/shard_map/ppermute | solution.py:41
  58.3 0.0 collective-permute-done.11
  58.3 0.1 bitcast_add_fusion
  58.4 4.8 %collective-permute-start.17 = (f32[2,256,128]{2,1,0:T(8,128)S(1)}, f32[2,256,128]{2,1,0:T(8,128)S(1)}, u32[]{:S(2)}, u32[]{:S(2)}) collective-permute-start(f32[2,256,128]{2,1,0:T(8,128)S(1)} %bitcast_add_fusion), channel_id=1, source_target_pairs={{0,48},{16,32},{32,16},{48,0},{1,49},{17,33},{33,17},{49,1},{2,50}... | collective-permute-start | bytes 786440 | tf_op jit(solution)/shard_map/ppermute | solution.py:41
  63.1 0.0 collective-permute-done.10
  63.2 0.1 collective-permute-start.13
  63.3 0.3 collective-permute-done.9
  63.6 2.0 %collective-permute-start.12 = (f32[2,128,128]{2,1,0:T(8,128)S(1)}, f32[2,128,128]{2,1,0:T(8,128)S(1)}, u32[]{:S(2)}, u32[]{:S(2)}) collective-permute-start(f32[2,128,128]{2,1,0:T(8,128)S(1)} %bitcast_add_fusion.12), channel_id=1, source_target_pairs={{0,192},{64,128},{128,64},{192,0},{1,193},{65,129},{129,65},{193,1... | collective-permute-start | bytes 393224 | tf_op jit(solution)/shard_map/ppermute | solution.py:41
  65.6 2.6 %collective-permute-done.13 = f32[2,128,128]{2,1,0:T(8,128)S(1)} collective-permute-done((f32[2,128,128]{2,1,0:T(8,128)S(1)}, f32[2,128,128]{2,1,0:T(8,128)S(1)}, u32[]{:S(2)}, u32[]{:S(2)}) %collective-permute-start.13) | collective-permute-done | bytes 131104 | tf_op jit(solution)/shard_map/ppermute | solution.py:41
  68.2 2.3 %collective-permute-start.16 = (f32[128,128]{1,0:T(8,128)S(1)}, f32[128,128]{1,0:T(8,128)S(1)}, u32[]{:S(2)}, u32[]{:S(2)}) collective-permute-start(f32[128,128]{1,0:T(8,128)S(1)} %bitcast_add_fusion.25), channel_id=1, source_target_pairs={{0,192},{64,128},{128,64},{192,0},{1,193},{65,129},{129,65},{193,1... | collective-permute-start | bytes 196616 | tf_op jit(solution)/shard_map/ppermute | solution.py:41
  70.5 0.1 collective-permute-done.12
  70.6 5.2 %collective-permute-start.15 = (f32[128,128]{1,0:T(8,128)S(1)}, f32[128,128]{1,0:T(8,128)S(1)}, u32[]{:S(2)}, u32[]{:S(2)}) collective-permute-start(f32[128,128]{1,0:T(8,128)S(1)} %bitcast_add_fusion.23), channel_id=1, source_target_pairs={{0,64},{64,0},{128,192},{192,128},{1,65},{65,1},{129,193},{193,129... | collective-permute-start | bytes 196616 | tf_op jit(solution)/shard_map/ppermute | solution.py:41
  75.8 0.0 collective-permute-done.8
  75.8 0.6 collective-permute-start.14
  76.4 0.0 collective-permute-done.17
  76.4 3.0 %collective-permute-start.18 = (f32[256,128]{1,0:T(8,128)S(1)}, f32[256,128]{1,0:T(8,128)S(1)}, u32[]{:S(2)}, u32[]{:S(2)}) collective-permute-start(f32[256,128]{1,0:T(8,128)S(1)} %bitcast_add_fusion.6), channel_id=1, source_target_pairs={{0,16},{16,0},{32,48},{48,32},{1,17},{17,1},{33,49},{49,33},{2,18}... | collective-permute-start | bytes 393224 | tf_op jit(solution)/shard_map/ppermute | solution.py:41
  79.4 0.0 collective-permute-done.16
  79.4 0.0 collective-permute-done.15
  79.5 4.9 %collective-permute-done.14 = f32[256,128]{1,0:T(8,128)S(1)} collective-permute-done((f32[256,128]{1,0:T(8,128)S(1)}, f32[256,128]{1,0:T(8,128)S(1)}, u32[]{:S(2)}, u32[]{:S(2)}) %collective-permute-start.14) | collective-permute-done | bytes 131104 | tf_op jit(solution)/shard_map/ppermute | solution.py:41
  84.4 0.0 copy-start
  84.4 0.0 copy-start.1
  84.4 0.0 copy-start.2
  84.4 0.0 collective-permute-done.18
  84.5 0.7 shard_map.97
  85.2 6.6 %all-to-all-start = ((f32[32,1,128]{2,1,0:T(1,128)}), f32[32,1,128]{2,1,0:T(1,128)S(1)}, u32[]{:S(2)}, u32[]{:S(2)}) async-start(f32[32,1,128]{2,1,0:T(1,128)} %shard_map.97), calls=%async_computation | async-start | bytes 32768 | tf_op jit(solution)/shard_map/all_to_all | solution.py:315
  91.9 0.2 copy.16
  92.1 9.5 %all-to-all-done = f32[32,1,128]{2,1,0:T(1,128)S(1)} async-done(((f32[32,1,128]{2,1,0:T(1,128)}), f32[32,1,128]{2,1,0:T(1,128)S(1)}, u32[]{:S(2)}, u32[]{:S(2)}) %all-to-all-start) | async-done | bytes 16416 | tf_op jit(solution)/shard_map/all_to_all | solution.py:315
  101.5 0.1 reduce_sum.18
  101.6 12.4 %all_to_all.10 = f32[8,16,896]{2,1,0:T(8,128)S(1)} all-to-all(f32[8,16,896]{2,1,0:T(8,128)S(1)} %pad_maximum_fusion), channel_id=1, replica_groups=mesh['y'=4,'z'=4,'core'=2,'z_lo'=2,'x'=4] {'z_lo','x'}, dimensions={0} | all-to-all | bytes 917504 | tf_op jit(solution)/shard_map/all_to_all | solution.py:318
  114.1 0.1 slice_reduce_fusion
  114.2 0.0 copy-done
  114.2 0.0 copy-done.1
  114.2 0.0 copy-done.2
  114.2 1.3 %multiply_subtract_fusion = (f32[16,6144]{1,0:T(8,128)}, f32[16,6144]{1,0:T(8,128)}, f32[16,6144]{1,0:T(8,128)}) fusion(f32[16,6144]{1,0:T(8,128)S(1)} %copy-done, f32[16,6144]{1,0:T(8,128)S(1)} %bitcast.166, f32[16]{0:T(128)S(1)} %divide_minimum_fusion, f32[16,6144]{1,0:T(8,128)S(1)} %copy-done.1, f32[16,6144]{1,0:T(8,128)S(1)} %copy-done.2), kind=kLoop, calls=%fused_computation.8 | loop fusion | flops 1572864 | bytes 2752576 | tf_op jit(solution)/shard_map/sub | solution.py:327
  (19 shorter events, 0.5 us)
Async XLA Ops:
  5.7 5.8 %collective-permute-start = (f32[2,2,2,2,256,128]{5,4,3,2,1,0:T(8,128)S(1)}, f32[2,2,2,2,256,128]{5,4,3,2,1,0:T(8,128)S(1)}, u32[]{:S(2)}, u32[]{:S(2)}) collective-permute-start(f32[2,2,2,2,256,128]{5,4,3,2,1,0:T(8,128)S(1)} %get-tuple-element.52), channel_id=1, source_target_pairs={{0,8},{8,0},{1,9},{9,1},{2,10},{10,2},{3,11},{11,3},{4,12},{12,4},... | collective-permute-start | bytes 6291464 | tf_op jit(solution)/shard_map/ppermute | solution.py:41
  5.8 5.6 %collective-permute-start.1 = (f32[2,2,2,2,128,128]{5,4,3,2,1,0:T(8,128)S(1)}, f32[2,2,2,2,128,128]{5,4,3,2,1,0:T(8,128)S(1)}, u32[]{:S(2)}, u32[]{:S(2)}) collective-permute-start(f32[2,2,2,2,128,128]{5,4,3,2,1,0:T(8,128)S(1)} %get-tuple-element.53), channel_id=1, source_target_pairs={{0,8},{8,0},{1,9},{9,1},{2,10},{10,2},{3,11},{11,3},{4,12},{12,4},... | collective-permute-start | bytes 3145736 | tf_op jit(solution)/shard_map/ppermute | solution.py:41
  12.3 11.8 %collective-permute-start.3 = (f32[6144,128]{1,0:T(8,128)S(1)}, f32[6144,128]{1,0:T(8,128)S(1)}, u32[]{:S(2)}, u32[]{:S(2)}) collective-permute-start(f32[6144,128]{1,0:T(8,128)S(1)} %get-tuple-element.71), channel_id=1, source_target_pairs={{0,8},{8,0},{1,9},{9,1},{2,10},{10,2},{3,11},{11,3},{4,12},{12,4},... | collective-permute-start | bytes 9437192 | tf_op jit(solution)/shard_map/ppermute | solution.py:41
  12.5 25.4 %collective-permute-start.2 = (f32[2,2,2,256,128]{4,3,2,1,0:T(8,128)S(1)}, f32[2,2,2,256,128]{4,3,2,1,0:T(8,128)S(1)}, u32[]{:S(2)}, u32[]{:S(2)}) collective-permute-start(f32[2,2,2,256,128]{4,3,2,1,0:T(8,128)S(1)} %get-tuple-element.62), channel_id=1, source_target_pairs={{0,64},{64,0},{128,192},{192,128},{1,65},{65,1},{129,193},{193,129... | collective-permute-start | bytes 3145736 | tf_op jit(solution)/shard_map/ppermute | solution.py:41
  14.1 26.4 %collective-permute-start.4 = (f32[2,2,2,256,128]{4,3,2,1,0:T(8,128)S(1)}, f32[2,2,2,256,128]{4,3,2,1,0:T(8,128)S(1)}, u32[]{:S(2)}, u32[]{:S(2)}) collective-permute-start(f32[2,2,2,256,128]{4,3,2,1,0:T(8,128)S(1)} %get-tuple-element.68), channel_id=1, source_target_pairs={{0,192},{64,128},{128,64},{192,0},{1,193},{65,129},{129,65},{193,1... | collective-permute-start | bytes 3145736 | tf_op jit(solution)/shard_map/ppermute | solution.py:41
  16.3 33.3 %collective-permute-start.6 = (f32[2,2,2,128,128]{4,3,2,1,0:T(8,128)S(1)}, f32[2,2,2,128,128]{4,3,2,1,0:T(8,128)S(1)}, u32[]{:S(2)}, u32[]{:S(2)}) collective-permute-start(f32[2,2,2,128,128]{4,3,2,1,0:T(8,128)S(1)} %get-tuple-element.70), channel_id=1, source_target_pairs={{0,48},{16,32},{32,16},{48,0},{1,49},{17,33},{33,17},{49,1},{2,50}... | collective-permute-start | bytes 1572872 | tf_op jit(solution)/shard_map/ppermute | solution.py:41
  22.6 25.5 %collective-permute-start.7 = (f32[2,2,2,128,128]{4,3,2,1,0:T(8,128)S(1)}, f32[2,2,2,128,128]{4,3,2,1,0:T(8,128)S(1)}, u32[]{:S(2)}, u32[]{:S(2)}) collective-permute-start(f32[2,2,2,128,128]{4,3,2,1,0:T(8,128)S(1)} %get-tuple-element.69), channel_id=1, source_target_pairs={{0,16},{16,0},{32,48},{48,32},{1,17},{17,1},{33,49},{49,33},{2,18}... | collective-permute-start | bytes 1572872 | tf_op jit(solution)/shard_map/ppermute | solution.py:41
  40.6 14.4 %collective-permute-start.5 = (f32[2,2,256,128]{3,2,1,0:T(8,128)S(1)}, f32[2,2,256,128]{3,2,1,0:T(8,128)S(1)}, u32[]{:S(2)}, u32[]{:S(2)}) collective-permute-start(f32[2,2,256,128]{3,2,1,0:T(8,128)S(1)} %fusion), channel_id=1, source_target_pairs={{0,192},{64,128},{128,64},{192,0},{1,193},{65,129},{129,65},{193,1... | collective-permute-start | bytes 1572872 | tf_op jit(solution)/shard_map/ppermute | solution.py:41
  42.9 15.4 %collective-permute-start.11 = (f32[2,2,256,128]{3,2,1,0:T(8,128)S(1)}, f32[2,2,256,128]{3,2,1,0:T(8,128)S(1)}, u32[]{:S(2)}, u32[]{:S(2)}) collective-permute-start(f32[2,2,256,128]{3,2,1,0:T(8,128)S(1)} %add_bitcast_fusion), channel_id=1, source_target_pairs={{0,64},{64,0},{128,192},{192,128},{1,65},{65,1},{129,193},{193,129... | collective-permute-start | bytes 1572872 | tf_op jit(solution)/shard_map/ppermute | solution.py:41
  48.2 15.0 %collective-permute-start.10 = (f32[2,2,128,128]{3,2,1,0:T(8,128)S(1)}, f32[2,2,128,128]{3,2,1,0:T(8,128)S(1)}, u32[]{:S(2)}, u32[]{:S(2)}) collective-permute-start(f32[2,2,128,128]{3,2,1,0:T(8,128)S(1)} %add_bitcast_fusion.2), channel_id=1, source_target_pairs={{0,48},{16,32},{32,16},{48,0},{1,49},{17,33},{33,17},{49,1},{2,50}... | collective-permute-start | bytes 786440 | tf_op jit(solution)/shard_map/ppermute | solution.py:41
  49.6 13.9 %collective-permute-start.9 = (f32[2,2,128,128]{3,2,1,0:T(8,128)S(1)}, f32[2,2,128,128]{3,2,1,0:T(8,128)S(1)}, u32[]{:S(2)}, u32[]{:S(2)}) collective-permute-start(f32[2,2,128,128]{3,2,1,0:T(8,128)S(1)} %add_bitcast_fusion.1), channel_id=1, source_target_pairs={{0,16},{16,0},{32,48},{48,32},{1,17},{17,1},{33,49},{49,33},{2,18}... | collective-permute-start | bytes 786440 | tf_op jit(solution)/shard_map/ppermute | solution.py:41
  55.0 20.8 %collective-permute-start.8 = (f32[2,256,128]{2,1,0:T(8,128)S(1)}, f32[2,256,128]{2,1,0:T(8,128)S(1)}, u32[]{:S(2)}, u32[]{:S(2)}) collective-permute-start(f32[2,256,128]{2,1,0:T(8,128)S(1)} %fusion.2), channel_id=1, source_target_pairs={{0,16},{16,0},{32,48},{48,32},{1,17},{17,1},{33,49},{49,33},{2,18}... | collective-permute-start | bytes 786440 | tf_op jit(solution)/shard_map/ppermute | solution.py:41
  58.4 18.0 %collective-permute-start.17 = (f32[2,256,128]{2,1,0:T(8,128)S(1)}, f32[2,256,128]{2,1,0:T(8,128)S(1)}, u32[]{:S(2)}, u32[]{:S(2)}) collective-permute-start(f32[2,256,128]{2,1,0:T(8,128)S(1)} %bitcast_add_fusion), channel_id=1, source_target_pairs={{0,48},{16,32},{32,16},{48,0},{1,49},{17,33},{33,17},{49,1},{2,50}... | collective-permute-start | bytes 786440 | tf_op jit(solution)/shard_map/ppermute | solution.py:41
  63.2 5.1 %collective-permute-start.13 = (f32[2,128,128]{2,1,0:T(8,128)S(1)}, f32[2,128,128]{2,1,0:T(8,128)S(1)}, u32[]{:S(2)}, u32[]{:S(2)}) collective-permute-start(f32[2,128,128]{2,1,0:T(8,128)S(1)} %bitcast_add_fusion.14), channel_id=1, source_target_pairs={{0,64},{64,0},{128,192},{192,128},{1,65},{65,1},{129,193},{193,129... | collective-permute-start | bytes 393224 | tf_op jit(solution)/shard_map/ppermute | solution.py:41
  63.6 7.0 %collective-permute-start.12 = (f32[2,128,128]{2,1,0:T(8,128)S(1)}, f32[2,128,128]{2,1,0:T(8,128)S(1)}, u32[]{:S(2)}, u32[]{:S(2)}) collective-permute-start(f32[2,128,128]{2,1,0:T(8,128)S(1)} %bitcast_add_fusion.12), channel_id=1, source_target_pairs={{0,192},{64,128},{128,64},{192,0},{1,193},{65,129},{129,65},{193,1... | collective-permute-start | bytes 393224 | tf_op jit(solution)/shard_map/ppermute | solution.py:41
  68.2 11.2 %collective-permute-start.16 = (f32[128,128]{1,0:T(8,128)S(1)}, f32[128,128]{1,0:T(8,128)S(1)}, u32[]{:S(2)}, u32[]{:S(2)}) collective-permute-start(f32[128,128]{1,0:T(8,128)S(1)} %bitcast_add_fusion.25), channel_id=1, source_target_pairs={{0,192},{64,128},{128,64},{192,0},{1,193},{65,129},{129,65},{193,1... | collective-permute-start | bytes 196616 | tf_op jit(solution)/shard_map/ppermute | solution.py:41
  70.6 8.8 %collective-permute-start.15 = (f32[128,128]{1,0:T(8,128)S(1)}, f32[128,128]{1,0:T(8,128)S(1)}, u32[]{:S(2)}, u32[]{:S(2)}) collective-permute-start(f32[128,128]{1,0:T(8,128)S(1)} %bitcast_add_fusion.23), channel_id=1, source_target_pairs={{0,64},{64,0},{128,192},{192,128},{1,65},{65,1},{129,193},{193,129... | collective-permute-start | bytes 196616 | tf_op jit(solution)/shard_map/ppermute | solution.py:41
  75.8 8.6 %collective-permute-start.14 = (f32[256,128]{1,0:T(8,128)S(1)}, f32[256,128]{1,0:T(8,128)S(1)}, u32[]{:S(2)}, u32[]{:S(2)}) collective-permute-start(f32[256,128]{1,0:T(8,128)S(1)} %fusion.4), channel_id=1, source_target_pairs={{0,48},{16,32},{32,16},{48,0},{1,49},{17,33},{33,17},{49,1},{2,50}... | collective-permute-start | bytes 393224 | tf_op jit(solution)/shard_map/ppermute | solution.py:41
  76.4 8.0 %collective-permute-start.18 = (f32[256,128]{1,0:T(8,128)S(1)}, f32[256,128]{1,0:T(8,128)S(1)}, u32[]{:S(2)}, u32[]{:S(2)}) collective-permute-start(f32[256,128]{1,0:T(8,128)S(1)} %bitcast_add_fusion.6), channel_id=1, source_target_pairs={{0,16},{16,0},{32,48},{48,32},{1,17},{17,1},{33,49},{49,33},{2,18}... | collective-permute-start | bytes 393224 | tf_op jit(solution)/shard_map/ppermute | solution.py:41
  84.4 29.8 %copy-start = (f32[16,6144]{1,0:T(8,128)S(1)}, f32[16,6144]{1,0:T(8,128)}, u32[]{:S(2)}) copy-start(f32[16,6144]{1,0:T(8,128)} %param.11) | copy-start | bytes 1179652
  84.4 29.8 %copy-start.1 = (f32[16,6144]{1,0:T(8,128)S(1)}, f32[16,6144]{1,0:T(8,128)}, u32[]{:S(2)}) copy-start(f32[16,6144]{1,0:T(8,128)} %param.12) | copy-start | bytes 1179652
  84.4 29.8 %copy-start.2 = (f32[16,6144]{1,0:T(8,128)S(1)}, f32[16,6144]{1,0:T(8,128)}, u32[]{:S(2)}) copy-start(f32[16,6144]{1,0:T(8,128)} %param.13) | copy-start | bytes 1179652
  85.2 16.3 %all-to-all-start = ((f32[32,1,128]{2,1,0:T(1,128)}), f32[32,1,128]{2,1,0:T(1,128)S(1)}, u32[]{:S(2)}, u32[]{:S(2)}) async-start(f32[32,1,128]{2,1,0:T(1,128)} %shard_map.97), calls=%async_computation | async-start | bytes 32768 | tf_op jit(solution)/shard_map/all_to_all | solution.py:315

commit v5 on v4

--- a/solution.py
+++ b/solution.py
@@ -48,7 +48,7 @@
     return (y * 4 + z) * 2 + core
 
 
-def multiply(mt_ref, x_buf, stores, ready=lambda i: None):
+def multiply(mt_ref, x_buf, stores, ready=lambda i: None, pairs=(0, 1)):
     for i in range(4):
         ready(i)
         runs, first = [], 0
@@ -58,7 +58,7 @@
                 for t in range(4):
                     bit = {("y", 1): i // 2, ("y", 3): i % 2, ("z", 1): t // 2, ("z", 3): t % 2}
                     at = [bit[step] for step in steps]
-                    if stores[at[0]]:
+                    if stores[at[0]] and n in pairs:
                         tiles.append((t, at[0], 4 * at[1] + 2 * at[2] + at[3]))
                 lanes = [t for t, _, _ in tiles]
                 if runs and runs[-1][0] == lanes:
@@ -90,9 +90,9 @@
     return store
 
 
-def into_pairs(refs):
+def into_pair(ref):
     def store(n, half, place, value):
-        refs[n][half, place // 4, place // 2 % 2, place % 2] = value
+        ref[half, place // 4, place // 2 % 2, place % 2] = value
 
     return store
 
@@ -122,7 +122,7 @@
 
 
 def sent_kernel(ff_hbm, active_hbm, x_ref, m_ref, *refs):
-    outs, refs = refs[: len(PAIRS)], refs[len(PAIRS) :]
+    out, refs = refs[0], refs[1:]
     x_other, x_own, mt_ref, ff_ref, active_ref, sem, x_sem, own_sem, m_buf, m_sem = refs
     numbers = [
         pltpu.make_async_copy(ff_hbm, ff_ref, sem.at[0]),
@@ -150,9 +150,14 @@
         keep = column < BLOCK * ff_ref[live[s]]
         values = jnp.where(keep, values, jnp.zeros_like(values))
         mt_ref[:, s * 256 : (s + 1) * 256] = values.T
-    multiply(mt_ref, x_other, (into_pairs(outs), None), functools.partial(await_tiles, x_other, x_sem))
+    ready = functools.partial(await_tiles, x_other, x_sem)
+    multiply(mt_ref, x_other, (into_pair(out), None), ready, pairs=(0,))
     for i in range(4):
         await_tiles(x_own, own_sem, i)
+
+
+def next_kernel(mt_ref, x_other, out):
+    multiply(mt_ref, x_other, (into_pair(out), None), pairs=(1,))
 
 
 def rest_kernel(mt_ref, x_other, x_own, other_kept, *refs):
@@ -176,11 +181,12 @@
     hbm, vmem, sems = pltpu.HBM, pltpu.VMEM, pltpu.SemaphoreType.DMA
     pieces = [vmem((2, 2, 2, rows, LANES), jnp.float32) for rows, _ in PAIRS for _ in range(2)]
     tiles = vmem((4, LIVE, 256, 4 * LANES), jnp.bfloat16)
-    *sent, x_other, x_own, turned = call(
+    halves = [vmem((2, 2, 2, 2, rows, LANES), jnp.float32) for rows, _ in PAIRS]
+    sent, x_other, x_own, turned = call(
         sent_kernel,
         (ff_blocks, layer_active, x, m),
         (hbm, hbm, hbm, hbm),
-        [vmem((2, 2, 2, 2, rows, LANES), jnp.float32) for rows, _ in PAIRS] + [tiles, tiles, vmem((m.shape[2], LIVE * 256), jnp.bfloat16)],
+        halves[:1] + [tiles, tiles, vmem((m.shape[2], LIVE * 256), jnp.bfloat16)],
         [
             pltpu.SMEM((4,), jnp.int32),
             pltpu.SMEM((4,), jnp.int32),
@@ -193,6 +199,9 @@
         6,
     )
 
+    def next_sent(tie):
+        return call(next_kernel, (tie(turned), x_other), (vmem, vmem), halves[1:], [], 4)[0]
+
     def rest(tie):
         return call(
             rest_kernel,
@@ -203,7 +212,7 @@
             6,
         )
 
-    return sent, rest
+    return sent, next_sent, rest
 
 
 def sum_kernel(*refs):
@@ -280,8 +289,8 @@
 
 
 def shards(inputs, gate_cotangent, ff_blocks, layer_active, param, moment, second_moment):
-    sent, rest = products(ff_blocks, layer_active, inputs, gate_cotangent)
-    flying, firsts, line = {}, None, Line(sent[0])
+    sent, next_sent, rest = products(ff_blocks, layer_active, inputs, gate_cotangent)
+    flying, firsts, line = {}, None, Line(sent)
     streams = {(n, half): Stream(pair[1][half]) for n, pair in enumerate(PAIRS) for half in range(2)}
     for act, *names in (event.split(":") for event in ORDER):
         if act == "rest":
@@ -294,7 +303,7 @@
             continue
         if act == "sent":
             n = int(names[0])
-            line.token = line.tie(sent[n])
+            line.token = line.tie(sent if n == 0 else next_sent(line.tie))
             flying[n] = swap(line.token, "core", 1)
             continue
         n, half = (int(c) for c in names[0])

time: 116 us -> 115 us (level)
    pallas_call x2 -> x3, Pallas kernels: 8.94 us -> 8.93 us  [call(): pl.pallas_call(kernel, in_specs=[pl.BlockSpec(memory_space=space) for spa...]
  transfers between devices with their start and end apart: 20 -> 20, of which waited for: 10 -> 10; matrix products, arithmetic and copies ran while one was open for 1% -> 1% of each run, Pallas kernels for 3% -> 4%
where the time goes in v5:
time: 115 us
  starting transfers between devices  45.4 us (39%)
  waiting for transfers between devices  42.9 us (37%)
  blocking collectives  12.4 us (11%)
  Pallas kernels  10.5 us (9%)
  other arithmetic  2.45 us (2%)
    ppermute x19, starting transfers between devices, swap(): lax.ppermute(value, axis, [(i, i ^ mask) for i in range(SIZES[axis])])  38.8 us
    ppermute x19, waiting for transfers between devices, swap(): lax.ppermute(value, axis, [(i, i ^ mask) for i in range(SIZES[axis])])  33.4 us
    all_to_all x1, blocking collectives, shards(): lax.all_to_all(jnp.concatenate([blocks, beside], axis=2), MP, 0, 0, tiled...  12.4 us
    all_to_all x1, waiting for transfers between devices, shards(): lax.all_to_all(message(done), DP, 0, 0, tiled=True)  9.48 us
    pallas_call x3, Pallas kernels, call(): pl.pallas_call(kernel, in_specs=[pl.BlockSpec(memory_space=space) for spa...  8.93 us
    all_to_all x1, starting transfers between devices, shards(): lax.all_to_all(message(done), DP, 0, 0, tiled=True)  6.59 us
  transfers between devices with their start and end apart: 20, of which 10 were waited for; matrix products, arithmetic and copies ran while one was open for 1% of the time, Pallas kernels for 4%

profile of v5, /device:TPU:2, one launch (start us, length us, event | category | flops | bytes accessed | tf_op | source)
XLA Modules:
  0.0 114.9 jit_solution(2291785071979547990)
XLA Ops:
  0.6 4.5 %shard_map.94 = (f32[2,2,2,2,256,128]{5,4,3,2,1,0:T(8,128)S(1)}, bf16[4,3,256,512]{3,2,1,0:T(8,128)(2,1)S(1)}, bf16[4,3,256,512]{3,2,1,0:T(8,128)(2,1)S(1)}, bf16[768,768]{1,0:T(8,128)(2,1)S(1)}) custom-call(s32[4]{0:T(128)} %ff_hbm.1, s32[4]{0:T(128)} %active_hbm.1, bf16[4,256,4096]{2,1,0:T(8,128)(2,1)} %x_ref.1, bf16[4,256,768]{2,1,0:T(8,128)(2,1)} %m_ref.1), custom_call_target="tpu_custom_call" | custom-call | tf_op jit(solution)/shard_map/pallas_call | solution.py:170
  5.1 0.1 collective-permute-start
  5.2 0.6 shard_map.95
  5.8 0.6 collective-permute-start.1
  6.4 3.8 %shard_map.96 = (f32[6144,128]{1,0:T(8,128)S(1)}, f32[2,2,2,256,128]{4,3,2,1,0:T(8,128)S(1)}, f32[2,2,2,256,128]{4,3,2,1,0:T(8,128)S(1)}, f32[2,2,2,128,128]{4,3...) custom-call(bf16[768,768]{1,0:T(8,128)(2,1)S(1)} %get-tuple-element., ...), custom_call_target="tpu_custom_call" | custom-call | tf_op jit(solution)/shard_map/pallas_call | solution.py:170
  10.3 0.6 collective-permute-done.1.refs_5_
  10.9 0.0 collective-permute-done.refs_4_
  10.9 0.8 shard_map.97
  11.7 0.2 collective-permute-start.3
  12.0 1.6 %collective-permute-start.2 = (f32[2,2,2,256,128]{4,3,2,1,0:T(8,128)S(1)}, f32[2,2,2,256,128]{4,3,2,1,0:T(8,128)S(1)}, u32[]{:S(2)}, u32[]{:S(2)}) collective-permute-start(f32[2,2,2,256,128]{4,3,2,1,0:T(8,128)S(1)} %get-tuple-element.60), channel_id=1, source_target_pairs={{0,64},{64,0},{128,192},{192,128},{1,65},{65,1},{129,193},{193,129... | collective-permute-start | bytes 3145736 | tf_op jit(solution)/shard_map/ppermute | solution.py:41
  13.6 2.2 %collective-permute-start.4 = (f32[2,2,2,256,128]{4,3,2,1,0:T(8,128)S(1)}, f32[2,2,2,256,128]{4,3,2,1,0:T(8,128)S(1)}, u32[]{:S(2)}, u32[]{:S(2)}) collective-permute-start(f32[2,2,2,256,128]{4,3,2,1,0:T(8,128)S(1)} %get-tuple-element.66), channel_id=1, source_target_pairs={{0,192},{64,128},{128,64},{192,0},{1,193},{65,129},{129,65},{193,1... | collective-permute-start | bytes 3145736 | tf_op jit(solution)/shard_map/ppermute | solution.py:41
  15.7 6.3 %collective-permute-start.6 = (f32[2,2,2,128,128]{4,3,2,1,0:T(8,128)S(1)}, f32[2,2,2,128,128]{4,3,2,1,0:T(8,128)S(1)}, u32[]{:S(2)}, u32[]{:S(2)}) collective-permute-start(f32[2,2,2,128,128]{4,3,2,1,0:T(8,128)S(1)} %get-tuple-element.68), channel_id=1, source_target_pairs={{0,48},{16,32},{32,16},{48,0},{1,49},{17,33},{33,17},{49,1},{2,50}... | collective-permute-start | bytes 1572872 | tf_op jit(solution)/shard_map/ppermute | solution.py:41
  22.0 1.5 %collective-permute-start.7 = (f32[2,2,2,128,128]{4,3,2,1,0:T(8,128)S(1)}, f32[2,2,2,128,128]{4,3,2,1,0:T(8,128)S(1)}, u32[]{:S(2)}, u32[]{:S(2)}) collective-permute-start(f32[2,2,2,128,128]{4,3,2,1,0:T(8,128)S(1)} %get-tuple-element.67), channel_id=1, source_target_pairs={{0,16},{16,0},{32,48},{48,32},{1,17},{17,1},{33,49},{49,33},{2,18}... | collective-permute-start | bytes 1572872 | tf_op jit(solution)/shard_map/ppermute | solution.py:41
  23.5 0.0 collective-permute-done.3
  23.5 0.1 fusion.10
  23.6 0.1 add.168
  23.8 0.1 add.167
  23.9 13.5 %collective-permute-done.2 = f32[2,2,2,256,128]{4,3,2,1,0:T(8,128)S(1)} collective-permute-done((f32[2,2,2,256,128]{4,3,2,1,0:T(8,128)S(1)}, f32[2,2,2,256,128]{4,3,2,1,0:T(8,128)S(1)}, u32[]{:S(2)}, u32[]{:S(2)}) %collective-permute-start.2) | collective-permute-done | bytes 1048608 | tf_op jit(solution)/shard_map/ppermute | solution.py:41
  37.4 0.1 fusion
  37.5 2.4 %collective-permute-done.4 = f32[2,2,2,256,128]{4,3,2,1,0:T(8,128)S(1)} collective-permute-done((f32[2,2,2,256,128]{4,3,2,1,0:T(8,128)S(1)}, f32[2,2,2,256,128]{4,3,2,1,0:T(8,128)S(1)}, u32[]{:S(2)}, u32[]{:S(2)}) %collective-permute-start.4) | collective-permute-done | bytes 1048608 | tf_op jit(solution)/shard_map/ppermute | solution.py:41
  39.9 0.1 add_bitcast_fusion
  40.0 2.3 %collective-permute-start.5 = (f32[2,2,256,128]{3,2,1,0:T(8,128)S(1)}, f32[2,2,256,128]{3,2,1,0:T(8,128)S(1)}, u32[]{:S(2)}, u32[]{:S(2)}) collective-permute-start(f32[2,2,256,128]{3,2,1,0:T(8,128)S(1)} %fusion), channel_id=1, source_target_pairs={{0,192},{64,128},{128,64},{192,0},{1,193},{65,129},{129,65},{193,1... | collective-permute-start | bytes 1572872 | tf_op jit(solution)/shard_map/ppermute | solution.py:41
  42.3 0.1 fusion.11
  42.3 0.1 collective-permute-start.11
  42.4 0.1 add.174
  42.5 0.1 add.173
  42.6 5.0 %collective-permute-done.7 = f32[2,2,2,128,128]{4,3,2,1,0:T(8,128)S(1)} collective-permute-done((f32[2,2,2,128,128]{4,3,2,1,0:T(8,128)S(1)}, f32[2,2,2,128,128]{4,3,2,1,0:T(8,128)S(1)}, u32[]{:S(2)}, u32[]{:S(2)}) %collective-permute-start.7) | collective-permute-done | bytes 524320 | tf_op jit(solution)/shard_map/ppermute | solution.py:41
  47.6 1.4 %collective-permute-start.10 = (f32[2,2,128,128]{3,2,1,0:T(8,128)S(1)}, f32[2,2,128,128]{3,2,1,0:T(8,128)S(1)}, u32[]{:S(2)}, u32[]{:S(2)}) collective-permute-start(f32[2,2,128,128]{3,2,1,0:T(8,128)S(1)} %add_bitcast_fusion.2), channel_id=1, source_target_pairs={{0,48},{16,32},{32,16},{48,0},{1,49},{17,33},{33,17},{49,1},{2,50}... | collective-permute-start | bytes 786440 | tf_op jit(solution)/shard_map/ppermute | solution.py:41
  49.0 0.0 collective-permute-done.6
  49.1 1.5 %collective-permute-start.9 = (f32[2,2,128,128]{3,2,1,0:T(8,128)S(1)}, f32[2,2,128,128]{3,2,1,0:T(8,128)S(1)}, u32[]{:S(2)}, u32[]{:S(2)}) collective-permute-start(f32[2,2,128,128]{3,2,1,0:T(8,128)S(1)} %add_bitcast_fusion.1), channel_id=1, source_target_pairs={{0,16},{16,0},{32,48},{48,32},{1,17},{17,1},{33,49},{49,33},{2,18}... | collective-permute-start | bytes 786440 | tf_op jit(solution)/shard_map/ppermute | solution.py:41
  50.6 3.8 %collective-permute-done.5 = f32[2,2,256,128]{3,2,1,0:T(8,128)S(1)} collective-permute-done((f32[2,2,256,128]{3,2,1,0:T(8,128)S(1)}, f32[2,2,256,128]{3,2,1,0:T(8,128)S(1)}, u32[]{:S(2)}, u32[]{:S(2)}) %collective-permute-start.5) | collective-permute-done | bytes 524320 | tf_op jit(solution)/shard_map/ppermute | solution.py:41
  54.4 3.4 %collective-permute-start.8 = (f32[2,256,128]{2,1,0:T(8,128)S(1)}, f32[2,256,128]{2,1,0:T(8,128)S(1)}, u32[]{:S(2)}, u32[]{:S(2)}) collective-permute-start(f32[2,256,128]{2,1,0:T(8,128)S(1)} %fusion.2), channel_id=1, source_target_pairs={{0,16},{16,0},{32,48},{48,32},{1,17},{17,1},{33,49},{49,33},{2,18}... | collective-permute-start | bytes 786440 | tf_op jit(solution)/shard_map/ppermute | solution.py:41
  57.8 0.0 collective-permute-done.11
  57.8 0.1 bitcast_add_fusion
  57.8 4.8 %collective-permute-start.17 = (f32[2,256,128]{2,1,0:T(8,128)S(1)}, f32[2,256,128]{2,1,0:T(8,128)S(1)}, u32[]{:S(2)}, u32[]{:S(2)}) collective-permute-start(f32[2,256,128]{2,1,0:T(8,128)S(1)} %bitcast_add_fusion), channel_id=1, source_target_pairs={{0,48},{16,32},{32,16},{48,0},{1,49},{17,33},{33,17},{49,1},{2,50}... | collective-permute-start | bytes 786440 | tf_op jit(solution)/shard_map/ppermute | solution.py:41
  62.6 0.0 collective-permute-done.10
  62.6 0.1 collective-permute-start.13
  62.7 0.4 collective-permute-done.9
  63.1 1.9 %collective-permute-start.12 = (f32[2,128,128]{2,1,0:T(8,128)S(1)}, f32[2,128,128]{2,1,0:T(8,128)S(1)}, u32[]{:S(2)}, u32[]{:S(2)}) collective-permute-start(f32[2,128,128]{2,1,0:T(8,128)S(1)} %bitcast_add_fusion.12), channel_id=1, source_target_pairs={{0,192},{64,128},{128,64},{192,0},{1,193},{65,129},{129,65},{193,1... | collective-permute-start | bytes 393224 | tf_op jit(solution)/shard_map/ppermute | solution.py:41
  65.0 2.6 %collective-permute-done.13 = f32[2,128,128]{2,1,0:T(8,128)S(1)} collective-permute-done((f32[2,128,128]{2,1,0:T(8,128)S(1)}, f32[2,128,128]{2,1,0:T(8,128)S(1)}, u32[]{:S(2)}, u32[]{:S(2)}) %collective-permute-start.13) | collective-permute-done | bytes 131104 | tf_op jit(solution)/shard_map/ppermute | solution.py:41
  67.7 2.3 %collective-permute-start.16 = (f32[128,128]{1,0:T(8,128)S(1)}, f32[128,128]{1,0:T(8,128)S(1)}, u32[]{:S(2)}, u32[]{:S(2)}) collective-permute-start(f32[128,128]{1,0:T(8,128)S(1)} %bitcast_add_fusion.25), channel_id=1, source_target_pairs={{0,192},{64,128},{128,64},{192,0},{1,193},{65,129},{129,65},{193,1... | collective-permute-start | bytes 196616 | tf_op jit(solution)/shard_map/ppermute | solution.py:41
  69.9 0.1 collective-permute-done.12
  70.1 5.1 %collective-permute-start.15 = (f32[128,128]{1,0:T(8,128)S(1)}, f32[128,128]{1,0:T(8,128)S(1)}, u32[]{:S(2)}, u32[]{:S(2)}) collective-permute-start(f32[128,128]{1,0:T(8,128)S(1)} %bitcast_add_fusion.23), channel_id=1, source_target_pairs={{0,64},{64,0},{128,192},{192,128},{1,65},{65,1},{129,193},{193,129... | collective-permute-start | bytes 196616 | tf_op jit(solution)/shard_map/ppermute | solution.py:41
  75.2 0.0 collective-permute-done.8
  75.2 0.6 collective-permute-start.14
  75.8 0.0 collective-permute-done.17
  75.9 3.0 %collective-permute-start.18 = (f32[256,128]{1,0:T(8,128)S(1)}, f32[256,128]{1,0:T(8,128)S(1)}, u32[]{:S(2)}, u32[]{:S(2)}) collective-permute-start(f32[256,128]{1,0:T(8,128)S(1)} %bitcast_add_fusion.6), channel_id=1, source_target_pairs={{0,16},{16,0},{32,48},{48,32},{1,17},{17,1},{33,49},{49,33},{2,18}... | collective-permute-start | bytes 393224 | tf_op jit(solution)/shard_map/ppermute | solution.py:41
  78.8 0.0 collective-permute-done.16
  78.8 0.0 collective-permute-done.15
  78.9 4.9 %collective-permute-done.14 = f32[256,128]{1,0:T(8,128)S(1)} collective-permute-done((f32[256,128]{1,0:T(8,128)S(1)}, f32[256,128]{1,0:T(8,128)S(1)}, u32[]{:S(2)}, u32[]{:S(2)}) %collective-permute-start.14) | collective-permute-done | bytes 131104 | tf_op jit(solution)/shard_map/ppermute | solution.py:41
  83.8 0.0 copy-start
  83.8 0.0 copy-start.1
  83.8 0.0 copy-start.2
  83.9 0.0 collective-permute-done.18
  83.9 0.7 shard_map.98
  84.7 6.6 %all-to-all-start = ((f32[32,1,128]{2,1,0:T(1,128)}), f32[32,1,128]{2,1,0:T(1,128)S(1)}, u32[]{:S(2)}, u32[]{:S(2)}) async-start(f32[32,1,128]{2,1,0:T(1,128)} %shard_map.98), calls=%async_computation | async-start | bytes 32768 | tf_op jit(solution)/shard_map/all_to_all | solution.py:324
  91.3 0.2 copy.16
  91.5 9.5 %all-to-all-done = f32[32,1,128]{2,1,0:T(1,128)S(1)} async-done(((f32[32,1,128]{2,1,0:T(1,128)}), f32[32,1,128]{2,1,0:T(1,128)S(1)}, u32[]{:S(2)}, u32[]{:S(2)}) %all-to-all-start) | async-done | bytes 16416 | tf_op jit(solution)/shard_map/all_to_all | solution.py:324
  100.9 0.1 reduce_sum.18
  101.0 12.4 %all_to_all.10 = f32[8,16,896]{2,1,0:T(8,128)S(1)} all-to-all(f32[8,16,896]{2,1,0:T(8,128)S(1)} %pad_maximum_fusion), channel_id=1, replica_groups=mesh['y'=4,'z'=4,'core'=2,'z_lo'=2,'x'=4] {'z_lo','x'}, dimensions={0} | all-to-all | bytes 917504 | tf_op jit(solution)/shard_map/all_to_all | solution.py:327
  113.5 0.1 slice_reduce_fusion
  113.6 0.0 copy-done
  113.6 0.0 copy-done.1
  113.7 1.3 %multiply_subtract_fusion = (f32[16,6144]{1,0:T(8,128)}, f32[16,6144]{1,0:T(8,128)}, f32[16,6144]{1,0:T(8,128)}) fusion(f32[16,6144]{1,0:T(8,128)S(1)} %copy-done, f32[16,6144]{1,0:T(8,128)S(1)} %bitcast.166, f32[16]{0:T(128)S(1)} %divide_minimum_fusion, f32[16,6144]{1,0:T(8,128)S(1)} %copy-done.1, f32[16,6144]{1,0:T(8,128)S(1)} %copy-done.2), kind=kLoop, calls=%fused_computation.8 | loop fusion | flops 1572864 | bytes 2752576 | tf_op jit(solution)/shard_map/sub | solution.py:336
  (20 shorter events, 0.5 us)
Async XLA Ops:
  5.1 5.8 %collective-permute-start = (f32[2,2,2,2,256,128]{5,4,3,2,1,0:T(8,128)S(1)}, f32[2,2,2,2,256,128]{5,4,3,2,1,0:T(8,128)S(1)}, u32[]{:S(2)}, u32[]{:S(2)}) collective-permute-start(f32[2,2,2,2,256,128]{5,4,3,2,1,0:T(8,128)S(1)} %get-tuple-element.50), channel_id=1, source_target_pairs={{0,8},{8,0},{1,9},{9,1},{2,10},{10,2},{3,11},{11,3},{4,12},{12,4},... | collective-permute-start | bytes 6291464 | tf_op jit(solution)/shard_map/ppermute | solution.py:41
  5.8 5.1 %collective-permute-start.1 = (f32[2,2,2,2,128,128]{5,4,3,2,1,0:T(8,128)S(1)}, f32[2,2,2,2,128,128]{5,4,3,2,1,0:T(8,128)S(1)}, u32[]{:S(2)}, u32[]{:S(2)}) collective-permute-start(f32[2,2,2,2,128,128]{5,4,3,2,1,0:T(8,128)S(1)} %shard_map.95), channel_id=1, source_target_pairs={{0,8},{8,0},{1,9},{9,1},{2,10},{10,2},{3,11},{11,3},{4,12},{12,4},... | collective-permute-start | bytes 3145736 | tf_op jit(solution)/shard_map/ppermute | solution.py:41
  11.7 11.8 %collective-permute-start.3 = (f32[6144,128]{1,0:T(8,128)S(1)}, f32[6144,128]{1,0:T(8,128)S(1)}, u32[]{:S(2)}, u32[]{:S(2)}) collective-permute-start(f32[6144,128]{1,0:T(8,128)S(1)} %get-tuple-element.69), channel_id=1, source_target_pairs={{0,8},{8,0},{1,9},{9,1},{2,10},{10,2},{3,11},{11,3},{4,12},{12,4},... | collective-permute-start | bytes 9437192 | tf_op jit(solution)/shard_map/ppermute | solution.py:41
  12.0 25.4 %collective-permute-start.2 = (f32[2,2,2,256,128]{4,3,2,1,0:T(8,128)S(1)}, f32[2,2,2,256,128]{4,3,2,1,0:T(8,128)S(1)}, u32[]{:S(2)}, u32[]{:S(2)}) collective-permute-start(f32[2,2,2,256,128]{4,3,2,1,0:T(8,128)S(1)} %get-tuple-element.60), channel_id=1, source_target_pairs={{0,64},{64,0},{128,192},{192,128},{1,65},{65,1},{129,193},{193,129... | collective-permute-start | bytes 3145736 | tf_op jit(solution)/shard_map/ppermute | solution.py:41
  13.6 26.4 %collective-permute-start.4 = (f32[2,2,2,256,128]{4,3,2,1,0:T(8,128)S(1)}, f32[2,2,2,256,128]{4,3,2,1,0:T(8,128)S(1)}, u32[]{:S(2)}, u32[]{:S(2)}) collective-permute-start(f32[2,2,2,256,128]{4,3,2,1,0:T(8,128)S(1)} %get-tuple-element.66), channel_id=1, source_target_pairs={{0,192},{64,128},{128,64},{192,0},{1,193},{65,129},{129,65},{193,1... | collective-permute-start | bytes 3145736 | tf_op jit(solution)/shard_map/ppermute | solution.py:41
  15.7 33.3 %collective-permute-start.6 = (f32[2,2,2,128,128]{4,3,2,1,0:T(8,128)S(1)}, f32[2,2,2,128,128]{4,3,2,1,0:T(8,128)S(1)}, u32[]{:S(2)}, u32[]{:S(2)}) collective-permute-start(f32[2,2,2,128,128]{4,3,2,1,0:T(8,128)S(1)} %get-tuple-element.68), channel_id=1, source_target_pairs={{0,48},{16,32},{32,16},{48,0},{1,49},{17,33},{33,17},{49,1},{2,50}... | collective-permute-start | bytes 1572872 | tf_op jit(solution)/shard_map/ppermute | solution.py:41
  22.0 25.5 %collective-permute-start.7 = (f32[2,2,2,128,128]{4,3,2,1,0:T(8,128)S(1)}, f32[2,2,2,128,128]{4,3,2,1,0:T(8,128)S(1)}, u32[]{:S(2)}, u32[]{:S(2)}) collective-permute-start(f32[2,2,2,128,128]{4,3,2,1,0:T(8,128)S(1)} %get-tuple-element.67), channel_id=1, source_target_pairs={{0,16},{16,0},{32,48},{48,32},{1,17},{17,1},{33,49},{49,33},{2,18}... | collective-permute-start | bytes 1572872 | tf_op jit(solution)/shard_map/ppermute | solution.py:41
  40.0 14.4 %collective-permute-start.5 = (f32[2,2,256,128]{3,2,1,0:T(8,128)S(1)}, f32[2,2,256,128]{3,2,1,0:T(8,128)S(1)}, u32[]{:S(2)}, u32[]{:S(2)}) collective-permute-start(f32[2,2,256,128]{3,2,1,0:T(8,128)S(1)} %fusion), channel_id=1, source_target_pairs={{0,192},{64,128},{128,64},{192,0},{1,193},{65,129},{129,65},{193,1... | collective-permute-start | bytes 1572872 | tf_op jit(solution)/shard_map/ppermute | solution.py:41
  42.3 15.4 %collective-permute-start.11 = (f32[2,2,256,128]{3,2,1,0:T(8,128)S(1)}, f32[2,2,256,128]{3,2,1,0:T(8,128)S(1)}, u32[]{:S(2)}, u32[]{:S(2)}) collective-permute-start(f32[2,2,256,128]{3,2,1,0:T(8,128)S(1)} %add_bitcast_fusion), channel_id=1, source_target_pairs={{0,64},{64,0},{128,192},{192,128},{1,65},{65,1},{129,193},{193,129... | collective-permute-start | bytes 1572872 | tf_op jit(solution)/shard_map/ppermute | solution.py:41
  47.6 15.0 %collective-permute-start.10 = (f32[2,2,128,128]{3,2,1,0:T(8,128)S(1)}, f32[2,2,128,128]{3,2,1,0:T(8,128)S(1)}, u32[]{:S(2)}, u32[]{:S(2)}) collective-permute-start(f32[2,2,128,128]{3,2,1,0:T(8,128)S(1)} %add_bitcast_fusion.2), channel_id=1, source_target_pairs={{0,48},{16,32},{32,16},{48,0},{1,49},{17,33},{33,17},{49,1},{2,50}... | collective-permute-start | bytes 786440 | tf_op jit(solution)/shard_map/ppermute | solution.py:41
  49.1 14.0 %collective-permute-start.9 = (f32[2,2,128,128]{3,2,1,0:T(8,128)S(1)}, f32[2,2,128,128]{3,2,1,0:T(8,128)S(1)}, u32[]{:S(2)}, u32[]{:S(2)}) collective-permute-start(f32[2,2,128,128]{3,2,1,0:T(8,128)S(1)} %add_bitcast_fusion.1), channel_id=1, source_target_pairs={{0,16},{16,0},{32,48},{48,32},{1,17},{17,1},{33,49},{49,33},{2,18}... | collective-permute-start | bytes 786440 | tf_op jit(solution)/shard_map/ppermute | solution.py:41
  54.4 20.8 %collective-permute-start.8 = (f32[2,256,128]{2,1,0:T(8,128)S(1)}, f32[2,256,128]{2,1,0:T(8,128)S(1)}, u32[]{:S(2)}, u32[]{:S(2)}) collective-permute-start(f32[2,256,128]{2,1,0:T(8,128)S(1)} %fusion.2), channel_id=1, source_target_pairs={{0,16},{16,0},{32,48},{48,32},{1,17},{17,1},{33,49},{49,33},{2,18}... | collective-permute-start | bytes 786440 | tf_op jit(solution)/shard_map/ppermute | solution.py:41
  57.8 18.0 %collective-permute-start.17 = (f32[2,256,128]{2,1,0:T(8,128)S(1)}, f32[2,256,128]{2,1,0:T(8,128)S(1)}, u32[]{:S(2)}, u32[]{:S(2)}) collective-permute-start(f32[2,256,128]{2,1,0:T(8,128)S(1)} %bitcast_add_fusion), channel_id=1, source_target_pairs={{0,48},{16,32},{32,16},{48,0},{1,49},{17,33},{33,17},{49,1},{2,50}... | collective-permute-start | bytes 786440 | tf_op jit(solution)/shard_map/ppermute | solution.py:41
  62.6 5.1 %collective-permute-start.13 = (f32[2,128,128]{2,1,0:T(8,128)S(1)}, f32[2,128,128]{2,1,0:T(8,128)S(1)}, u32[]{:S(2)}, u32[]{:S(2)}) collective-permute-start(f32[2,128,128]{2,1,0:T(8,128)S(1)} %bitcast_add_fusion.14), channel_id=1, source_target_pairs={{0,64},{64,0},{128,192},{192,128},{1,65},{65,1},{129,193},{193,129... | collective-permute-start | bytes 393224 | tf_op jit(solution)/shard_map/ppermute | solution.py:41
  63.1 7.0 %collective-permute-start.12 = (f32[2,128,128]{2,1,0:T(8,128)S(1)}, f32[2,128,128]{2,1,0:T(8,128)S(1)}, u32[]{:S(2)}, u32[]{:S(2)}) collective-permute-start(f32[2,128,128]{2,1,0:T(8,128)S(1)} %bitcast_add_fusion.12), channel_id=1, source_target_pairs={{0,192},{64,128},{128,64},{192,0},{1,193},{65,129},{129,65},{193,1... | collective-permute-start | bytes 393224 | tf_op jit(solution)/shard_map/ppermute | solution.py:41
  67.7 11.2 %collective-permute-start.16 = (f32[128,128]{1,0:T(8,128)S(1)}, f32[128,128]{1,0:T(8,128)S(1)}, u32[]{:S(2)}, u32[]{:S(2)}) collective-permute-start(f32[128,128]{1,0:T(8,128)S(1)} %bitcast_add_fusion.25), channel_id=1, source_target_pairs={{0,192},{64,128},{128,64},{192,0},{1,193},{65,129},{129,65},{193,1... | collective-permute-start | bytes 196616 | tf_op jit(solution)/shard_map/ppermute | solution.py:41
  70.1 8.8 %collective-permute-start.15 = (f32[128,128]{1,0:T(8,128)S(1)}, f32[128,128]{1,0:T(8,128)S(1)}, u32[]{:S(2)}, u32[]{:S(2)}) collective-permute-start(f32[128,128]{1,0:T(8,128)S(1)} %bitcast_add_fusion.23), channel_id=1, source_target_pairs={{0,64},{64,0},{128,192},{192,128},{1,65},{65,1},{129,193},{193,129... | collective-permute-start | bytes 196616 | tf_op jit(solution)/shard_map/ppermute | solution.py:41
  75.2 8.6 %collective-permute-start.14 = (f32[256,128]{1,0:T(8,128)S(1)}, f32[256,128]{1,0:T(8,128)S(1)}, u32[]{:S(2)}, u32[]{:S(2)}) collective-permute-start(f32[256,128]{1,0:T(8,128)S(1)} %fusion.4), channel_id=1, source_target_pairs={{0,48},{16,32},{32,16},{48,0},{1,49},{17,33},{33,17},{49,1},{2,50}... | collective-permute-start | bytes 393224 | tf_op jit(solution)/shard_map/ppermute | solution.py:41
  75.9 8.0 %collective-permute-start.18 = (f32[256,128]{1,0:T(8,128)S(1)}, f32[256,128]{1,0:T(8,128)S(1)}, u32[]{:S(2)}, u32[]{:S(2)}) collective-permute-start(f32[256,128]{1,0:T(8,128)S(1)} %bitcast_add_fusion.6), channel_id=1, source_target_pairs={{0,16},{16,0},{32,48},{48,32},{1,17},{17,1},{33,49},{49,33},{2,18}... | collective-permute-start | bytes 393224 | tf_op jit(solution)/shard_map/ppermute | solution.py:41
  83.8 29.8 %copy-start = (f32[16,6144]{1,0:T(8,128)S(1)}, f32[16,6144]{1,0:T(8,128)}, u32[]{:S(2)}) copy-start(f32[16,6144]{1,0:T(8,128)} %param.11) | copy-start | bytes 1179652
  83.8 29.8 %copy-start.1 = (f32[16,6144]{1,0:T(8,128)S(1)}, f32[16,6144]{1,0:T(8,128)}, u32[]{:S(2)}) copy-start(f32[16,6144]{1,0:T(8,128)} %param.12) | copy-start | bytes 1179652
  83.8 29.8 %copy-start.2 = (f32[16,6144]{1,0:T(8,128)S(1)}, f32[16,6144]{1,0:T(8,128)}, u32[]{:S(2)}) copy-start(f32[16,6144]{1,0:T(8,128)} %param.13) | copy-start | bytes 1179652
  84.7 16.3 %all-to-all-start = ((f32[32,1,128]{2,1,0:T(1,128)}), f32[32,1,128]{2,1,0:T(1,128)S(1)}, u32[]{:S(2)}, u32[]{:S(2)}) async-start(f32[32,1,128]{2,1,0:T(1,128)} %shard_map.98), calls=%async_computation | async-start | bytes 32768 | tf_op jit(solution)/shard_map/all_to_all | solution.py:324

commit v6 on v5

--- a/solution.py
+++ b/solution.py
@@ -32,7 +32,7 @@
     "kept", "keep:00", "keep:01", "end:00", "end:01", "start:00", "start:01",
     "keep:10", "keep:11", "end:10", "start:10", "end:11", "start:11",
     "end:00", "start:00", "end:01", "start:01", "end:10", "start:10", "end:11", "start:11",
-    "end:10", "start:10", "end:11", "start:11", "end:00", "start:00", "end:01", "start:01",
+    "end:00", "start:00", "end:01", "start:01", "end:10", "start:10", "end:11", "start:11",
     "end:10", "end:11", "end:00", "end:01",
 )
 

time: 115 us -> 115 us (level)
  starting transfers between devices: 45.4 us -> 40.7 us
  waiting for transfers between devices: 42.9 us -> 46.6 us
    ppermute x19, starting transfers between devices: 38.8 us -> 34.8 us  [swap(): lax.ppermute(value, axis, [(i, i ^ mask) for i in range(SIZES[axis])])]
    ppermute x19, waiting for transfers between devices: 33.4 us -> 37.1 us  [swap(): lax.ppermute(value, axis, [(i, i ^ mask) for i in range(SIZES[axis])])]
  transfers between devices with their start and end apart: 20 -> 20, of which waited for: 10 -> 11; matrix products, arithmetic and copies ran while one was open for 1% -> 1% of each run, Pallas kernels for 4% -> 4%
where the time goes in v6:
time: 115 us
  waiting for transfers between devices  46.6 us (41%)
  starting transfers between devices  40.7 us (35%)
  blocking collectives  13.4 us (12%)
  Pallas kernels  10.5 us (9%)
  other arithmetic  2.45 us (2%)
    ppermute x19, waiting for transfers between devices, swap(): lax.ppermute(value, axis, [(i, i ^ mask) for i in range(SIZES[axis])])  37.1 us
    ppermute x19, starting transfers between devices, swap(): lax.ppermute(value, axis, [(i, i ^ mask) for i in range(SIZES[axis])])  34.8 us
    all_to_all x1, blocking collectives, shards(): lax.all_to_all(jnp.concatenate([blocks, beside], axis=2), MP, 0, 0, tiled...  13.4 us
    all_to_all x1, waiting for transfers between devices, shards(): lax.all_to_all(message(done), DP, 0, 0, tiled=True)  9.48 us
    pallas_call x3, Pallas kernels, call(): pl.pallas_call(kernel, in_specs=[pl.BlockSpec(memory_space=space) for spa...  8.93 us
    all_to_all x1, starting transfers between devices, shards(): lax.all_to_all(message(done), DP, 0, 0, tiled=True)  5.87 us
  transfers between devices with their start and end apart: 20, of which 11 were waited for; matrix products, arithmetic and copies ran while one was open for 1% of the time, Pallas kernels for 4%

profile of v6, /device:TPU:2, one launch (start us, length us, event | category | flops | bytes accessed | tf_op | source)
XLA Modules:
  0.0 115.0 jit_solution(18298540321847261712)
XLA Ops:
  0.6 4.5 %shard_map.94 = (f32[2,2,2,2,256,128]{5,4,3,2,1,0:T(8,128)S(1)}, bf16[4,3,256,512]{3,2,1,0:T(8,128)(2,1)S(1)}, bf16[4,3,256,512]{3,2,1,0:T(8,128)(2,1)S(1)}, bf16[768,768]{1,0:T(8,128)(2,1)S(1)}) custom-call(s32[4]{0:T(128)} %ff_hbm.1, s32[4]{0:T(128)} %active_hbm.1, bf16[4,256,4096]{2,1,0:T(8,128)(2,1)} %x_ref.1, bf16[4,256,768]{2,1,0:T(8,128)(2,1)} %m_ref.1), custom_call_target="tpu_custom_call" | custom-call | tf_op jit(solution)/shard_map/pallas_call | solution.py:170
  5.1 0.1 collective-permute-start
  5.2 0.6 shard_map.95
  5.8 0.6 collective-permute-start.1
  6.4 3.8 %shard_map.96 = (f32[6144,128]{1,0:T(8,128)S(1)}, f32[2,2,2,256,128]{4,3,2,1,0:T(8,128)S(1)}, f32[2,2,2,256,128]{4,3,2,1,0:T(8,128)S(1)}, f32[2,2,2,128,128]{4,3...) custom-call(bf16[768,768]{1,0:T(8,128)(2,1)S(1)} %get-tuple-element., ...), custom_call_target="tpu_custom_call" | custom-call | tf_op jit(solution)/shard_map/pallas_call | solution.py:170
  10.3 0.6 collective-permute-done.1.refs_5_
  10.9 0.0 collective-permute-done.refs_4_
  10.9 0.8 shard_map.97
  11.7 0.2 collective-permute-start.3
  12.0 1.6 %collective-permute-start.2 = (f32[2,2,2,256,128]{4,3,2,1,0:T(8,128)S(1)}, f32[2,2,2,256,128]{4,3,2,1,0:T(8,128)S(1)}, u32[]{:S(2)}, u32[]{:S(2)}) collective-permute-start(f32[2,2,2,256,128]{4,3,2,1,0:T(8,128)S(1)} %get-tuple-element.60), channel_id=1, source_target_pairs={{0,64},{64,0},{128,192},{192,128},{1,65},{65,1},{129,193},{193,129... | collective-permute-start | bytes 3145736 | tf_op jit(solution)/shard_map/ppermute | solution.py:41
  13.6 2.2 %collective-permute-start.4 = (f32[2,2,2,256,128]{4,3,2,1,0:T(8,128)S(1)}, f32[2,2,2,256,128]{4,3,2,1,0:T(8,128)S(1)}, u32[]{:S(2)}, u32[]{:S(2)}) collective-permute-start(f32[2,2,2,256,128]{4,3,2,1,0:T(8,128)S(1)} %get-tuple-element.66), channel_id=1, source_target_pairs={{0,192},{64,128},{128,64},{192,0},{1,193},{65,129},{129,65},{193,1... | collective-permute-start | bytes 3145736 | tf_op jit(solution)/shard_map/ppermute | solution.py:41
  15.7 6.3 %collective-permute-start.6 = (f32[2,2,2,128,128]{4,3,2,1,0:T(8,128)S(1)}, f32[2,2,2,128,128]{4,3,2,1,0:T(8,128)S(1)}, u32[]{:S(2)}, u32[]{:S(2)}) collective-permute-start(f32[2,2,2,128,128]{4,3,2,1,0:T(8,128)S(1)} %get-tuple-element.68), channel_id=1, source_target_pairs={{0,48},{16,32},{32,16},{48,0},{1,49},{17,33},{33,17},{49,1},{2,50}... | collective-permute-start | bytes 1572872 | tf_op jit(solution)/shard_map/ppermute | solution.py:41
  22.0 1.5 %collective-permute-start.7 = (f32[2,2,2,128,128]{4,3,2,1,0:T(8,128)S(1)}, f32[2,2,2,128,128]{4,3,2,1,0:T(8,128)S(1)}, u32[]{:S(2)}, u32[]{:S(2)}) collective-permute-start(f32[2,2,2,128,128]{4,3,2,1,0:T(8,128)S(1)} %get-tuple-element.67), channel_id=1, source_target_pairs={{0,16},{16,0},{32,48},{48,32},{1,17},{17,1},{33,49},{49,33},{2,18}... | collective-permute-start | bytes 1572872 | tf_op jit(solution)/shard_map/ppermute | solution.py:41
  23.5 0.0 collective-permute-done.3
  23.5 0.1 fusion.10
  23.6 0.1 add.168
  23.8 0.1 add.167
  23.9 13.5 %collective-permute-done.2 = f32[2,2,2,256,128]{4,3,2,1,0:T(8,128)S(1)} collective-permute-done((f32[2,2,2,256,128]{4,3,2,1,0:T(8,128)S(1)}, f32[2,2,2,256,128]{4,3,2,1,0:T(8,128)S(1)}, u32[]{:S(2)}, u32[]{:S(2)}) %collective-permute-start.2) | collective-permute-done | bytes 1048608 | tf_op jit(solution)/shard_map/ppermute | solution.py:41
  37.4 0.1 fusion
  37.5 2.4 %collective-permute-done.4 = f32[2,2,2,256,128]{4,3,2,1,0:T(8,128)S(1)} collective-permute-done((f32[2,2,2,256,128]{4,3,2,1,0:T(8,128)S(1)}, f32[2,2,2,256,128]{4,3,2,1,0:T(8,128)S(1)}, u32[]{:S(2)}, u32[]{:S(2)}) %collective-permute-start.4) | collective-permute-done | bytes 1048608 | tf_op jit(solution)/shard_map/ppermute | solution.py:41
  39.9 0.1 add_bitcast_fusion
  40.0 2.3 %collective-permute-start.5 = (f32[2,2,256,128]{3,2,1,0:T(8,128)S(1)}, f32[2,2,256,128]{3,2,1,0:T(8,128)S(1)}, u32[]{:S(2)}, u32[]{:S(2)}) collective-permute-start(f32[2,2,256,128]{3,2,1,0:T(8,128)S(1)} %fusion), channel_id=1, source_target_pairs={{0,192},{64,128},{128,64},{192,0},{1,193},{65,129},{129,65},{193,1... | collective-permute-start | bytes 1572872 | tf_op jit(solution)/shard_map/ppermute | solution.py:41
  42.3 0.1 fusion.11
  42.3 0.1 collective-permute-start.11
  42.4 0.1 add.174
  42.5 0.1 add.173
  42.6 5.0 %collective-permute-done.7 = f32[2,2,2,128,128]{4,3,2,1,0:T(8,128)S(1)} collective-permute-done((f32[2,2,2,128,128]{4,3,2,1,0:T(8,128)S(1)}, f32[2,2,2,128,128]{4,3,2,1,0:T(8,128)S(1)}, u32[]{:S(2)}, u32[]{:S(2)}) %collective-permute-start.7) | collective-permute-done | bytes 524320 | tf_op jit(solution)/shard_map/ppermute | solution.py:41
  47.6 1.4 %collective-permute-start.10 = (f32[2,2,128,128]{3,2,1,0:T(8,128)S(1)}, f32[2,2,128,128]{3,2,1,0:T(8,128)S(1)}, u32[]{:S(2)}, u32[]{:S(2)}) collective-permute-start(f32[2,2,128,128]{3,2,1,0:T(8,128)S(1)} %add_bitcast_fusion.2), channel_id=1, source_target_pairs={{0,48},{16,32},{32,16},{48,0},{1,49},{17,33},{33,17},{49,1},{2,50}... | collective-permute-start | bytes 786440 | tf_op jit(solution)/shard_map/ppermute | solution.py:41
  49.0 0.0 collective-permute-done.6
  49.1 1.5 %collective-permute-start.9 = (f32[2,2,128,128]{3,2,1,0:T(8,128)S(1)}, f32[2,2,128,128]{3,2,1,0:T(8,128)S(1)}, u32[]{:S(2)}, u32[]{:S(2)}) collective-permute-start(f32[2,2,128,128]{3,2,1,0:T(8,128)S(1)} %add_bitcast_fusion.1), channel_id=1, source_target_pairs={{0,16},{16,0},{32,48},{48,32},{1,17},{17,1},{33,49},{49,33},{2,18}... | collective-permute-start | bytes 786440 | tf_op jit(solution)/shard_map/ppermute | solution.py:41
  50.6 3.8 %collective-permute-done.5 = f32[2,2,256,128]{3,2,1,0:T(8,128)S(1)} collective-permute-done((f32[2,2,256,128]{3,2,1,0:T(8,128)S(1)}, f32[2,2,256,128]{3,2,1,0:T(8,128)S(1)}, u32[]{:S(2)}, u32[]{:S(2)}) %collective-permute-start.5) | collective-permute-done | bytes 524320 | tf_op jit(solution)/shard_map/ppermute | solution.py:41
  54.4 3.4 %collective-permute-start.8 = (f32[2,256,128]{2,1,0:T(8,128)S(1)}, f32[2,256,128]{2,1,0:T(8,128)S(1)}, u32[]{:S(2)}, u32[]{:S(2)}) collective-permute-start(f32[2,256,128]{2,1,0:T(8,128)S(1)} %fusion.2), channel_id=1, source_target_pairs={{0,16},{16,0},{32,48},{48,32},{1,17},{17,1},{33,49},{49,33},{2,18}... | collective-permute-start | bytes 786440 | tf_op jit(solution)/shard_map/ppermute | solution.py:41
  57.8 0.0 collective-permute-done.11
  57.8 0.1 bitcast_add_fusion
  57.8 4.8 %collective-permute-start.15 = (f32[2,256,128]{2,1,0:T(8,128)S(1)}, f32[2,256,128]{2,1,0:T(8,128)S(1)}, u32[]{:S(2)}, u32[]{:S(2)}) collective-permute-start(f32[2,256,128]{2,1,0:T(8,128)S(1)} %bitcast_add_fusion), channel_id=1, source_target_pairs={{0,48},{16,32},{32,16},{48,0},{1,49},{17,33},{33,17},{49,1},{2,50}... | collective-permute-start | bytes 786440 | tf_op jit(solution)/shard_map/ppermute | solution.py:41
  62.6 0.0 collective-permute-done.10
  62.6 0.1 collective-permute-start.14
  62.7 0.4 collective-permute-done.9
  63.1 1.9 %collective-permute-start.13 = (f32[2,128,128]{2,1,0:T(8,128)S(1)}, f32[2,128,128]{2,1,0:T(8,128)S(1)}, u32[]{:S(2)}, u32[]{:S(2)}) collective-permute-start(f32[2,128,128]{2,1,0:T(8,128)S(1)} %bitcast_add_fusion.12), channel_id=1, source_target_pairs={{0,192},{64,128},{128,64},{192,0},{1,193},{65,129},{129,65},{193,1... | collective-permute-start | bytes 393224 | tf_op jit(solution)/shard_map/ppermute | solution.py:41
  65.0 6.8 %collective-permute-done.8 = f32[2,256,128]{2,1,0:T(8,128)S(1)} collective-permute-done((f32[2,256,128]{2,1,0:T(8,128)S(1)}, f32[2,256,128]{2,1,0:T(8,128)S(1)}, u32[]{:S(2)}, u32[]{:S(2)}) %collective-permute-start.8) | collective-permute-done | bytes 262176 | tf_op jit(solution)/shard_map/ppermute | solution.py:41
  71.9 4.0 %collective-permute-start.12 = (f32[256,128]{1,0:T(8,128)S(1)}, f32[256,128]{1,0:T(8,128)S(1)}, u32[]{:S(2)}, u32[]{:S(2)}) collective-permute-start(f32[256,128]{1,0:T(8,128)S(1)} %fusion.4), channel_id=1, source_target_pairs={{0,48},{16,32},{32,16},{48,0},{1,49},{17,33},{33,17},{49,1},{2,50}... | collective-permute-start | bytes 393224 | tf_op jit(solution)/shard_map/ppermute | solution.py:41
  75.8 0.0 collective-permute-done.15
  75.9 0.1 collective-permute-start.18
  76.0 0.0 collective-permute-done.14
  76.0 2.8 %collective-permute-start.17 = (f32[128,128]{1,0:T(8,128)S(1)}, f32[128,128]{1,0:T(8,128)S(1)}, u32[]{:S(2)}, u32[]{:S(2)}) collective-permute-start(f32[128,128]{1,0:T(8,128)S(1)} %bitcast_add_fusion.25), channel_id=1, source_target_pairs={{0,192},{64,128},{128,64},{192,0},{1,193},{65,129},{129,65},{193,1... | collective-permute-start | bytes 196616 | tf_op jit(solution)/shard_map/ppermute | solution.py:41
  78.8 0.0 collective-permute-done.13
  78.8 0.1 collective-permute-start.16
  78.9 2.7 %collective-permute-done.17 = f32[128,128]{1,0:T(8,128)S(1)} collective-permute-done((f32[128,128]{1,0:T(8,128)S(1)}, f32[128,128]{1,0:T(8,128)S(1)}, u32[]{:S(2)}, u32[]{:S(2)}) %collective-permute-start.17) | collective-permute-done | bytes 65568 | tf_op jit(solution)/shard_map/ppermute | solution.py:41
  81.6 1.6 %collective-permute-done.16 = f32[128,128]{1,0:T(8,128)S(1)} collective-permute-done((f32[128,128]{1,0:T(8,128)S(1)}, f32[128,128]{1,0:T(8,128)S(1)}, u32[]{:S(2)}, u32[]{:S(2)}) %collective-permute-start.16) | collective-permute-done | bytes 65568 | tf_op jit(solution)/shard_map/ppermute | solution.py:41
  83.2 0.0 collective-permute-done.12
  83.2 0.0 copy-start
  83.2 0.0 copy-start.1
  83.2 0.0 copy-start.2
  83.3 0.3 collective-permute-done.18
  83.6 0.7 shard_map.98
  84.3 5.9 %all-to-all-start = ((f32[32,1,128]{2,1,0:T(1,128)}), f32[32,1,128]{2,1,0:T(1,128)S(1)}, u32[]{:S(2)}, u32[]{:S(2)}) async-start(f32[32,1,128]{2,1,0:T(1,128)} %shard_map.98), calls=%async_computation | async-start | bytes 32768 | tf_op jit(solution)/shard_map/all_to_all | solution.py:324
  90.3 0.2 copy.16
  90.4 9.5 %all-to-all-done = f32[32,1,128]{2,1,0:T(1,128)S(1)} async-done(((f32[32,1,128]{2,1,0:T(1,128)}), f32[32,1,128]{2,1,0:T(1,128)S(1)}, u32[]{:S(2)}, u32[]{:S(2)}) %all-to-all-start) | async-done | bytes 16416 | tf_op jit(solution)/shard_map/all_to_all | solution.py:324
  99.9 0.1 reduce_sum.18
  100.0 13.4 %all_to_all.10 = f32[8,16,896]{2,1,0:T(8,128)S(1)} all-to-all(f32[8,16,896]{2,1,0:T(8,128)S(1)} %pad_maximum_fusion), channel_id=1, replica_groups=mesh['y'=4,'z'=4,'core'=2,'z_lo'=2,'x'=4] {'z_lo','x'}, dimensions={0} | all-to-all | bytes 917504 | tf_op jit(solution)/shard_map/all_to_all | solution.py:327
  113.5 0.1 slice_reduce_fusion
  113.7 0.0 copy-done
  113.7 0.0 copy-done.1
  113.7 1.3 %multiply_subtract_fusion = (f32[16,6144]{1,0:T(8,128)}, f32[16,6144]{1,0:T(8,128)}, f32[16,6144]{1,0:T(8,128)}) fusion(f32[16,6144]{1,0:T(8,128)S(1)} %copy-done, f32[16,6144]{1,0:T(8,128)S(1)} %bitcast.166, f32[16]{0:T(128)S(1)} %divide_minimum_fusion, f32[16,6144]{1,0:T(8,128)S(1)} %copy-done.1, f32[16,6144]{1,0:T(8,128)S(1)} %copy-done.2), kind=kLoop, calls=%fused_computation.8 | loop fusion | flops 1572864 | bytes 2752576 | tf_op jit(solution)/shard_map/sub | solution.py:336
  (20 shorter events, 0.5 us)
Async XLA Ops:
  5.1 5.8 %collective-permute-start = (f32[2,2,2,2,256,128]{5,4,3,2,1,0:T(8,128)S(1)}, f32[2,2,2,2,256,128]{5,4,3,2,1,0:T(8,128)S(1)}, u32[]{:S(2)}, u32[]{:S(2)}) collective-permute-start(f32[2,2,2,2,256,128]{5,4,3,2,1,0:T(8,128)S(1)} %get-tuple-element.50), channel_id=1, source_target_pairs={{0,8},{8,0},{1,9},{9,1},{2,10},{10,2},{3,11},{11,3},{4,12},{12,4},... | collective-permute-start | bytes 6291464 | tf_op jit(solution)/shard_map/ppermute | solution.py:41
  5.8 5.1 %collective-permute-start.1 = (f32[2,2,2,2,128,128]{5,4,3,2,1,0:T(8,128)S(1)}, f32[2,2,2,2,128,128]{5,4,3,2,1,0:T(8,128)S(1)}, u32[]{:S(2)}, u32[]{:S(2)}) collective-permute-start(f32[2,2,2,2,128,128]{5,4,3,2,1,0:T(8,128)S(1)} %shard_map.95), channel_id=1, source_target_pairs={{0,8},{8,0},{1,9},{9,1},{2,10},{10,2},{3,11},{11,3},{4,12},{12,4},... | collective-permute-start | bytes 3145736 | tf_op jit(solution)/shard_map/ppermute | solution.py:41
  11.7 11.8 %collective-permute-start.3 = (f32[6144,128]{1,0:T(8,128)S(1)}, f32[6144,128]{1,0:T(8,128)S(1)}, u32[]{:S(2)}, u32[]{:S(2)}) collective-permute-start(f32[6144,128]{1,0:T(8,128)S(1)} %get-tuple-element.69), channel_id=1, source_target_pairs={{0,8},{8,0},{1,9},{9,1},{2,10},{10,2},{3,11},{11,3},{4,12},{12,4},... | collective-permute-start | bytes 9437192 | tf_op jit(solution)/shard_map/ppermute | solution.py:41
  12.0 25.4 %collective-permute-start.2 = (f32[2,2,2,256,128]{4,3,2,1,0:T(8,128)S(1)}, f32[2,2,2,256,128]{4,3,2,1,0:T(8,128)S(1)}, u32[]{:S(2)}, u32[]{:S(2)}) collective-permute-start(f32[2,2,2,256,128]{4,3,2,1,0:T(8,128)S(1)} %get-tuple-element.60), channel_id=1, source_target_pairs={{0,64},{64,0},{128,192},{192,128},{1,65},{65,1},{129,193},{193,129... | collective-permute-start | bytes 3145736 | tf_op jit(solution)/shard_map/ppermute | solution.py:41
  13.6 26.4 %collective-permute-start.4 = (f32[2,2,2,256,128]{4,3,2,1,0:T(8,128)S(1)}, f32[2,2,2,256,128]{4,3,2,1,0:T(8,128)S(1)}, u32[]{:S(2)}, u32[]{:S(2)}) collective-permute-start(f32[2,2,2,256,128]{4,3,2,1,0:T(8,128)S(1)} %get-tuple-element.66), channel_id=1, source_target_pairs={{0,192},{64,128},{128,64},{192,0},{1,193},{65,129},{129,65},{193,1... | collective-permute-start | bytes 3145736 | tf_op jit(solution)/shard_map/ppermute | solution.py:41
  15.7 33.3 %collective-permute-start.6 = (f32[2,2,2,128,128]{4,3,2,1,0:T(8,128)S(1)}, f32[2,2,2,128,128]{4,3,2,1,0:T(8,128)S(1)}, u32[]{:S(2)}, u32[]{:S(2)}) collective-permute-start(f32[2,2,2,128,128]{4,3,2,1,0:T(8,128)S(1)} %get-tuple-element.68), channel_id=1, source_target_pairs={{0,48},{16,32},{32,16},{48,0},{1,49},{17,33},{33,17},{49,1},{2,50}... | collective-permute-start | bytes 1572872 | tf_op jit(solution)/shard_map/ppermute | solution.py:41
  22.0 25.5 %collective-permute-start.7 = (f32[2,2,2,128,128]{4,3,2,1,0:T(8,128)S(1)}, f32[2,2,2,128,128]{4,3,2,1,0:T(8,128)S(1)}, u32[]{:S(2)}, u32[]{:S(2)}) collective-permute-start(f32[2,2,2,128,128]{4,3,2,1,0:T(8,128)S(1)} %get-tuple-element.67), channel_id=1, source_target_pairs={{0,16},{16,0},{32,48},{48,32},{1,17},{17,1},{33,49},{49,33},{2,18}... | collective-permute-start | bytes 1572872 | tf_op jit(solution)/shard_map/ppermute | solution.py:41
  40.0 14.4 %collective-permute-start.5 = (f32[2,2,256,128]{3,2,1,0:T(8,128)S(1)}, f32[2,2,256,128]{3,2,1,0:T(8,128)S(1)}, u32[]{:S(2)}, u32[]{:S(2)}) collective-permute-start(f32[2,2,256,128]{3,2,1,0:T(8,128)S(1)} %fusion), channel_id=1, source_target_pairs={{0,192},{64,128},{128,64},{192,0},{1,193},{65,129},{129,65},{193,1... | collective-permute-start | bytes 1572872 | tf_op jit(solution)/shard_map/ppermute | solution.py:41
  42.3 15.4 %collective-permute-start.11 = (f32[2,2,256,128]{3,2,1,0:T(8,128)S(1)}, f32[2,2,256,128]{3,2,1,0:T(8,128)S(1)}, u32[]{:S(2)}, u32[]{:S(2)}) collective-permute-start(f32[2,2,256,128]{3,2,1,0:T(8,128)S(1)} %add_bitcast_fusion), channel_id=1, source_target_pairs={{0,64},{64,0},{128,192},{192,128},{1,65},{65,1},{129,193},{193,129... | collective-permute-start | bytes 1572872 | tf_op jit(solution)/shard_map/ppermute | solution.py:41
  47.6 15.0 %collective-permute-start.10 = (f32[2,2,128,128]{3,2,1,0:T(8,128)S(1)}, f32[2,2,128,128]{3,2,1,0:T(8,128)S(1)}, u32[]{:S(2)}, u32[]{:S(2)}) collective-permute-start(f32[2,2,128,128]{3,2,1,0:T(8,128)S(1)} %add_bitcast_fusion.2), channel_id=1, source_target_pairs={{0,48},{16,32},{32,16},{48,0},{1,49},{17,33},{33,17},{49,1},{2,50}... | collective-permute-start | bytes 786440 | tf_op jit(solution)/shard_map/ppermute | solution.py:41
  49.1 14.0 %collective-permute-start.9 = (f32[2,2,128,128]{3,2,1,0:T(8,128)S(1)}, f32[2,2,128,128]{3,2,1,0:T(8,128)S(1)}, u32[]{:S(2)}, u32[]{:S(2)}) collective-permute-start(f32[2,2,128,128]{3,2,1,0:T(8,128)S(1)} %add_bitcast_fusion.1), channel_id=1, source_target_pairs={{0,16},{16,0},{32,48},{48,32},{1,17},{17,1},{33,49},{49,33},{2,18}... | collective-permute-start | bytes 786440 | tf_op jit(solution)/shard_map/ppermute | solution.py:41
  54.4 17.4 %collective-permute-start.8 = (f32[2,256,128]{2,1,0:T(8,128)S(1)}, f32[2,256,128]{2,1,0:T(8,128)S(1)}, u32[]{:S(2)}, u32[]{:S(2)}) collective-permute-start(f32[2,256,128]{2,1,0:T(8,128)S(1)} %fusion.2), channel_id=1, source_target_pairs={{0,16},{16,0},{32,48},{48,32},{1,17},{17,1},{33,49},{49,33},{2,18}... | collective-permute-start | bytes 786440 | tf_op jit(solution)/shard_map/ppermute | solution.py:41
  57.8 18.0 %collective-permute-start.15 = (f32[2,256,128]{2,1,0:T(8,128)S(1)}, f32[2,256,128]{2,1,0:T(8,128)S(1)}, u32[]{:S(2)}, u32[]{:S(2)}) collective-permute-start(f32[2,256,128]{2,1,0:T(8,128)S(1)} %bitcast_add_fusion), channel_id=1, source_target_pairs={{0,48},{16,32},{32,16},{48,0},{1,49},{17,33},{33,17},{49,1},{2,50}... | collective-permute-start | bytes 786440 | tf_op jit(solution)/shard_map/ppermute | solution.py:41
  62.6 13.4 %collective-permute-start.14 = (f32[2,128,128]{2,1,0:T(8,128)S(1)}, f32[2,128,128]{2,1,0:T(8,128)S(1)}, u32[]{:S(2)}, u32[]{:S(2)}) collective-permute-start(f32[2,128,128]{2,1,0:T(8,128)S(1)} %bitcast_add_fusion.14), channel_id=1, source_target_pairs={{0,64},{64,0},{128,192},{192,128},{1,65},{65,1},{129,193},{193,129... | collective-permute-start | bytes 393224 | tf_op jit(solution)/shard_map/ppermute | solution.py:41
  63.1 15.7 %collective-permute-start.13 = (f32[2,128,128]{2,1,0:T(8,128)S(1)}, f32[2,128,128]{2,1,0:T(8,128)S(1)}, u32[]{:S(2)}, u32[]{:S(2)}) collective-permute-start(f32[2,128,128]{2,1,0:T(8,128)S(1)} %bitcast_add_fusion.12), channel_id=1, source_target_pairs={{0,192},{64,128},{128,64},{192,0},{1,193},{65,129},{129,65},{193,1... | collective-permute-start | bytes 393224 | tf_op jit(solution)/shard_map/ppermute | solution.py:41
  71.9 11.3 %collective-permute-start.12 = (f32[256,128]{1,0:T(8,128)S(1)}, f32[256,128]{1,0:T(8,128)S(1)}, u32[]{:S(2)}, u32[]{:S(2)}) collective-permute-start(f32[256,128]{1,0:T(8,128)S(1)} %fusion.4), channel_id=1, source_target_pairs={{0,48},{16,32},{32,16},{48,0},{1,49},{17,33},{33,17},{49,1},{2,50}... | collective-permute-start | bytes 393224 | tf_op jit(solution)/shard_map/ppermute | solution.py:41
  75.9 7.7 %collective-permute-start.18 = (f32[256,128]{1,0:T(8,128)S(1)}, f32[256,128]{1,0:T(8,128)S(1)}, u32[]{:S(2)}, u32[]{:S(2)}) collective-permute-start(f32[256,128]{1,0:T(8,128)S(1)} %bitcast_add_fusion.6), channel_id=1, source_target_pairs={{0,16},{16,0},{32,48},{48,32},{1,17},{17,1},{33,49},{49,33},{2,18}... | collective-permute-start | bytes 393224 | tf_op jit(solution)/shard_map/ppermute | solution.py:41
  76.0 5.6 %collective-permute-start.17 = (f32[128,128]{1,0:T(8,128)S(1)}, f32[128,128]{1,0:T(8,128)S(1)}, u32[]{:S(2)}, u32[]{:S(2)}) collective-permute-start(f32[128,128]{1,0:T(8,128)S(1)} %bitcast_add_fusion.25), channel_id=1, source_target_pairs={{0,192},{64,128},{128,64},{192,0},{1,193},{65,129},{129,65},{193,1... | collective-permute-start | bytes 196616 | tf_op jit(solution)/shard_map/ppermute | solution.py:41
  78.8 4.4 %collective-permute-start.16 = (f32[128,128]{1,0:T(8,128)S(1)}, f32[128,128]{1,0:T(8,128)S(1)}, u32[]{:S(2)}, u32[]{:S(2)}) collective-permute-start(f32[128,128]{1,0:T(8,128)S(1)} %bitcast_add_fusion.21), channel_id=1, source_target_pairs={{0,64},{64,0},{128,192},{192,128},{1,65},{65,1},{129,193},{193,129... | collective-permute-start | bytes 196616 | tf_op jit(solution)/shard_map/ppermute | solution.py:41
  83.2 30.4 %copy-start = (f32[16,6144]{1,0:T(8,128)S(1)}, f32[16,6144]{1,0:T(8,128)}, u32[]{:S(2)}) copy-start(f32[16,6144]{1,0:T(8,128)} %param.11) | copy-start | bytes 1179652
  83.2 30.4 %copy-start.1 = (f32[16,6144]{1,0:T(8,128)S(1)}, f32[16,6144]{1,0:T(8,128)}, u32[]{:S(2)}) copy-start(f32[16,6144]{1,0:T(8,128)} %param.12) | copy-start | bytes 1179652
  83.2 30.4 %copy-start.2 = (f32[16,6144]{1,0:T(8,128)S(1)}, f32[16,6144]{1,0:T(8,128)}, u32[]{:S(2)}) copy-start(f32[16,6144]{1,0:T(8,128)} %param.13) | copy-start | bytes 1179652
  84.3 15.6 %all-to-all-start = ((f32[32,1,128]{2,1,0:T(1,128)}), f32[32,1,128]{2,1,0:T(1,128)S(1)}, u32[]{:S(2)}, u32[]{:S(2)}) async-start(f32[32,1,128]{2,1,0:T(1,128)} %shard_map.98), calls=%async_computation | async-start | bytes 32768 | tf_op jit(solution)/shard_map/all_to_all | solution.py:324
